TPU v7x, 32 devices: a whole 2x2x4 slice. The times are simulated.
32 devices in a mesh: head: 4 (over y, x), seq: 8 (over z, core).
Axes of the slice: x: 2, y: 2, z: 4, core: 2. Of those that a mesh axis runs over, the one named last changes fastest.
Arguments:
- tokens: bfloat16 [8192, 1024], P(('seq', 'head')), may hold values from -6 to 6
- cotangent: bfloat16 [8192, 1024], P(('seq', 'head')), may hold values from -6 to 6
- segments: int32 [8192], replicated, may hold values from 0 to 42, as said below
- w_query: bfloat16 [1024, 1024], P(('head', 'seq')), may hold values from -0.1875 to 0.1875
- w_key: bfloat16 [1024, 1024], P(('head', 'seq')), may hold values from -0.1875 to 0.1875
- w_value: bfloat16 [1024, 1024], P(('head', 'seq')), may hold values from -0.1875 to 0.1875
- w_out: bfloat16 [1024, 1024], P(('head', 'seq')), may hold values from -0.75 to 0.75
- w_up: bfloat16 [1024, 4096], P(('head', 'seq')), may hold values from -0.1875 to 0.1875
- w_down: bfloat16 [4096, 1024], P(('head', 'seq')), may hold values from -0.09375 to 0.09375
- norm_one: bfloat16 [1024], P(('head', 'seq')), may hold values from 0.5 to 1.5
- norm_two: bfloat16 [1024], P(('head', 'seq')), may hold values from 0.5 to 1.5
- rel_table: float32 [8, 32], P('head'), may hold values from -4 to 4
- decay_rate: float32 [8], P('head'), may hold values from 0.0001 to 0.06
Outputs:
- output: bfloat16 [8192, 1024], P(('seq', 'head'))
- input_grad: bfloat16 [8192, 1024], P(('seq', 'head'))
- grad_query: float32 [1024, 1024], P(('head', 'seq'))
- grad_key: float32 [1024, 1024], P(('head', 'seq'))
- grad_value: float32 [1024, 1024], P(('head', 'seq'))
- grad_out: float32 [1024, 1024], P(('head', 'seq'))
- grad_up: float32 [1024, 4096], P(('head', 'seq'))
- grad_down: float32 [4096, 1024], P(('head', 'seq'))
- grad_norm_one: float32 [1024], P(('head', 'seq'))
- grad_norm_two: float32 [1024], P(('head', 'seq'))
- grad_rel_table: float32 [8, 32], P('head')
- grad_decay_rate: float32 [8], P('head')
Inputs may be any that keep to these rules, and one draw needn't show every extreme that they name: `segments`: document numbers never fall and are distinct between documents; no document spans two sequences. The documents of sequence s carry numbers from s * 43 to (s + 1) * 43 - 1, its first document the lowest of them and its last document the highest, with gaps allowed between. Within a sequence every document has 200 to 2000 tokens except the first and the last, which may be shorter, and one document of each sequence has exactly 2000.
All inputs are finite; a program needn't handle non-finite values.
Results may differ from a plain program's by a relative error of at most 0.013.
Values may be sent and summed in bfloat16 or wider, within the bound.
A program may use at most 256 MiB of HBM per device.

v0:
```python
import math

import jax
import jax.numpy as jnp
import numpy as np
from jax import lax
from jax.sharding import PartitionSpec as P

HD = 128
BUCKETS = 32
WIN = 512


epsilon = 1e-06
negative = -1e30
state_scale = 1.0 / 1024.0
highest = lax.Precision.HIGHEST


def from_behind(value, axis, by):
    size = lax.axis_size(axis)
    pairs = [(i, i + by) for i in range(size) if 0 <= i + by < size]
    return lax.ppermute(value, axis, pairs)


def prefix(value, axis, join, neutral, backward):
    count = lax.axis_size(axis)
    place = lax.axis_index(axis)
    ahead = count - 1 - place if backward else place
    gathered = jax.tree.map(
        lambda a, kind: lax.all_gather(a.astype(kind), axis), value, (jnp.bfloat16, jnp.bfloat16)
    )
    state = jax.tree.map(lambda a, e: jnp.zeros_like(a) + jnp.asarray(e, a.dtype), value, neutral)

    def one(lap, state):
        source = count - 1 - lap if backward else lap
        return join(
            state,
            jax.tree.map(
                lambda a, own: lax.dynamic_index_in_dim(a, source, 0, False).astype(own.dtype),
                gathered,
                value,
            ),
        )

    return lax.fori_loop(0, ahead, one, state)


def bucket_onehot(window_len, bucket_count):
    distance = np.arange(window_len)
    scaled = np.floor(np.log(np.maximum(distance, 1) / 16.0) / np.log(8.0) * 16.0)
    larger = np.minimum(16 + np.maximum(scaled, 0), bucket_count - 1)
    bucket = np.where(distance < 16, distance, larger).astype(np.int32)
    return (bucket[:, None] == np.arange(bucket_count)[None, :]).astype(np.float32)


def skewed(extended, row_count, col_count):
    head_count = extended.shape[0]
    span = row_count + col_count
    flipped = jnp.concatenate(
        [extended[:, ::-1], jnp.zeros((head_count, 1), extended.dtype)], axis=1
    )
    tiled = jnp.broadcast_to(flipped[:, None, :], (head_count, row_count, span)).reshape(
        head_count, row_count * span
    )
    tiled = tiled[:, : row_count * (span - 1)].reshape(head_count, row_count, span - 1)
    return tiled[:, :, row_count - 1 : row_count - 1 + col_count]


def rms_scale(values, gain):
    return values * lax.rsqrt(jnp.mean(values * values, axis=-1, keepdims=True) + epsilon) * gain


def times_transposed(left, right):
    return lax.dot_general(
        left, right, (((1,), (1,)), ((), ())), preferred_element_type=jnp.float32
    )


def transposed_times(left, right):
    return lax.dot_general(
        left, right, (((0,), (0,)), ((), ())), preferred_element_type=jnp.float32
    )


def compose(earlier, later):
    return (earlier[0] * later[0], later[0][:, None, None] * earlier[1] + later[1])


def group_state(carried_state, query_c, key_c, value_c, seg_group, seg_before, decay_rate):
    length_c = query_c.shape[0]
    position = jnp.arange(length_c).astype(jnp.float32)
    distance = position[:, None] - position[None, :]
    inside = (distance >= 0) & (seg_group[:, None] == seg_group[None, :])
    decay_w = jnp.where(
        inside[None], jnp.exp(-decay_rate[:, None, None] * jnp.maximum(distance, 0.0)[None]), 0.0
    )
    affinity = jnp.einsum("ihd,jhd->hij", query_c, key_c, precision=highest) * state_scale
    readout = jnp.einsum("hij,jhd->ihd", affinity * decay_w, value_c, precision=highest)
    live_mask = (seg_group == seg_before).astype(jnp.float32)
    entering = (
        jnp.exp(-decay_rate[None, :] * (position[:, None] + 1.0)) * live_mask[:, None] * state_scale
    )
    readout = (
        readout
        + jnp.einsum("ihd,hde->ihe", query_c, carried_state, precision=highest)
        * entering[:, :, None]
    )
    keeping = (seg_group == seg_group[-1]).astype(jnp.float32)
    leaving = (
        jnp.exp(-decay_rate[None, :] * (length_c - 1.0 - position[:, None])) * keeping[:, None]
    )
    carry_keep = jnp.exp(-decay_rate * length_c) * (seg_group[-1] == seg_before).astype(jnp.float32)
    updated = jnp.einsum("jhd,jhe->hde", key_c * leaving[:, :, None], value_c, precision=highest)
    updated = updated + carry_keep[:, None, None] * carried_state
    return (updated, readout)


def local_states(query_f, key_f, value_f, decay_rate, seg_block, seg_before):
    block_len, head_count, head_width = query_f.shape
    count = block_len // WIN
    items = (
        query_f.reshape(count, WIN, head_count, head_width),
        key_f.reshape(count, WIN, head_count, head_width),
        value_f.reshape(count, WIN, head_count, head_width),
        seg_block.reshape(count, WIN),
    )

    def step(carry, item):
        carried_state, prior = carry
        updated, readout = group_state(
            carried_state, item[0], item[1], item[2], item[3], prior, decay_rate
        )
        return ((updated, item[3][-1]), readout)

    start_carry = (jnp.zeros((head_count, head_width, head_width), jnp.float32), seg_before)
    (final_state, _), readouts = lax.scan(step, start_carry, items)
    return (readouts.reshape(block_len, head_count, head_width), final_state)


def shards(
    tokens,
    cotangent,
    segments,
    w_query,
    w_key,
    w_value,
    w_out,
    w_up,
    w_down,
    norm_one,
    norm_two,
    rel_table,
    decay_rate,
):
    heads_here = rel_table.shape[0]
    head_width = HD
    tok_here = tokens.shape[0]
    block_len = lax.axis_size("head") * tok_here
    block_count = block_len // WIN
    pair_width = heads_here * head_width
    scale = 1.0 / math.sqrt(head_width)
    gathered = (
        lax.all_gather(w_query, ("head", "seq"), axis=0, tiled=True),
        lax.all_gather(w_key, ("head", "seq"), axis=0, tiled=True),
        lax.all_gather(w_value, ("head", "seq"), axis=0, tiled=True),
        lax.all_gather(w_out, ("head", "seq"), axis=0, tiled=True),
        lax.all_gather(w_up, ("head", "seq"), axis=0, tiled=True),
        lax.all_gather(w_down, ("head", "seq"), axis=0, tiled=True),
        lax.all_gather(norm_one, ("head", "seq"), axis=0, tiled=True),
        lax.all_gather(norm_two, ("head", "seq"), axis=0, tiled=True),
    )
    full_query, full_key, full_value, full_out, full_up, full_down, gain_one, gain_two = gathered
    inputs_f = tokens.astype(jnp.float32)
    scaled_one, norm_back_one = jax.vjp(rms_scale, inputs_f, gain_one.astype(jnp.float32))
    normed = scaled_one.astype(jnp.bfloat16)
    projected = jnp.stack(
        [
            jnp.dot(normed, full_query, preferred_element_type=jnp.float32),
            jnp.dot(normed, full_key, preferred_element_type=jnp.float32),
            jnp.dot(normed, full_value, preferred_element_type=jnp.float32),
        ]
    ).astype(jnp.bfloat16)
    regrouped = lax.all_to_all(projected, "head", split_axis=2, concat_axis=1, tiled=True)
    prior_pairs = from_behind(regrouped[1:, block_len - WIN :], "seq", 1)
    pairs_ext = jnp.concatenate([prior_pairs, regrouped[1:]], axis=1)
    query_heads = regrouped[0].reshape(block_len, heads_here, head_width)
    key_ext = pairs_ext[0].reshape(block_len + WIN, heads_here, head_width)
    value_ext = pairs_ext[1].reshape(block_len + WIN, heads_here, head_width)
    block_base = lax.axis_index("seq") * block_len
    padded_segs = jnp.concatenate([jnp.full((WIN,), -1, jnp.int32), segments])
    seg_ext = lax.dynamic_slice_in_dim(padded_segs, block_base, block_len + WIN, 0)
    seg_block = seg_ext[WIN:]
    seg_before = seg_ext[WIN - 1]
    onehot_table = jnp.asarray(bucket_onehot(WIN, BUCKETS))
    by_distance = jnp.dot(rel_table, onehot_table.T, precision=highest)
    bias_ext = jnp.concatenate(
        [
            jnp.zeros((heads_here, WIN - 1), jnp.float32),
            by_distance,
            jnp.zeros((heads_here, WIN), jnp.float32),
        ],
        axis=1,
    )
    bias_full, skew_back = jax.vjp(lambda extended: skewed(extended, WIN, 2 * WIN), bias_ext)
    row_pos = jnp.arange(WIN, dtype=jnp.int32)[:, None]
    col_pos = jnp.arange(2 * WIN, dtype=jnp.int32)[None, :]
    near = (row_pos - col_pos + WIN >= 0) & (row_pos - col_pos + WIN < WIN)

    def block_inputs(number):
        start = number * WIN
        query_b = lax.dynamic_slice_in_dim(query_heads, start, WIN, 0)
        key_b = lax.dynamic_slice_in_dim(key_ext, start, 2 * WIN, 0)
        value_b = lax.dynamic_slice_in_dim(value_ext, start, 2 * WIN, 0)
        seg_q = lax.dynamic_slice_in_dim(seg_block, start, WIN, 0)
        seg_k = lax.dynamic_slice_in_dim(seg_ext, start, 2 * WIN, 0)
        visible = near & (seg_q[:, None] == seg_k[None, :])
        raw = jnp.einsum("ihd,jhd->hij", query_b, key_b, preferred_element_type=jnp.float32) * scale
        scores = jnp.where(visible[None], raw + bias_full, negative)
        return (query_b, key_b, value_b, scores)

    def forward_block(number):
        query_b, key_b, value_b, scores = block_inputs(number)
        top_score = jnp.max(scores, axis=-1, keepdims=True)
        exp_scores = jnp.exp(scores - top_score)
        total_mass = jnp.sum(exp_scores, axis=-1, keepdims=True)
        softmax_w = exp_scores / total_mass
        attended_b = jnp.einsum(
            "hij,jhd->ihd",
            softmax_w.astype(jnp.bfloat16),
            value_b,
            preferred_element_type=jnp.float32,
        )
        return (attended_b, (top_score + jnp.log(total_mass))[..., 0])

    numbers = jnp.arange(block_count, dtype=jnp.int32)
    attended_blocks, log_mass = lax.map(forward_block, numbers)
    attended = attended_blocks.reshape(block_len, heads_here, head_width)
    query_f = query_heads.astype(jnp.float32)
    key_f = key_ext[WIN:].astype(jnp.float32)
    value_f = value_ext[WIN:].astype(jnp.float32)

    def states_here(query_a, key_a, value_a, rates):
        return local_states(query_a, key_a, value_a, rates, seg_block, seg_before)

    (readout_local, state_local), states_back = jax.vjp(
        states_here, query_f, key_f, value_f, decay_rate
    )
    position = jnp.arange(block_len).astype(jnp.float32)
    live_mask = (seg_block == seg_before).astype(jnp.float32)
    enter_decay = (
        jnp.exp(-decay_rate[None, :] * (position[:, None] + 1.0)) * live_mask[:, None] * state_scale
    )
    carry_keep = jnp.exp(-decay_rate * block_len) * (seg_block[-1] == seg_before).astype(
        jnp.float32
    )
    identity = (jnp.ones_like(carry_keep), jnp.zeros_like(state_local))
    carried = prefix((carry_keep, state_local), "seq", compose, identity, False)
    carry_in = carried[1]
    carry_term = (
        jnp.einsum("ihd,hde->ihe", query_f, carry_in, precision=highest) * enter_decay[:, :, None]
    )
    mixed_heads = (
        (attended + readout_local + carry_term).astype(jnp.bfloat16).reshape(block_len, pair_width)
    )
    mixed_tok = lax.all_to_all(mixed_heads, "head", split_axis=0, concat_axis=1, tiled=True)
    resid_one = inputs_f + jnp.dot(mixed_tok, full_out, preferred_element_type=jnp.float32)
    scaled_two, norm_back_two = jax.vjp(rms_scale, resid_one, gain_two.astype(jnp.float32))
    normed_two = scaled_two.astype(jnp.bfloat16)
    up_proj = jnp.dot(normed_two, full_up, preferred_element_type=jnp.float32)
    activated, gelu_back = jax.vjp(jax.nn.gelu, up_proj)
    act_low = activated.astype(jnp.bfloat16)
    output = (resid_one + jnp.dot(act_low, full_down, preferred_element_type=jnp.float32)).astype(
        jnp.bfloat16
    )
    back_query, back_key, back_value = (full_query, full_key, full_value)
    back_out, back_up, back_down = (full_out, full_up, full_down)
    grad_down_w = transposed_times(act_low, cotangent)
    act_grad = times_transposed(cotangent, back_down)
    up_grad = gelu_back(act_grad)[0].astype(jnp.bfloat16)
    grad_up_w = transposed_times(normed_two, up_grad)
    normed_two_grad = times_transposed(up_grad, back_up)
    resid_grad_n, grad_gain_two = norm_back_two(normed_two_grad)
    resid_grad = cotangent.astype(jnp.float32) + resid_grad_n
    attn_grad = resid_grad.astype(jnp.bfloat16)
    grad_out_w = transposed_times(mixed_tok, attn_grad)
    mixed_grad = times_transposed(attn_grad, back_out).astype(jnp.bfloat16)
    heads_grad = lax.all_to_all(mixed_grad, "head", split_axis=1, concat_axis=0, tiled=True)
    heads_grad3 = heads_grad.reshape(block_len, heads_here, head_width)

    def backward_block(item):
        number, log_block = item
        query_b, key_b, value_b, scores = block_inputs(number)
        out_grad_b = lax.dynamic_slice_in_dim(heads_grad3, number * WIN, WIN, 0)
        softmax_w = jnp.exp(scores - log_block[..., None])
        prob_grad = jnp.einsum(
            "ihd,jhd->hij", out_grad_b, value_b, preferred_element_type=jnp.float32
        )
        score_grad = softmax_w * (
            prob_grad - jnp.sum(softmax_w * prob_grad, axis=-1, keepdims=True)
        )
        score_low = score_grad.astype(jnp.bfloat16)
        query_grad_b = (
            jnp.einsum("hij,jhd->ihd", score_low, key_b, preferred_element_type=jnp.float32) * scale
        )
        key_grad_b = (
            jnp.einsum("hij,ihd->jhd", score_low, query_b, preferred_element_type=jnp.float32)
            * scale
        )
        value_grad_b = jnp.einsum(
            "hij,ihd->jhd",
            softmax_w.astype(jnp.bfloat16),
            out_grad_b,
            preferred_element_type=jnp.float32,
        )
        ext_grad_b = skew_back(score_low.astype(jnp.float32))[0]
        return (query_grad_b, key_grad_b, value_grad_b, ext_grad_b)

    query_grads, key_grads, value_grads, ext_grads = lax.map(backward_block, (numbers, log_mass))
    query_grad_att = query_grads.reshape(block_len, heads_here, head_width)

    def fold_pairs(pieces):
        zero_edge = jnp.zeros_like(pieces[:1, :WIN])
        return jnp.concatenate([pieces[:, :WIN], zero_edge], axis=0) + jnp.concatenate(
            [zero_edge, pieces[:, WIN:]], axis=0
        )

    key_folded = fold_pairs(key_grads)
    value_folded = fold_pairs(value_grads)
    sent_pairs = jnp.stack([key_folded[0], value_folded[0]]).reshape(2, WIN, pair_width)
    received = from_behind(sent_pairs.astype(jnp.bfloat16), "seq", -1).astype(sent_pairs.dtype)
    tail_pairs = jnp.concatenate(
        [jnp.zeros((2, block_len - WIN, pair_width), jnp.float32), received], axis=1
    )
    tail_pairs = tail_pairs.reshape(2, block_len, heads_here, head_width)
    key_grad_att = key_folded[1:].reshape(block_len, heads_here, head_width) + tail_pairs[0]
    value_grad_att = value_folded[1:].reshape(block_len, heads_here, head_width) + tail_pairs[1]
    heads_grad_f = heads_grad3.astype(jnp.float32)
    grad_local = jnp.einsum(
        "ihd,ihe->hde", query_f * enter_decay[:, :, None], heads_grad_f, precision=highest
    )
    back_chain = prefix((carry_keep, grad_local), "seq", compose, identity, True)
    carry_out_grad = back_chain[1]
    query_grad_s, key_grad_s, value_grad_s, rate_grad_s = states_back(
        (heads_grad_f, carry_out_grad)
    )
    query_grad_c = (
        jnp.einsum("ihe,hde->ihd", heads_grad_f, carry_in, precision=highest)
        * enter_decay[:, :, None]
    )
    rate_grad_c = -jnp.sum(heads_grad_f * carry_term * (position[:, None, None] + 1.0), axis=(0, 2))
    rate_grad_a = -block_len * carry_keep * jnp.sum(carry_out_grad * carry_in, axis=(1, 2))
    rate_grad = rate_grad_s + rate_grad_c + rate_grad_a
    query_grad = query_grad_att + query_grad_s + query_grad_c
    key_grad = key_grad_att + key_grad_s
    value_grad = value_grad_att + value_grad_s
    triple_grad = (
        jnp.stack([query_grad, key_grad, value_grad])
        .reshape(3, block_len, pair_width)
        .astype(jnp.bfloat16)
    )
    token_grads = lax.all_to_all(triple_grad, "head", split_axis=1, concat_axis=2, tiled=True)
    grad_query_w = transposed_times(normed, token_grads[0])
    grad_key_w = transposed_times(normed, token_grads[1])
    grad_value_w = transposed_times(normed, token_grads[2])
    normed_grad = (
        times_transposed(token_grads[0], back_query)
        + times_transposed(token_grads[1], back_key)
        + times_transposed(token_grads[2], back_value)
    )
    input_grad_n, grad_gain_one = norm_back_one(normed_grad)
    input_grad = (resid_grad + input_grad_n).astype(jnp.bfloat16)
    ext_total = jnp.sum(ext_grads, axis=0)
    table_grad = jnp.dot(ext_total[:, WIN - 1 : 2 * WIN - 1], onehot_table, precision=highest)
    table_grad, rate_grad = lax.psum((table_grad, rate_grad), "seq")
    summed = (
        lax.psum_scatter(grad_query_w, ("head", "seq"), scatter_dimension=0, tiled=True),
        lax.psum_scatter(grad_key_w, ("head", "seq"), scatter_dimension=0, tiled=True),
        lax.psum_scatter(grad_value_w, ("head", "seq"), scatter_dimension=0, tiled=True),
        lax.psum_scatter(grad_out_w, ("head", "seq"), scatter_dimension=0, tiled=True),
        lax.psum_scatter(grad_up_w, ("head", "seq"), scatter_dimension=0, tiled=True),
        lax.psum_scatter(grad_down_w, ("head", "seq"), scatter_dimension=0, tiled=True),
        lax.psum_scatter(grad_gain_one, ("head", "seq"), scatter_dimension=0, tiled=True),
        lax.psum_scatter(grad_gain_two, ("head", "seq"), scatter_dimension=0, tiled=True),
    )
    grad_query, grad_key, grad_value, grad_out, grad_up, grad_down, grad_norm_one, grad_norm_two = (
        summed
    )
    return (
        output,
        input_grad,
        grad_query,
        grad_key,
        grad_value,
        grad_out,
        grad_up,
        grad_down,
        grad_norm_one,
        grad_norm_two,
        table_grad,
        rate_grad,
    )


def solution(mesh):
    return jax.shard_map(
        shards,
        mesh=mesh,
        in_specs=(
            P(("seq", "head"), None),
            P(("seq", "head"), None),
            P(),
            P(("head", "seq"), None),
            P(("head", "seq"), None),
            P(("head", "seq"), None),
            P(("head", "seq"), None),
            P(("head", "seq"), None),
            P(("head", "seq"), None),
            P(("head", "seq")),
            P(("head", "seq")),
            P("head", None),
            P("head"),
        ),
        out_specs=(
            P(("seq", "head"), None),
            P(("seq", "head"), None),
            P(("head", "seq"), None),
            P(("head", "seq"), None),
            P(("head", "seq"), None),
            P(("head", "seq"), None),
            P(("head", "seq"), None),
            P(("head", "seq"), None),
            P(("head", "seq")),
            P(("head", "seq")),
            P("head", None),
            P("head"),
        ),
        check_vma=False,
    )
```

profile of v0, /device:TPU:0, one launch (start us, length us, event | category | flops | bytes accessed | tf_op | source)
XLA Modules:
  0.0 1545.7 jit_solution(12134204792197994471)
XLA Ops:
  12.9 42.1 %all-reduce.16 = (bf16[1024]{0:T(1024)(128)(2,1)S(1)}, bf16[1024]{0:T(1024)(128)(2,1)}) all-reduce(bf16[1024]{0:T(1024)(128)(2,1)S(1)} %dynamic-update-slice, bf16[1024]{0:T(1024)(128)(2,1)S(1)} %dynamic-update-slice.2), channel_id=1, replica_groups=mesh['head'=4,'seq'=8] {'head','seq'}, use_global_device_ids=true, to_apply=%add.9 | all-reduce | flops 2048 | bytes 8192
  72.6 56.0 %all-gather.12.cloned.1.call-done = bf16[1024,1024]{1,0:T(8,128)(2,1)} async-done(((bf16[32,1024]{1,0:T(8,128)(2,1)}), bf16[1024,1024]{1,0:T(8,128)(2,1)}) %all-gather.12.cloned.1.call-update) | async-done | bytes 2097168 | tf_op jit(solution)/shard_map/all_gather | solution.py:165
  131.0 56.0 %all-gather.10.cloned.1.call-done = bf16[1024,1024]{1,0:T(8,128)(2,1)} async-done(((bf16[32,1024]{1,0:T(8,128)(2,1)}), bf16[1024,1024]{1,0:T(8,128)(2,1)}) %all-gather.10.cloned.1.call-update) | async-done | bytes 2097168 | tf_op jit(solution)/shard_map/all_gather | solution.py:164
  198.8 15.6 %all-reduce.10 = bf16[16]{0:T(256)(128)(2,1)S(1)} all-reduce(bf16[16]{0:T(256)(128)(2,1)S(1)} %dynamic-update-slice.1), channel_id=2, replica_groups=mesh['head'=4,'seq'=8] {'seq'}, use_global_device_ids=true, to_apply=%add.10 | all-reduce | flops 16 | bytes 64
  226.0 12.9 reshape.700
  272.3 47.4 %while.129 = (s32[]{:T(128)}, f32[2,128,128]{2,1,0:T(8,128)S(1)}, s32[]{:T(128)}, f32[2,512,2,128]{1,3,2,0:T(8,128)}, pred[2,2,512,512]{3,2,1,0:T(32,128)(4,1)},...) while((s32[]{:T(128)}, f32[2,128,128]{2,1,0:T(8,128)S(1)}, ...), condition=%wide.region_6.7_spmd.clone.clone.clone, body=%wide.region_5.6_spmd.clone.clone.clone.sunk | while | flops 2019735552 | bytes 42637320 | solution.py:137
  319.7 16.8 %all-gather.1 = bf16[16,128,128]{2,1,0:T(8,128)(2,1)S(1)} all-gather(bf16[2,128,128]{2,1,0:T(8,128)(2,1)S(1)} %convert_element_type.257), channel_id=3, replica_groups=mesh['head'=4,'seq'=8] {'seq'}, dimensions={0}, use_global_device_ids=true | all-gather | bytes 589824 | tf_op jit(solution)/shard_map/all_gather | solution.py:31
  350.3 17.7 %while.127 = (s32[]{:T(128)}, f32[2,512,2,128]{1,3,2,0:T(8,128)}, f32[2,2,512]{2,1,0:T(2,128)}, s32[2]{0:T(128)S(1)}, bf16[1536,2,128]{0,2,1:T(8,128)(2,1)S(1)},...) while((s32[]{:T(128)}, f32[2,512,2,128]{1,3,2,0:T(8,128)}, ...), condition=%wide.region_4.5_spmd.clone, body=%wide.region_1.4_spmd.clone.sunk | while | flops 549977088 | bytes 28100924 | solution.py:237
  400.4 17.1 %all-gather.18.cloned.1.call-done = bf16[1024,4096]{1,0:T(8,128)(2,1)} async-done(((bf16[32,4096]{1,0:T(8,128)(2,1)}), bf16[1024,4096]{1,0:T(8,128)(2,1)}) %all-gather.18.cloned.1.call-update) | async-done | bytes 8388624 | tf_op jit(solution)/shard_map/all_gather | solution.py:168
  417.5 11.4 fusion.186
  449.1 16.1 %all-gather.2 = bf16[16,128,128]{2,1,0:T(8,128)(2,1)S(1)} all-gather(bf16[2,128,128]{2,1,0:T(8,128)(2,1)S(1)} %convolution_convert_fusion.4), channel_id=4, replica_groups=mesh['head'=4,'seq'=8] {'seq'}, dimensions={0}, use_global_device_ids=true | all-gather | bytes 589824 | tf_op jit(solution)/shard_map/all_gather | solution.py:31
  475.7 72.2 %while.128 = (s32[]{:T(128)}, f32[2,512,2,128]{3,1,2,0:T(8,128)}, f32[2,1024,2,128]{1,3,2,0:T(8,128)}, f32[2,1024,2,128]{1,3,2,0:T(8,128)}, f32[2,2,1535]{2,1,0:...) while((s32[]{:T(128)}, f32[2,512,2,128]{3,1,2,0:T(8,128)}, ...), condition=%wide.region_14.15_spmd.clone, body=%wide.region_11.14_spmd.clone.sunk | while | flops 1359867904 | bytes 143219280 | solution.py:319
  551.5 122.8 %while.130 = (s32[]{:T(128)}, f32[2]{0:T(128)}, f32[2,128,128]{2,1,0:T(8,128)S(1)}, f32[2,512,2,128]{3,1,2,0:T(8,128)}, f32[2,512,2,128]{1,0,3,2:T(2,128)}, /*in...) while((s32[]{:T(128)}, f32[2]{0:T(128)}, ...), condition=%wide.region_24.25_spmd.clone.clone.clone, body=%wide.region_17.24_spmd.clone.clone.clone.sunk | while | flops 4033751552 | bytes 99034424 | solution.py:137
  591.3 10.3 dynamic_update_slice.241
  652.5 10.3 dynamic_update_slice.241
  706.0 29.5 %all_to_all.68 = bf16[3,1024,256]{2,0,1:T(4,128)(2,1)S(1)} all-to-all(bf16[3,1024,256]{2,0,1:T(4,128)(2,1)S(1)} %copy.228), channel_id=1, replica_groups=mesh['head'=4,'seq'=8] {'head'}, dimensions={1} | all-to-all | bytes 3145728 | tf_op jit(solution)/shard_map/all_to_all | solution.py:362
  760.5 10.9 fusion.229
  782.4 14.5 all-reduce.15
  802.2 37.3 %all-reduce.14 = (f32[1024]{0:T(1024)S(1)}, f32[1024]{0:T(1024)S(1)}) all-reduce(f32[1024]{0:T(1024)S(1)} %get-tuple-element.1961, f32[1024]{0:T(1024)S(1)} %copy-done.114), channel_id=11, replica_groups=mesh['head'=4,'seq'=8] {'head','seq'}, use_global_device_ids=true, to_apply=%region_33.34.clone | all-reduce | flops 2048 | bytes 16384
  841.9 38.9 %reduce-scatter.7.cloned.1.call-done = f32[32,1024]{1,0:T(8,128)} async-done(((f32[1024,1024]{1,0:T(8,128)}), f32[32,1024]{1,0:T(8,128)}) %reduce-scatter.7.cloned.1.call-update) | async-done | bytes 131088 | tf_op jit(solution)/shard_map/reduce_scatter | solution.py:377
  880.8 141.9 %reduce-scatter.9.cloned.1.call-done = f32[32,1024]{1,0:T(8,128)} async-done(((f32[1024,1024]{1,0:T(8,128)}), f32[32,1024]{1,0:T(8,128)}) %reduce-scatter.9.cloned.1.call-update) | async-done | bytes 131088 | tf_op jit(solution)/shard_map/reduce_scatter | solution.py:378
  1022.7 142.5 %reduce-scatter.11.cloned.1.call-done = f32[32,1024]{1,0:T(8,128)} async-done(((f32[1024,1024]{1,0:T(8,128)}), f32[32,1024]{1,0:T(8,128)}) %reduce-scatter.11.cloned.1.call-update) | async-done | bytes 131088 | tf_op jit(solution)/shard_map/reduce_scatter | solution.py:379
  1165.3 186.2 %reduce-scatter.15.cloned.1.call-done = f32[32,4096]{1,0:T(8,128)} async-done(((f32[1024,4096]{1,0:T(8,128)}), f32[32,4096]{1,0:T(8,128)}) %reduce-scatter.15.cloned.1.call-update) | async-done | bytes 524304 | tf_op jit(solution)/shard_map/reduce_scatter | solution.py:381
  1351.5 187.1 %reduce-scatter.17.cloned.1.call-done = f32[128,1024]{1,0:T(8,128)} async-done(((f32[4096,1024]{1,0:T(8,128)}), f32[128,1024]{1,0:T(8,128)}) %reduce-scatter.17.cloned.1.call-update) | async-done | bytes 524304 | tf_op jit(solution)/shard_map/reduce_scatter | solution.py:382
  (685 shorter events, 472.4 us)
Async XLA Ops:
  7.2 49.6 %copy-start = (f32[2,32]{1,0:T(2,128)S(1)}, f32[2,32]{1,0:T(2,128)}, u32[]{:S(2)}) copy-start(f32[2,32]{1,0:T(2,128)} %param.37) | copy-start | bytes 772
  7.2 63.1 %all-gather.14.cloned.1.call-start = ((), (), s32[]{:S(2)}) async-start(), calls=%async_computation.12 | async-start | bytes 2162688 | tf_op jit(solution)/shard_map/all_gather | solution.py:166
  7.9 120.7 %all-gather.12.cloned.1.call-start = ((), (), s32[]{:S(2)}) async-start(), calls=%async_computation.11 | async-start | bytes 2162688 | tf_op jit(solution)/shard_map/all_gather | solution.py:165
  8.7 178.3 %all-gather.10.cloned.1.call-start = ((), (), s32[]{:S(2)}) async-start(), calls=%async_computation.10 | async-start | bytes 2162688 | tf_op jit(solution)/shard_map/all_gather | solution.py:164
  9.4 379.9 %all-gather.16.cloned.1.call-start = ((), (), s32[]{:S(2)}) async-start(), calls=%async_computation.13 | async-start | bytes 2162688 | tf_op jit(solution)/shard_map/all_gather | solution.py:167
  10.0 381.9 %all-gather.20.cloned.1.call-start = ((), (), s32[]{:S(2)}) async-start(), calls=%async_computation.15 | async-start | bytes 8650752 | tf_op jit(solution)/shard_map/all_gather | solution.py:169
  10.6 406.9 %all-gather.18.cloned.1.call-start = ((), (), s32[]{:S(2)}) async-start(), calls=%async_computation.14 | async-start | bytes 8650752 | tf_op jit(solution)/shard_map/all_gather | solution.py:168
  55.0 132.0 %copy-start.94 = (f32[1024]{0:T(1024)}, f32[1024]{0:T(1024)S(1)}, u32[]{:S(2)}) copy-start(f32[1024]{0:T(1024)S(1)} %convert_element_type.246) | copy-start | bytes 12292
  56.2 130.8 %copy-start.103 = (f32[256]{0:T(256)}, f32[256]{0:T(256)S(1)}, u32[]{:S(2)}) copy-start(f32[256]{0:T(256)S(1)} %fusion.223) | copy-start | bytes 3076
  192.1 55.2 %all-to-all-start = ((bf16[3,256,1024]{1,0,2:T(4,128)(2,1)}), bf16[3,256,1024]{1,0,2:T(4,128)(2,1)}, u32[]{:S(2)}, u32[]{:S(2)}) async-start(bf16[3,256,1024]{1,0,2:T(4,128)(2,1)} %copy.180), calls=%async_computation | async-start | bytes 4194304 | tf_op jit(solution)/shard_map/all_to_all | solution.py:184
  198.8 45.8 %copy-start.92 = (s32[1024]{0:T(1024)}, s32[1024]{0:T(1024)S(1)}, u32[]{:S(2)}) copy-start(s32[1024]{0:T(1024)S(1)} %get-tuple-element.3115) | copy-start | bytes 12292
  252.7 89.1 %collective-permute-start = (bf16[2,512,256]{2,1,0:T(8,128)(2,1)}, bf16[2,512,256]{2,1,0:T(8,128)(2,1)}, u32[]{:S(2)}, u32[]{:S(2)}) collective-permute-start(bf16[2,512,256]{2,1,0:T(8,128)(2,1)} %slice.152), channel_id=1, source_target_pairs={{0,1},{1,2},{2,3},{3,4},{4,5},{5,6},{6,7},{8,9},{9,10},{10,11},{11... | collective-permute-start | bytes 1572872 | tf_op jit(solution)/shard_map/ppermute | solution.py:23
  375.1 13.2 all-to-all-start.1
  379.0 53.2 %copy-start.90 = (f32[1024]{0:T(1024)}, f32[1024]{0:T(1024)S(1)}, u32[]{:S(2)}) copy-start(f32[1024]{0:T(1024)S(1)} %convert_element_type.261) | copy-start | bytes 12292
  391.9 40.2 %copy-start.109 = (f32[256]{0:T(256)}, f32[256]{0:T(256)S(1)}, u32[]{:S(2)}) copy-start(f32[256]{0:T(256)S(1)} %fusion.224) | copy-start | bytes 3076
  435.6 12.2 all-to-all-start.2
  439.1 402.8 %reduce-scatter.13.cloned.1.call-start = ((), (), s32[]{:S(2)}) async-start(), calls=%async_computation.19 | async-start | bytes 4325376 | tf_op jit(solution)/shard_map/reduce_scatter | solution.py:380
  444.2 436.6 %reduce-scatter.7.cloned.1.call-start = ((), (), s32[]{:S(2)}) async-start(), calls=%async_computation.16 | async-start | bytes 4325376 | tf_op jit(solution)/shard_map/reduce_scatter | solution.py:377
  682.0 17.7 %collective-permute-start.1 = (bf16[2,512,256]{1,2,0:T(8,128)(2,1)}, bf16[2,512,256]{1,2,0:T(8,128)(2,1)}, u32[]{:S(2)}, u32[]{:S(2)}) collective-permute-start(bf16[2,512,256]{1,2,0:T(8,128)(2,1)} %bitcast.26), channel_id=1, source_target_pairs={{1,0},{2,1},{3,2},{4,3},{5,4},{6,5},{7,6},{9,8},{10,9},{11,10},{12... | collective-permute-start | bytes 1572872 | tf_op jit(solution)/shard_map/ppermute | solution.py:23
  741.1 281.7 %reduce-scatter.9.cloned.1.call-start = ((), (), s32[]{:S(2)}) async-start(), calls=%async_computation.17 | async-start | bytes 4325376 | tf_op jit(solution)/shard_map/reduce_scatter | solution.py:378
  745.2 420.1 %reduce-scatter.11.cloned.1.call-start = ((), (), s32[]{:S(2)}) async-start(), calls=%async_computation.18 | async-start | bytes 4325376 | tf_op jit(solution)/shard_map/reduce_scatter | solution.py:379
  749.3 602.2 %reduce-scatter.15.cloned.1.call-start = ((), (), s32[]{:S(2)}) async-start(), calls=%async_computation.20 | async-start | bytes 17301504 | tf_op jit(solution)/shard_map/reduce_scatter | solution.py:381
  760.4 778.2 %reduce-scatter.17.cloned.1.call-start = ((), (), s32[]{:S(2)}) async-start(), calls=%async_computation.21 | async-start | bytes 17301504 | tf_op jit(solution)/shard_map/reduce_scatter | solution.py:382
  801.3 737.4 %copy-start.1 = (f32[2,32]{1,0:T(2,128)S(1)}, f32[2,32]{1,0:T(2,128)}, u32[]{:S(2)}) copy-start(f32[2,32]{1,0:T(2,128)} %param.37) | copy-start | bytes 772
  (158 other events, 831.9 us)
Sparse Core Ops, SparseCore 0:
  11.0 59.2 all-gather.13
  73.3 55.2 all-gather.11
  131.6 55.3 all-gather.9
  189.8 64.8 all-gather.15
  257.5 79.4 all-gather.19
  339.9 77.5 all-gather.17
  444.3 143.9 reduce-scatter.12
  741.2 139.5 reduce-scatter.6
  883.7 139.0 reduce-scatter.8
  1025.4 139.7 reduce-scatter.10
  1168.1 183.3 reduce-scatter.14
  1354.2 184.3 reduce-scatter.16
where the time goes:
time: 1560 us; the launch traced here: 1550 us
  waiting for transfers between devices  847 us (54%)
  local copies, waits for them, and re-layouts  227 us (15%)
  matrix products  183 us (12%)
  blocking collectives  172 us (11%)
  other arithmetic  73.9 us (5%)
  between operations  17.6 us (1%)
  starting transfers between devices  16.7 us (1%)
    reduce_scatter x1, waiting for transfers between devices, shards(): lax.psum_scatter(grad_down_w, ('head', 'seq'), scatter_dimension=0, tiled...  187 us
    reduce_scatter x1, waiting for transfers between devices, shards(): lax.psum_scatter(grad_up_w, ('head', 'seq'), scatter_dimension=0, tiled=T...  186 us
    reduce_scatter x1, waiting for transfers between devices, shards(): lax.psum_scatter(grad_value_w, ('head', 'seq'), scatter_dimension=0, tile...  143 us
    reduce_scatter x1, waiting for transfers between devices, shards(): lax.psum_scatter(grad_key_w, ('head', 'seq'), scatter_dimension=0, tiled=...  142 us
    unnamed x3, blocking collectives  95.1 us
    all_gather x1, waiting for transfers between devices, shards(): lax.all_gather(w_query, ('head', 'seq'), axis=0, tiled=True)  56 us
    all_gather x1, waiting for transfers between devices, shards(): lax.all_gather(w_key, ('head', 'seq'), axis=0, tiled=True)  56 us
    reduce_scatter x1, waiting for transfers between devices, shards(): lax.psum_scatter(grad_query_w, ('head', 'seq'), scatter_dimension=0, tile...  38.9 us
  transfers between devices with their start and end apart: 17, of which 11 were waited for; matrix products, arithmetic and copies ran while one was open for 29% of the time, Pallas kernels for 0%

commit v1 on v0

--- a/solution.py
+++ b/solution.py
@@ -1,19 +1,1024 @@
+import functools
 import math
 
 import jax
 import jax.numpy as jnp
 import numpy as np
 from jax import lax
+from jax.experimental import pallas as pl
+from jax.experimental.pallas import tpu as pltpu
 from jax.sharding import PartitionSpec as P
 
 HD = 128
 BUCKETS = 32
 WIN = 512
-
+TILE = 256
 
 epsilon = 1e-06
 negative = -1e30
 state_scale = 1.0 / 1024.0
+MESH = pl.DeviceIdType.MESH
+f32 = jnp.float32
+bf16 = jnp.bfloat16
+
+
+def dot(a, b):
+    return jnp.dot(a, b, preferred_element_type=f32)
+
+
+def dot_t(a, b):
+    return lax.dot_general(a, b, (((1,), (1,)), ((), ())), preferred_element_type=f32)
+
+
+def t_dot(a, b):
+    return lax.dot_general(a, b, (((0,), (0,)), ((), ())), preferred_element_type=f32)
+
+
+class Place:
+    def __init__(self):
+        self.h = lax.axis_index("head")
+        self.s = lax.axis_index("seq")
+        self.n = lax.axis_size("seq")
+        self.nz = self.n // 2
+        self.z = self.s // 2
+        self.core = self.s % 2
+        x, y = self.h % 2, self.h // 2
+        self.heads = [2 * y + 1 - x, 2 * (1 - y) + x, 2 * (1 - y) + 1 - x]
+
+    def head_dev(self, k):
+        return (self.heads[k], self.s)
+
+    def z_to(self, k):
+        return ((self.z + k) % self.nz) * 2 + self.core
+
+    def z_from(self, k):
+        return ((self.z + self.nz - k) % self.nz) * 2 + self.core
+
+    def z_dev(self, k):
+        return (self.h, self.z_to(k))
+
+    def other(self):
+        return self.z * 2 + 1 - self.core
+
+    def core_dev(self):
+        return (self.h, self.other())
+
+    def seq_dev(self, by):
+        return (self.h, (self.s + self.n + by) % self.n)
+
+
+def greet(devices):
+    barrier = pltpu.get_barrier_semaphore()
+    for device in devices:
+        pl.semaphore_signal(barrier, inc=1, device_id=device, device_id_type=MESH)
+    pl.semaphore_wait(barrier, len(devices))
+
+
+class Sends:
+    def __init__(self, send_sems, recv_sems):
+        self.send_sems, self.recv_sems = send_sems, recv_sems
+        self.at, self.all = 0, []
+
+    def put(self, src, dst, device, start=True):
+        copy = pltpu.make_async_remote_copy(
+            src_ref=src,
+            dst_ref=dst,
+            send_sem=self.send_sems.at[self.at],
+            recv_sem=self.recv_sems.at[self.at],
+            device_id=device,
+            device_id_type=MESH,
+        )
+        self.at += 1
+        self.all.append(copy)
+        if start:
+            copy.start()
+        return copy
+
+    def finish(self):
+        for copy in self.all:
+            copy.wait_send()
+
+
+def rms(x):
+    return lax.rsqrt(jnp.mean(x * x, axis=-1, keepdims=True) + epsilon)
+
+
+def kernel_one(
+    tok_ref, p1_ref, wo_ref, hall_ref, qkv_ref, wb_ref, woz_ref, gains_ref,
+    xa, a1, send_sems, recv_sems,
+):
+    me = Place()
+    nz, rows = me.nz, wo_ref.shape[0]
+    tok = tok_ref.shape[0]
+    peers = [me.head_dev(k) for k in range(3)]
+    greet(peers + [me.z_dev(k) for k in range(1, nz)] + [me.core_dev()])
+    sends = Sends(send_sems, recv_sems)
+    first = [sends.put(p1_ref.at[me.heads[k]], a1.at[me.h], peers[k]) for k in range(3)]
+    wo_z = [sends.put(wo_ref, woz_ref.at[me.s], me.z_dev(k)) for k in range(1, nz)]
+    toks = [sends.put(tok_ref, xa.at[me.h], peers[k]) for k in range(3)]
+    wo_c = [sends.put(wo_ref, woz_ref.at[me.s], me.core_dev())]
+    woz_ref[me.s] = wo_ref[...]
+    a1[me.h] = p1_ref[me.h]
+    xa[me.h] = tok_ref[...]
+    for copy in first:
+        copy.wait_recv()
+    w_z = [sends.put(a1, wb_ref.at[:, me.s], me.z_dev(k)) for k in range(1, nz)]
+    w_c = [sends.put(a1, wb_ref.at[:, me.s], me.core_dev())]
+    wb_ref[:, me.s] = a1[...]
+    for k in range(1, nz):
+        wo_z[k - 1].wait_recv()
+        piece = woz_ref.at[me.z_from(k)]
+        wo_c.append(sends.put(piece, piece, me.core_dev()))
+    for k in range(1, nz):
+        w_z[k - 1].wait_recv()
+        piece = wb_ref.at[:, me.z_from(k)]
+        w_c.append(sends.put(piece, piece, me.core_dev()))
+    for copy in wo_c + w_c:
+        copy.wait_recv()
+    group = 128 // rows
+    lanes = []
+    for h in range(4):
+        for s in range(0, me.n, group):
+            lanes.append(sum(wb_ref[h, s + i, :, 768:896].astype(f32) for i in range(group)))
+    gains = jnp.concatenate(lanes, axis=1)[0:8]
+    gains_ref[...] = gains
+    gain_one = gains[0:1]
+    for copy in toks:
+        copy.wait_recv()
+
+    def block(b, _):
+        x = xa[b].astype(f32)
+        hb = (x * rms(x) * gain_one).astype(bf16)
+        at = pl.ds(pl.multiple_of(b * tok, tok), tok)
+        hall_ref[at] = hb
+        w = wb_ref[...].reshape(4 * me.n * rows, 896)
+        for j in range(3):
+            out = dot(hb, w[:, j * 256 : j * 256 + 256]).astype(bf16)
+            qkv_ref[2 * j, at] = out[:, :HD]
+            qkv_ref[2 * j + 1, at] = out[:, HD:]
+        return 0
+
+    lax.fori_loop(0, 4, block, 0)
+    sends.finish()
+
+
+def call(kernel, collective_id, outs, scratch, copies, name, *args, scalars=0):
+    return pl.pallas_call(
+        kernel,
+        out_shape=[jax.ShapeDtypeStruct(shape, kind) for shape, kind in outs],
+        in_specs=[pl.BlockSpec(memory_space=pltpu.SMEM)] * scalars
+        + [pl.BlockSpec(memory_space=pltpu.VMEM)] * (len(args) - scalars),
+        out_specs=[pl.BlockSpec(memory_space=pltpu.VMEM)] * len(outs),
+        scratch_shapes=[pltpu.VMEM(shape, kind) for shape, kind in scratch]
+        + [pltpu.SemaphoreType.DMA((copies,)), pltpu.SemaphoreType.DMA((copies,))],
+        compiler_params=pltpu.CompilerParams(
+            collective_id=collective_id, has_side_effects=True, vmem_limit_bytes=60 << 20
+        ),
+        name=name,
+    )(*args)
+
+
+def packed_rows(w_query, w_key, w_value, norm_one, norm_two):
+    rows = w_query.shape[0]
+    group = 128 // rows
+    lane = np.arange(128) // rows
+    mine = jnp.asarray(lane) == lax.axis_index("seq") % group
+    gains = [jnp.where(mine, jnp.tile(g, group), 0)[None] for g in (norm_one, norm_two)]
+    gains = jnp.concatenate(gains + [jnp.zeros((rows - 2, 128), bf16)], axis=0)
+    gains = jnp.broadcast_to(gains[:, None], (rows, 4, 128))
+    parts = [w.reshape(rows, 4, 256) for w in (w_query, w_key, w_value)]
+    return jnp.concatenate(parts + [gains], axis=2).transpose(1, 0, 2)
+
+
+def stage_one(tokens, w_query, w_key, w_value, w_out, norm_one, norm_two):
+    n = lax.axis_size("seq")
+    rows = w_query.shape[0]
+    p1 = packed_rows(w_query, w_key, w_value, norm_one, norm_two)
+    tok = tokens.shape[0]
+    outs = [
+        ((4 * tok, 1024), bf16),
+        ((6, 4 * tok, HD), bf16),
+        ((4, n, rows, 896), bf16),
+        ((n, rows, 1024), bf16),
+        ((8, 1024), f32),
+    ]
+    scratch = [((4, tok, 1024), bf16), ((4, rows, 896), bf16)]
+    copies = 6 + 2 * (n // 2 - 1) + 2 * (n // 2)
+    return call(kernel_one, 0, outs, scratch, copies, "gather_qkv", tokens, p1, w_out)
+
+
+LOG2E = math.log2(math.e)
+KEY_SCALE = LOG2E / math.sqrt(HD)
+
+
+def bucket_starts():
+    distance = np.arange(WIN)
+    scaled = np.floor(np.log(np.maximum(distance, 1) / 16.0) / np.log(8.0) * 16.0)
+    larger = np.minimum(16 + np.maximum(scaled, 0), BUCKETS - 1)
+    bucket = np.where(distance < 16, distance, larger).astype(np.int32)
+    return [int(np.argmax(bucket == b)) for b in range(BUCKETS)]
+
+
+STARTS = bucket_starts()
+
+
+def grid_of(axis, shape=(TILE, TILE)):
+    return lax.broadcasted_iota(jnp.int32, shape, axis)
+
+
+def column(row):
+    eye = grid_of(0) == grid_of(1)
+    return jnp.sum(jnp.where(eye, row, 0.0), axis=1, keepdims=True)
+
+
+class Segs:
+    def __init__(self, me, seg_ref, rows, cols):
+        total = 4 * me.n
+        self.rows, self.cols = rows, cols
+
+        def row_at(offset):
+            return seg_ref[pl.ds((4 * me.s + total + offset) % total, 1)].astype(f32)
+
+        for j in range(6):
+            row = row_at(j - 2)
+            rows[j] = row
+            if j >= 2:
+                cols[j - 2] = column(row)
+        last = lambda offset: row_at(offset)[:, TILE - 1 : TILE]
+        self.last = [last(j - 2) for j in range(6)]
+        same = lambda a, b: (a == b).astype(f32)
+        self.keep = [same(self.last[t + 2], self.last[t + 1]) for t in range(4)]
+        self.keep_before = same(last(-1), last(-5))
+        self.keep_after = same(last(7), last(3))
+
+    def live(self, t):
+        return (self.cols[t] == self.last[t + 1]).astype(f32)
+
+    def kept(self, t):
+        return (self.cols[t] == self.last[t + 2]).astype(f32)
+
+
+def fill_tables(table_ref, decay_ref, near, far, decay, enter, leave):
+    gap = grid_of(0) - grid_of(1)
+    place = grid_of(0, (TILE, 1)).astype(f32)
+    for head in range(2):
+        rate = decay_ref[0, head]
+        for out, shift in ((near, 0), (far, TILE)):
+            bias = jnp.full((TILE, TILE), table_ref[head, 0] * LOG2E, f32)
+            for b in range(1, BUCKETS):
+                bias = jnp.where(gap + shift >= STARTS[b], table_ref[head, b] * LOG2E, bias)
+            out[head] = jnp.where(gap + shift >= 0, bias, negative)
+        fall = jnp.exp(-rate * jnp.maximum(gap, 0).astype(f32)) * state_scale
+        decay[head] = jnp.where(gap >= 0, fall, 0.0)
+        enter[head] = jnp.exp(-rate * (place + 1.0)) * state_scale
+        leave[head] = jnp.exp(-rate * (TILE - 1.0 - place))
+
+
+def power(rate, steps):
+    return jnp.exp(jnp.full((1, HD), -rate * steps, f32))
+
+
+def tile_scores(raw, head, t, table_ref, near, far, segs):
+    col = segs.cols[t]
+    same = [col == segs.rows[t + j] for j in range(3)]
+    reach = grid_of(0) < grid_of(1)
+    rest = table_ref[head, BUCKETS - 1] * LOG2E
+    s0 = jnp.where(same[0] & reach, raw[:, :TILE] * KEY_SCALE + rest, negative)
+    s1 = jnp.where(same[1], raw[:, TILE : 2 * TILE] * KEY_SCALE + far[head], negative)
+    s2 = jnp.where(same[2], raw[:, 2 * TILE :] * KEY_SCALE + near[head], negative)
+    return s0, s1, s2, same[2]
+
+
+def kernel_two(
+    table_ref, decay_ref, seg_ref, qkv_ref, wup_ref, wdn_ref, cot_ref, woz_ref,
+    y_ref, lse_ref, state_ref, kvx, call_ref, up_ref, dn_ref, wo_ref,
+    u1, near, far, decay, enter, leave, rows, cols, yacc, local, sent, got,
+    send_sems, recv_sems,
+):
+    me = Place()
+    nz = me.nz
+    peers = [me.head_dev(k) for k in range(3)]
+    greet(
+        peers
+        + [me.z_dev(k) for k in range(1, nz)]
+        + [me.core_dev(), me.seq_dev(-1), me.seq_dev(-2)]
+    )
+    sends = Sends(send_sems, recv_sems)
+    half = pl.ds(me.core * nz, nz)
+    other_half = pl.ds((1 - me.core) * nz, nz)
+    width = up_ref.shape[-1]
+    halo = sends.put(qkv_ref.at[2:6, 2 * TILE :], kvx.at[:, : 2 * TILE], me.seq_dev(1))
+    first = []
+    for k in range(3):
+        columns = pl.ds(pl.multiple_of(me.heads[k] * width, width), width)
+        first.append(sends.put(wup_ref.at[:, columns], u1.at[me.h], peers[k]))
+    wo_h = [sends.put(woz_ref.at[half], wo_ref.at[me.h, half], peers[k]) for k in range(3)]
+    cots = [sends.put(cot_ref, call_ref.at[me.h], peers[k]) for k in range(3)]
+    kvx[:, 2 * TILE :] = qkv_ref[2:6]
+    u1[me.h] = wup_ref[:, pl.ds(pl.multiple_of(me.h * width, width), width)]
+    wo_ref[me.h] = woz_ref[...]
+    call_ref[me.h] = cot_ref[...]
+    segs = Segs(me, seg_ref, rows, cols)
+    fill_tables(table_ref, decay_ref, near, far, decay, enter, leave)
+    for head in range(2):
+        fall = power(decay_ref[0, head], float(TILE))
+        state = jnp.zeros((HD, HD), f32)
+        for t in range(4):
+            at = pl.ds(t * TILE, TILE)
+            key = (qkv_ref[2 + head, at].astype(f32) * (leave[head] * segs.kept(t))).astype(bf16)
+            add = t_dot(key, qkv_ref[4 + head, at])
+            local[4 * head + t] = add
+            state = fall * segs.keep[t] * state + add
+        sent[head] = state.astype(bf16)
+    carry = [sends.put(sent, got.at[k - 1], me.seq_dev(k)) for k in (1, 2)]
+    for copy in first:
+        copy.wait_recv()
+    up_z = [sends.put(u1, up_ref.at[:, me.s], me.z_dev(k)) for k in range(1, nz)]
+    core = [sends.put(u1, up_ref.at[:, me.s], me.core_dev())]
+    up_ref[:, me.s] = u1[...]
+    dn_z = [sends.put(wdn_ref, dn_ref.at[me.s], me.z_dev(k)) for k in range(1, nz)]
+    core.append(sends.put(wdn_ref, dn_ref.at[me.s], me.core_dev()))
+    dn_ref[me.s] = wdn_ref[...]
+
+    def tile(index, base):
+        head, t = index // 2, base + index % 2
+        at = pl.ds(pl.multiple_of(t * TILE, TILE), TILE)
+        wide = pl.ds(pl.multiple_of(t * TILE, TILE), 3 * TILE)
+        raw = dot_t(qkv_ref[head, at], kvx[head, wide])
+        s0, s1, s2, same = tile_scores(raw, head, t, table_ref, near, far, segs)
+        top = jnp.maximum(jnp.maximum(s0, s1), s2).max(axis=1, keepdims=True)
+        e0, e1, e2 = jnp.exp2(s0 - top), jnp.exp2(s1 - top), jnp.exp2(s2 - top)
+        mass = (e0 + e1 + e2).sum(axis=1, keepdims=True)
+        lse_ref[4 * head + t] = top + jnp.log2(mass)
+        mix = jnp.concatenate([e0.astype(bf16), e1.astype(bf16), e2.astype(bf16)], axis=1)
+        att = dot(mix, kvx[2 + head, wide]) / mass
+        weight = jnp.where(same, raw[:, 2 * TILE :] * decay[head], 0.0).astype(bf16)
+        yacc[head, at] = att + dot(weight, qkv_ref[4 + head, at])
+        return base
+
+    lax.fori_loop(0, 4, tile, 2)
+    halo.wait_recv()
+    lax.fori_loop(0, 4, tile, 0)
+    for copy in wo_h:
+        copy.wait_recv()
+    for k in range(3):
+        piece = wo_ref.at[me.heads[k], half]
+        core.append(sends.put(piece, piece, me.core_dev()))
+    for copy in carry:
+        copy.wait_recv()
+    for head in range(2):
+        rate = decay_ref[0, head]
+        fall = power(rate, float(TILE))
+        past = power(rate, 4.0 * TILE) * segs.keep_before
+        state = got[0, head].astype(f32) + past * got[1, head].astype(f32)
+        for t in range(4):
+            at = pl.ds(t * TILE, TILE)
+            state_ref[4 * head + t] = state
+            reach = enter[head] * segs.live(t)
+            y = yacc[head, at] + dot(qkv_ref[head, at], state.astype(bf16)) * reach
+            y_ref[at, head * HD : head * HD + HD] = y.astype(bf16)
+            state = fall * segs.keep[t] * state + local[4 * head + t]
+    for k in range(1, nz):
+        up_z[k - 1].wait_recv()
+        piece = up_ref.at[:, me.z_from(k)]
+        core.append(sends.put(piece, piece, me.core_dev()))
+    for k in range(1, nz):
+        dn_z[k - 1].wait_recv()
+        piece = dn_ref.at[me.z_from(k)]
+        core.append(sends.put(piece, piece, me.core_dev()))
+    for copy in cots + core:
+        copy.wait_recv()
+    sends.finish()
+
+
+def stage_two(table, decay, segments, qkv, w_up, w_down, cotangent, woz):
+    n = lax.axis_size("seq")
+    nz = n // 2
+    rows = w_up.shape[0]
+    tok = cotangent.shape[0]
+    outs = [
+        ((4 * tok, 2 * HD), bf16),
+        ((8, TILE, 1), f32),
+        ((8, HD, HD), f32),
+        ((4, 6 * TILE, HD), bf16),
+        ((4, tok, 1024), bf16),
+        ((4, n, rows, w_up.shape[1] // 4), bf16),
+        ((n,) + w_down.shape, bf16),
+        ((4, n, rows, 1024), bf16),
+    ]
+    scratch = [
+        ((4, rows, w_up.shape[1] // 4), bf16),
+        ((2, TILE, TILE), f32),
+        ((2, TILE, TILE), f32),
+        ((2, TILE, TILE), f32),
+        ((2, TILE, 1), f32),
+        ((2, TILE, 1), f32),
+        ((6, 1, TILE), f32),
+        ((4, TILE, 1), f32),
+        ((2, 4 * TILE, HD), f32),
+        ((8, HD, HD), f32),
+        ((2, HD, HD), bf16),
+        ((2, 2, HD, HD), bf16),
+    ]
+    copies = 1 + 3 + 3 + 3 + 2 + 2 * (nz - 1) + 2 * nz + 3
+    return call(
+        kernel_two, 1, outs, scratch, copies, "attention_forward",
+        table, decay.reshape(1, 2), segments.reshape(-1, TILE), qkv, w_up, w_down, cotangent, woz,
+        scalars=2,
+    )
+
+
+GELU_C = math.sqrt(2.0 / math.pi)
+GELU_A = 0.044715
+
+
+def part(i, size):
+    return pl.ds(pl.multiple_of(i * size, size), size)
+
+
+class Reduce:
+    def __init__(self, me, sends, own, given, core_in, z_in):
+        self.me, self.sends = me, sends
+        self.own, self.given, self.core_in, self.z_in = own, given, core_in, z_in
+
+    def start(self):
+        self.core = self.sends.put(self.given, self.core_in, self.me.core_dev())
+
+    def along(self):
+        me = self.me
+        self.core.wait_recv()
+        self.core.wait_send()
+        self.sends.all = [c for c in self.sends.all if c is not self.core]
+        self.copies = []
+        for k in range(1, me.nz):
+            to = (me.z + k) % me.nz
+            self.given[to] = (self.own[to] + self.core_in[to].astype(f32)).astype(bf16)
+            self.copies.append(
+                self.sends.put(self.given.at[to], self.z_in.at[k - 1], me.z_dev(k))
+            )
+
+    def total(self):
+        me = self.me
+        total = self.own[me.z] + self.core_in[me.z].astype(f32)
+        for k, copy in enumerate(self.copies):
+            copy.wait_recv()
+            total = total + self.z_in[k].astype(f32)
+        return total
+
+
+def kernel_three(
+    tok_ref, y_ref, wo_ref, up_ref, dn_ref, cot_ref, gains_ref,
+    base_ref, outp_ref, ymix_ref, da_ref, dx1_ref, dyh_ref, gdown_ref, gupo_ref, gupg_ref, gnorm_ref,
+    h2all, act, du, dn2s, dn2in, dyt, tile, gown, ggiven, gcore, gz,
+    send_sems, recv_sems,
+):
+    me = Place()
+    nz = me.nz
+    tok = tok_ref.shape[0]
+    peers = [me.head_dev(k) for k in range(3)]
+    greet(peers + [me.z_dev(k) for k in range(1, nz)] + [me.core_dev()])
+    sends = Sends(send_sems, recv_sems)
+    ys = []
+    for k in range(3):
+        src = y_ref.at[part(me.heads[k], tok)]
+        ys.append(sends.put(src, ymix_ref.at[:, part(me.h, 2 * HD)], peers[k]))
+    ymix_ref[:, part(me.h, 2 * HD)] = y_ref[part(me.h, tok)]
+    for copy in ys:
+        copy.wait_recv()
+    gain = gains_ref[1:2]
+    x1 = dx1_ref
+
+    def out_tile(j, _):
+        cols = part(j, 256)
+        x1[:, cols] = tok_ref[:, cols].astype(f32) + dot(ymix_ref[...], wo_ref[:, cols])
+        return 0
+
+    lax.fori_loop(0, 4, out_tile, 0)
+    scale = rms(x1[...])
+    h2all[part(me.h, tok)] = (x1[...] * scale * gain).astype(bf16)
+    h2s = []
+    for k in range(3):
+        own = h2all.at[part(me.h, tok)]
+        h2s.append(sends.put(own, own, peers[k]))
+    base_ref[...] = x1[...]
+    dn2_copies = []
+    for k in range(-1, 3):
+        b = me.h if k < 0 else me.heads[k]
+        if k >= 0:
+            h2s[k].wait_recv()
+        rows = part(b, tok)
+
+        def hidden(j, _):
+            cols = part(j, 256)
+            u = dot(h2all[rows], up_ref[:, cols])
+            dg = dot_t(cot_ref[rows], dn_ref[cols])
+            uu = u * u
+            t = jnp.tanh(GELU_C * u * (1.0 + GELU_A * uu))
+            act[rows, cols] = (0.5 * u * (1.0 + t)).astype(bf16)
+            slope = 0.5 * (1.0 + t) + (0.5 * GELU_C) * u * (1.0 - t * t) * (1.0 + 3.0 * GELU_A * uu)
+            du[rows, cols] = (slope * dg).astype(bf16)
+            return 0
+
+        lax.fori_loop(0, 4, hidden, 0)
+
+        def back(j, _):
+            cols = part(j, 256)
+            dn2s[k + 1, :, cols] = dot_t(du[rows], up_ref[cols]).astype(bf16)
+            return 0
+
+        lax.fori_loop(0, 4, back, 0)
+        if k >= 0:
+            dn2_copies.append(sends.put(dn2s.at[k + 1], dn2in.at[k], peers[k]))
+
+        def ahead(j, _):
+            cols = part(j, 256)
+            out = dot(act[rows], dn_ref[:, cols])
+            if k < 0:
+                base_ref[:, cols] = base_ref[:, cols] + out
+            else:
+                outp_ref[k, :, cols] = out.astype(bf16)
+            return 0
+
+        lax.fori_loop(0, 4, ahead, 0)
+
+    half = 128
+
+    def down_tile(j, _):
+        tile[...] = t_dot(act[:, part(j, 256)], cot_ref[...])
+        gown[j] = tile[part(me.core, half)]
+        ggiven[j] = tile[part(1 - me.core, half)].astype(bf16)
+        return 0
+
+    lax.fori_loop(0, 4, down_tile, 0)
+    down = Reduce(me, sends, gown, ggiven, gcore, gz)
+    down.start()
+
+    def up_tile(j, _):
+        tile[...] = t_dot(h2all[:, part(j, 256)], du[...])
+        for z in range(nz):
+            gupo_ref[z, part(j, 32)] = tile[part(2 * z + me.core, 32)]
+            gupg_ref[z, part(j, 32)] = tile[part(2 * z + 1 - me.core, 32)].astype(bf16)
+        return 0
+
+    lax.fori_loop(0, 4, up_tile, 0)
+    down.along()
+    for copy in dn2_copies:
+        copy.wait_recv()
+    dn2 = dn2s[0].astype(f32) + dn2in[0].astype(f32) + dn2in[1].astype(f32) + dn2in[2].astype(f32)
+    n2 = x1[...] * scale
+    gnorm_ref[...] = jnp.broadcast_to(jnp.sum(dn2 * n2, axis=0, keepdims=True), gnorm_ref.shape)
+    wide = dn2 * gain
+    dx1 = cot_ref[part(me.h, tok)].astype(f32) + scale * (
+        wide - n2 * jnp.mean(wide * n2, axis=-1, keepdims=True)
+    )
+    dx1_ref[...] = dx1
+    da_ref[...] = dx1.astype(bf16)
+
+    def back_tile(j, _):
+        out = dot_t(da_ref[...], wo_ref[part(j, 256)]).astype(bf16)
+        dyt[2 * j] = out[:, :HD]
+        dyt[2 * j + 1] = out[:, HD:]
+        return 0
+
+    lax.fori_loop(0, 4, back_tile, 0)
+    dys = []
+    for k in range(3):
+        src = dyt.at[pl.ds(2 * me.heads[k], 2)]
+        dys.append(sends.put(src, dyh_ref.at[:, part(me.h, tok)], peers[k]))
+    dyh_ref[:, part(me.h, tok)] = dyt[pl.ds(2 * me.h, 2)]
+    gdown_ref[...] = down.total()
+    for copy in dys:
+        copy.wait_recv()
+    sends.finish()
+
+
+def stage_three(tokens, y, wo, up, dn, cots, gains):
+    nz = lax.axis_size("seq") // 2
+    tok = tokens.shape[0]
+    outs = [
+        ((tok, 1024), f32),
+        ((3, tok, 1024), bf16),
+        ((tok, 1024), bf16),
+        ((tok, 1024), bf16),
+        ((tok, 1024), f32),
+        ((2, 4 * tok, HD), bf16),
+        ((128, 1024), f32),
+        ((nz, 128, 1024), f32),
+        ((nz, 128, 1024), bf16),
+        ((8, 1024), f32),
+    ]
+    scratch = [
+        ((4 * tok, 1024), bf16),
+        ((4 * tok, 1024), bf16),
+        ((4 * tok, 1024), bf16),
+        ((4, tok, 1024), bf16),
+        ((3, tok, 1024), bf16),
+        ((8, tok, HD), bf16),
+        ((256, 1024), f32),
+        ((nz, 128, 1024), f32),
+        ((nz, 128, 1024), bf16),
+        ((nz, 128, 1024), bf16),
+        ((nz - 1, 128, 1024), bf16),
+    ]
+    copies = 12 + 1 + nz - 1
+    square = lambda a: a.reshape(1024, 1024)
+    return call(
+        kernel_three, 2, outs, scratch, copies, "feed_forward",
+        tokens, y, square(wo), square(up), square(dn), cots.reshape(4 * tok, 1024), gains,
+    )
+
+
+def kernel_four(
+    table_ref, decay_ref, seg_ref, q_ref, kvx, dy_ref, lse_ref, state_ref,
+    base_ref, outp_ref, ymix_ref, da_ref, gupo_ref, gupg_ref,
+    dqkv_ref, out_ref, gout_ref, gup_ref, small_ref,
+    near, far, decay, enter, leave, rows, cols, dqs, dks, dvs, local, sent, got, halo_out, halo_in,
+    diag, below, rest, sums, outin, ocore, oown, ogiven, ohead, ohin, ozin, ucore, uz, usum, tile,
+    send_sems, recv_sems,
+):
+    me = Place()
+    nz = me.nz
+    tok = base_ref.shape[0]
+    peers = [me.head_dev(k) for k in range(3)]
+    greet(
+        peers
+        + [me.z_dev(k) for k in range(1, nz)]
+        + [me.core_dev(), me.seq_dev(1), me.seq_dev(2)]
+    )
+    sends = Sends(send_sems, recv_sems)
+    up = Reduce(me, sends, gupo_ref, gupg_ref, ucore, uz)
+    up.start()
+    outs = [sends.put(outp_ref.at[k], outin.at[k], peers[k]) for k in range(3)]
+    segs = Segs(me, seg_ref, rows, cols)
+    fill_tables(table_ref, decay_ref, near, far, decay, enter, leave)
+    sums[...] = jnp.zeros_like(sums)
+    dks[...] = jnp.zeros_like(dks)
+    dvs[...] = jnp.zeros_like(dvs)
+    diag[...] = jnp.zeros_like(diag)
+    below[...] = jnp.zeros_like(below)
+    rest[...] = jnp.zeros_like(rest)
+    falls = [power(decay_ref[0, head], float(TILE)) for head in range(2)]
+    for head in range(2):
+        grad = jnp.zeros((HD, HD), f32)
+        for t in range(3, -1, -1):
+            at = pl.ds(t * TILE, TILE)
+            query = (q_ref[head, at].astype(f32) * (enter[head] * segs.live(t))).astype(bf16)
+            add = t_dot(query, dy_ref[head, at])
+            local[4 * head + t] = add
+            grad = falls[head] * segs.keep[t] * grad + add
+        sent[head] = grad.astype(bf16)
+    carry = [sends.put(sent, got.at[k - 1], me.seq_dev(-k)) for k in (1, 2)]
+
+    def out_tile(j, _):
+        tile[...] = t_dot(ymix_ref[:, part(j, 256)], da_ref[...])
+        for z in range(nz):
+            oown[j, part(z, 32)] = tile[part(2 * z + me.core, 32)]
+            ogiven[j, part(z, 32)] = tile[part(2 * z + 1 - me.core, 32)].astype(bf16)
+        return 0
+
+    lax.fori_loop(0, 4, out_tile, 0)
+    o_core = sends.put(ogiven, ocore, me.core_dev())
+    up.along()
+    gap = (grid_of(0) - grid_of(1)).astype(f32)
+
+    def tiles(index, base):
+        head, t = index // 2, base + index % 2
+        at, wide = part(t, TILE), pl.ds(pl.multiple_of(t * TILE, TILE), 3 * TILE)
+        query, dy = q_ref[head, at], dy_ref[head, at]
+        keys, values = kvx[head, wide], kvx[2 + head, wide]
+        raw = dot_t(query, keys)
+        s0, s1, s2, same = tile_scores(raw, head, t, table_ref, near, far, segs)
+        lse = lse_ref[4 * head + t]
+        p0, p1, p2 = jnp.exp2(s0 - lse), jnp.exp2(s1 - lse), jnp.exp2(s2 - lse)
+        dp = dot_t(dy, values)
+        dp0, dp1, dp2 = dp[:, :TILE], dp[:, TILE : 2 * TILE], dp[:, 2 * TILE :]
+        mean = (p0 * dp0 + p1 * dp1 + p2 * dp2).sum(axis=1, keepdims=True)
+        d0, d1, d2 = p0 * (dp0 - mean), p1 * (dp1 - mean), p2 * (dp2 - mean)
+        diag[head] += d2[:HD, :HD] + d2[HD:, HD:]
+        below[head] += d2[HD:, :HD] + d1[:HD, HD:]
+        rest[head] += (
+            (d0[:, :HD] + d0[:, HD:]).sum(axis=0, keepdims=True)
+            + d1[:, :HD].sum(axis=0, keepdims=True)
+            + d1[HD:, HD:].sum(axis=0, keepdims=True)
+        )
+        weight = jnp.where(same, decay[head], 0.0)
+        mixed = weight * raw[:, 2 * TILE :]
+        turn = weight * dp2
+        slope = mixed * dp2 * gap
+        sums[head] -= (slope[:, :HD] + slope[:, HD:]).sum(axis=0, keepdims=True)
+        scale = 1.0 / math.sqrt(HD)
+        x = jnp.concatenate(
+            [(d0 * scale).astype(bf16), (d1 * scale).astype(bf16), (d2 * scale + turn).astype(bf16)],
+            axis=1,
+        )
+        p = jnp.concatenate([p0.astype(bf16), p1.astype(bf16), (p2 + mixed).astype(bf16)], axis=1)
+        dqs[head, at] = dot(x, keys)
+        dks[head, wide] += t_dot(x, query)
+        dvs[head, wide] += t_dot(p, dy)
+        return base
+
+    lax.fori_loop(0, 4, tiles, 0)
+    for head in range(2):
+        halo_out[head] = dks[head, : 2 * TILE].astype(bf16)
+        halo_out[2 + head] = dvs[head, : 2 * TILE].astype(bf16)
+    halo = sends.put(halo_out, halo_in, me.seq_dev(-1))
+    o_core.wait_recv()
+    o_core.wait_send()
+    sends.all = [c for c in sends.all if c is not o_core]
+    o_head = []
+    for k in range(3):
+        to = me.heads[k]
+        ohead[k] = (oown[to] + ocore[to].astype(f32)).astype(bf16)
+        o_head.append(sends.put(ohead.at[k], ohin.at[k], peers[k]))
+    lax.fori_loop(0, 4, tiles, 2)
+    for copy in outs:
+        copy.wait_recv()
+    out_ref[...] = (
+        base_ref[...] + outin[0].astype(f32) + outin[1].astype(f32) + outin[2].astype(f32)
+    ).astype(bf16)
+    for copy in o_head:
+        copy.wait_recv()
+    o_sum = oown[me.h] + ocore[me.h].astype(f32)
+    for k in range(3):
+        o_sum = o_sum + ohin[k].astype(f32)
+    tile[0:128] = o_sum
+    ogiven[0] = o_sum.astype(bf16)
+    o_z = []
+    for k in range(1, nz):
+        src = ogiven.at[0, part((me.z + k) % nz, 32)]
+        o_z.append(sends.put(src, ozin.at[k - 1], me.z_dev(k)))
+    for copy in carry:
+        copy.wait_recv()
+    place = grid_of(0, (TILE, 1)).astype(f32)
+    halo.wait_recv()
+    for head in range(2):
+        rate = decay_ref[0, head]
+        past = power(rate, 4.0 * TILE) * segs.keep_after
+        grad = got[0, head].astype(f32) + past * got[1, head].astype(f32)
+        fall = falls[head]
+        total = jnp.zeros((1, HD), f32)
+        for t in range(3, -1, -1):
+            at = pl.ds(t * TILE, TILE)
+            ext = pl.ds((t + 2) * TILE, TILE)
+            low = grad.astype(bf16)
+            state = state_ref[4 * head + t]
+            give = leave[head] * segs.kept(t)
+            take = enter[head] * segs.live(t)
+            query, key, value = q_ref[head, at], kvx[head, ext], kvx[2 + head, ext]
+            dq = dot_t(dy_ref[head, at], state.astype(bf16)) * take
+            dv = dot(key, low) * give
+            dk = dot_t(value, low) * give + dks[head, ext]
+            slope = dq * query.astype(f32) * (place + 1.0)
+            slope = slope + dv * value.astype(f32) * (TILE - 1.0 - place)
+            crossing = fall * segs.keep[t]
+            total = total - slope.sum(axis=0, keepdims=True)
+            total = total - TILE * crossing * (grad * state).sum(axis=0, keepdims=True)
+            dv = dv + dvs[head, ext]
+            if t >= 2:
+                back = pl.ds((t - 2) * TILE, TILE)
+                dk = dk + halo_in[head, back].astype(f32)
+                dv = dv + halo_in[2 + head, back].astype(f32)
+            dqkv_ref[head, at] = (dqs[head, at] + dq).astype(bf16)
+            dqkv_ref[2 + head, at] = dk.astype(bf16)
+            dqkv_ref[4 + head, at] = dv.astype(bf16)
+            grad = local[4 * head + t] + crossing * grad
+        sums[head] += total
+    gap_near = grid_of(0, (HD, HD)) - grid_of(1, (HD, HD))
+    gap_far = gap_near + HD
+    table = []
+    for head in range(2):
+        last = rest[head]
+        for b in range(BUCKETS):
+            up_to = STARTS[b + 1] if b + 1 < BUCKETS else 2 * WIN
+            inside = lambda g: (g >= STARTS[b]) & (g < up_to)
+            total = jnp.where(inside(gap_near), diag[head], 0.0)
+            total = total + jnp.where(inside(gap_far), below[head], 0.0)
+            total = total.sum(axis=0, keepdims=True)
+            table.append(total + last if b == BUCKETS - 1 else total)
+    table += [sums[0], sums[1], jnp.zeros((HD - 2 * BUCKETS - 2, HD), f32)]
+    small_ref[...] = lax.dot_general(
+        jnp.ones((8, HD), f32), jnp.concatenate(table, axis=0), (((1,), (1,)), ((), ())),
+        precision=lax.Precision.HIGHEST, preferred_element_type=f32,
+    )
+    usum[...] = up.total()
+    width = usum.shape[1]
+    ups = []
+    for k in range(3):
+        src = usum.at[part(me.heads[k], 32)]
+        ups.append(sends.put(src, gup_ref.at[:, part(me.h, width)], peers[k]))
+    gup_ref[:, part(me.h, width)] = usum[part(me.h, 32)]
+    total = tile[part(me.z, 32)]
+    for k in range(nz - 1):
+        o_z[k].wait_recv()
+        total = total + ozin[k].astype(f32)
+    gout_ref[...] = total
+    for copy in ups:
+        copy.wait_recv()
+    sends.finish()
+
+
+def stage_four(table, decay, segments, qkv, kvx, dy, lse, states, base, outp, ymix, da, gupo, gupg):
+    nz = lax.axis_size("seq") // 2
+    tok = base.shape[0]
+    outs = [
+        ((6, 4 * tok, HD), bf16),
+        ((tok, 1024), bf16),
+        ((32, 1024), f32),
+        ((32, 4096), f32),
+        ((8, HD), f32),
+    ]
+    scratch = [
+        ((2, TILE, TILE), f32),
+        ((2, TILE, TILE), f32),
+        ((2, TILE, TILE), f32),
+        ((2, TILE, 1), f32),
+        ((2, TILE, 1), f32),
+        ((6, 1, TILE), f32),
+        ((4, TILE, 1), f32),
+        ((2, 4 * TILE, HD), f32),
+        ((2, 6 * TILE, HD), f32),
+        ((2, 6 * TILE, HD), f32),
+        ((8, HD, HD), f32),
+        ((2, HD, HD), bf16),
+        ((2, 2, HD, HD), bf16),
+        ((4, 2 * TILE, HD), bf16),
+        ((4, 2 * TILE, HD), bf16),
+        ((2, HD, HD), f32),
+        ((2, HD, HD), f32),
+        ((2, 1, HD), f32),
+        ((2, 1, HD), f32),
+        ((3, tok, 1024), bf16),
+        ((4, 128, 1024), bf16),
+        ((4, 128, 1024), f32),
+        ((4, 128, 1024), bf16),
+        ((3, 128, 1024), bf16),
+        ((3, 128, 1024), bf16),
+        ((nz - 1, 32, 1024), bf16),
+        ((nz, 128, 1024), bf16),
+        ((nz - 1, 128, 1024), bf16),
+        ((128, 1024), f32),
+        ((256, 1024), f32),
+    ]
+    copies = 1 + 3 + 2 + 1 + (nz - 1) + 1 + 3 + (nz - 1) + 3
+    return call(
+        kernel_four, 3, outs, scratch, copies, "attention_backward",
+        table, decay.reshape(1, 2), segments.reshape(-1, TILE), qkv[0:2], kvx, dy, lse, states,
+        base, outp, ymix, da, gupo, gupg, scalars=2,
+    )
+
+
+def kernel_five(
+    dqkv_ref, hall_ref, w_ref, gains_ref, tok_ref, dx1_ref, gnorm_ref, small_ref,
+    in_ref, gq_ref, gk_ref, gv_ref, norms_ref, sums_ref,
+    dall, dsend, din, own_dn, gown, ggiven, gcore, gz, gsum, gin, tile, nsend, ncore, nz_in, nhead,
+    send_sems, recv_sems,
+):
+    me = Place()
+    nz = me.nz
+    tok = tok_ref.shape[0]
+    peers = [me.head_dev(k) for k in range(3)]
+    greet(peers + [me.z_dev(k) for k in range(1, nz)] + [me.core_dev()])
+    sends = Sends(send_sems, recv_sems)
+    for j in range(6):
+        dall[:, j * HD : j * HD + HD] = dqkv_ref[j]
+    wide = 6 * HD
+    backs = []
+    for k in range(3):
+        rows = part(me.heads[k], tok)
+
+        def back(j, _):
+            dsend[k, :, part(j, 256)] = dot_t(dall[rows], w_ref[part(j, 256), 0:wide]).astype(bf16)
+            return 0
+
+        lax.fori_loop(0, 4, back, 0)
+        backs.append(sends.put(dsend.at[k], din.at[k], peers[k]))
+
+    def grad_tile(j, _):
+        tile[...] = t_dot(hall_ref[:, part(j, 256)], dall[...])
+        for z in range(nz):
+            gown[z, part(j, 32)] = tile[part(2 * z + me.core, 32)]
+            ggiven[z, part(j, 32)] = tile[part(2 * z + 1 - me.core, 32)].astype(bf16)
+        return 0
+
+    lax.fori_loop(0, 4, grad_tile, 0)
+    grads = Reduce(me, sends, gown, ggiven, gcore, gz)
+    grads.start()
+
+    def own(j, _):
+        own_dn[:, part(j, 256)] = dot_t(dall[part(me.h, tok)], w_ref[part(j, 256), 0:wide])
+        return 0
+
+    lax.fori_loop(0, 4, own, 0)
+    grads.along()
+    gain = gains_ref[0:1]
+    x = tok_ref[...].astype(f32)
+    scale = rms(x)
+    n1 = x * scale
+    for copy in backs:
+        copy.wait_recv()
+    dn1 = own_dn[...] + din[0].astype(f32) + din[1].astype(f32) + din[2].astype(f32)
+    nsend[...] = jnp.zeros_like(nsend)
+    nsend[0:1] = jnp.sum(dn1 * n1, axis=0, keepdims=True)
+    nsend[1:2] = gnorm_ref[0:1]
+    nsend[2:3, 0:HD] = small_ref[0:1]
+    n_core = sends.put(nsend, ncore, me.core_dev())
+    dn1 = dn1 * gain
+    dx = dx1_ref[...] + scale * (dn1 - n1 * jnp.mean(dn1 * n1, axis=-1, keepdims=True))
+    in_ref[...] = dx.astype(bf16)
+    n_core.wait_recv()
+    n_core.wait_send()
+    sends.all = [c for c in sends.all if c is not n_core]
+    nsend[...] = nsend[...] + ncore[...]
+    n_z = [sends.put(nsend, nz_in.at[k - 1], me.z_dev(k)) for k in range(1, nz)]
+    gsum[...] = grads.total()
+    g_head = []
+    for k in range(3):
+        src = gsum.at[part(me.heads[k], 32)]
+        g_head.append(sends.put(src, gin.at[me.h], peers[k]))
+    gin[me.h] = gsum[part(me.h, 32)]
+    total = nsend[...]
+    for k in range(nz - 1):
+        n_z[k].wait_recv()
+        total = total + nz_in[k]
+    ncore[...] = total
+    n_head = [sends.put(ncore, nhead.at[k], peers[k]) for k in range(3)]
+    sums_ref[...] = total[:, 0:HD]
+    for copy in g_head:
+        copy.wait_recv()
+    for h in range(4):
+        for out, at in ((gq_ref, 0), (gk_ref, 1), (gv_ref, 2)):
+            out[:, h * 256 : h * 256 + 256] = gin[h, :, at * 256 : at * 256 + 256]
+    for copy in n_head:
+        copy.wait_recv()
+    norms_ref[...] = ncore[...] + nhead[0] + nhead[1] + nhead[2]
+    sends.finish()
+
+
+def stage_five(dqkv, hall, wb, gains, tokens, dx1, gnorm, small):
+    nz = lax.axis_size("seq") // 2
+    tok = tokens.shape[0]
+    wide = 6 * HD
+    outs = [
+        ((tok, 1024), bf16),
+        ((32, 1024), f32),
+        ((32, 1024), f32),
+        ((32, 1024), f32),
+        ((8, 1024), f32),
+        ((8, HD), f32),
+    ]
+    scratch = [
+        ((4 * tok, wide), bf16),
+        ((3, tok, 1024), bf16),
+        ((3, tok, 1024), bf16),
+        ((tok, 1024), f32),
+        ((nz, 128, wide), f32),
+        ((nz, 128, wide), bf16),
+        ((nz, 128, wide), bf16),
+        ((nz - 1, 128, wide), bf16),
+        ((128, wide), f32),
+        ((4, 32, wide), f32),
+        ((256, wide), f32),
+        ((8, 1024), f32),
+        ((8, 1024), f32),
+        ((nz - 1, 8, 1024), f32),
+        ((3, 8, 1024), f32),
+    ]
+    copies = 3 + 1 + (nz - 1) + 1 + (nz - 1) + 3 + 3
+    return call(
+        kernel_five, 4, outs, scratch, copies, "input_gradient",
+        dqkv, hall, wb.reshape(1024, 896), gains, tokens, dx1, gnorm, small,
+    )
+
+
+def shards(
+    tokens, cotangent, segments, w_query, w_key, w_value, w_out, w_up, w_down,
+    norm_one, norm_two, rel_table, decay_rate,
+):
+    hall, qkv, wb, woz, gains = stage_one(
+        tokens, w_query, w_key, w_value, w_out, norm_one, norm_two
+    )
+    y, lse, states, kvx, cots, up, dn, wo = stage_two(
+        rel_table, decay_rate, segments, qkv, w_up, w_down, cotangent, woz
+    )
+    base, outp, ymix, da, dx1, dyh, grad_down, gupo, gupg, gnorm = stage_three(
+        tokens, y, wo, up, dn, cots, gains
+    )
+    dqkv, output, grad_out, grad_up, small = stage_four(
+        rel_table, decay_rate, segments, qkv, kvx, dyh, lse, states, base, outp, ymix, da, gupo, gupg
+    )
+    input_grad, grad_query, grad_key, grad_value, norms, sums = stage_five(
+        dqkv, hall, wb, gains, tokens, dx1, gnorm, small
+    )
+    rows = w_query.shape[0]
+    at = lax.axis_index("head") * 256 + lax.axis_index("seq") * rows
+    mine = lax.dynamic_slice(norms, (0, at), (2, rows))
+    sums = sums[2]
+    return (
+        output, input_grad, grad_query, grad_key, grad_value, grad_out, grad_up, grad_down,
+        mine[0], mine[1], sums[: 2 * BUCKETS].reshape(2, BUCKETS), sums[2 * BUCKETS : 2 * BUCKETS + 2],
+    )
+
+
 highest = lax.Precision.HIGHEST
 
 
@@ -138,7 +1143,7 @@
     return (readouts.reshape(block_len, head_count, head_width), final_state)
 
 
-def shards(
+def general_shards(
     tokens,
     cotangent,
     segments,
@@ -403,8 +1408,10 @@
 
 
 def solution(mesh):
+    devices = mesh.shape["head"] * mesh.shape["seq"]
+    tiled = mesh.shape["head"] == 4 and 1024 // devices == 32
     return jax.shard_map(
-        shards,
+        shards if tiled else general_shards,
         mesh=mesh,
         in_specs=(
             P(("seq", "head"), None),

time: 1560 us -> 300 us (0.19)
  waiting for transfers between devices: 847 us -> 0 us
  Pallas kernels: 0 us -> 280 us
  local copies, waits for them, and re-layouts: 227 us -> 17.4 us
  matrix products: 183 us -> 0 us
  blocking collectives: 172 us -> 0 us
  other arithmetic: 73.9 us -> 1.45 us
  between operations: 17.6 us -> 0.77 us
  starting transfers between devices: 16.7 us -> 0 us
    reduce_scatter x6 -> x0, waiting for transfers between devices: 697 us -> none  [the longest x1 187 us: shards(): lax.psum_scatter(grad_down_w, ('head', 'seq'), scatter_dimension=0, tiled...]
    pallas_call x0 -> x5, Pallas kernels: none -> 280 us  [call(): pl.pallas_call(kernel, out_shape=[jax.ShapeDtypeStruct(shape, kind) for s...]
    dot_general x61 -> x0, matrix products: 183 us -> none  [the longest x6 33.1 us: transposed_times(): lax.dot_general(left, right, (((0,), (0,)), ((), ())), preferred_element_...]
    all_gather x6 -> x0, waiting for transfers between devices: 133 us -> none  [the longest x1 56 us: shards(): lax.all_gather(w_query, ('head', 'seq'), axis=0, tiled=True)]
    unnamed x3 -> x0, blocking collectives: 95.1 us -> none
    dynamic_update_slice x18 -> x0, local copies, waits for them, and re-layouts: 38.3 us -> none  [the longest x12 36.3 us: shards(): attended_blocks, log_mass = lax.map(forward_block, numbers)]
    all_gather x2 -> x0, blocking collectives: 32.9 us -> none  [prefix(): lax.all_gather(a.astype(kind), axis)]
    all_to_all x1 -> x0, blocking collectives: 29.5 us -> none  [shards(): lax.all_to_all(triple_grad, 'head', split_axis=1, concat_axis=2, tiled=True)]
  transfers between devices with their start and end apart: 17 -> 0, of which waited for: 11 -> 0; matrix products, arithmetic and copies ran while one was open for 29% -> 0% of each run, Pallas kernels for 0% -> 0%
where the time goes in v1:
time: 300 us
  Pallas kernels  280 us (93%)
  local copies, waits for them, and re-layouts  17.4 us (6%)
    pallas_call x5, Pallas kernels, call(): pl.pallas_call(kernel, out_shape=[jax.ShapeDtypeStruct(shape, kind) for s...  280 us
    unnamed x22, local copies, waits for them, and re-layouts  6.9 us

profile of v1, /device:TPU:0, one launch (start us, length us, event | category | flops | bytes accessed | tf_op | source)
XLA Modules:
  0.0 299.5 jit_solution(13736607818356906259)
XLA Ops:
  0.7 0.7 tile.8
  1.5 0.7 tile.20
  2.2 0.7 fusion
  3.0 1.4 reshape.66.seg_ref
  4.4 0.8 copy.35
  5.2 0.9 copy_bitcast_fusion
  6.1 0.7 maximum_bitcast_fusion.p1_ref
  6.8 39.7 %gather_qkv.1 = (bf16[1024,1024]{1,0:T(8,128)(2,1)}, bf16[6,1024,128]{2,1,0:T(8,128)(2,1)}, bf16[4,8,32,896]{3,2,1,0:T(8,128)(2,1)}, bf16[8,32,1024]{2,1,0:T(8,128)(2,1)}, f32[8,1024]{1,0:T(8,128)}) custom-call(bf16[256,1024]{1,0:T(8,128)(2,1)} %tok_ref.5, bf16[4,32,896]{2,1,0:T(8,128)(2,1)} %maximum_bitcast_fusion.p1_ref, bf16[32,1024]{1,0:T(8,128)(2,1)} %wo_ref.1), custom_call_target="tpu_custom_call" | custom-call | tf_op jit(solution)/shard_map/gather_qkv/pallas_call | solution.py:166
  46.6 1.9 slice.22.q_ref
  48.4 61.2 %attention_forward.1 = (bf16[1024,256]{1,0:T(8,128)(2,1)}, f32[8,256,1]{2,1,0:T(8,128)}, f32[8,128,128]{2,1,0:T(8,128)}, bf16[4,1536,128]{2,1,0:T(8,128)(2,1)}, ...) custom-call(f32[2,32]{1,0:T(2,128)} %table_ref.3, ...), custom_call_target="tpu_custom_call" | custom-call | tf_op jit(solution)/shard_map/attention_forward/pallas_call | solution.py:166
  109.6 79.8 %feed_forward.1 = (f32[256,1024]{1,0:T(8,128)}, bf16[3,256,1024]{2,1,0:T(8,128)(2,1)}, bf16[256,1024]{1,0:T(8,128)(2,1)}, bf16[256,1024]{1,0:T(8,128)(2,1)}, f32...) custom-call(bf16[256,1024]{1,0:T(8,128)(2,1)} %tok_ref.5, ...), custom_call_target="tpu_custom_call" | custom-call | tf_op jit(solution)/shard_map/feed_forward/pallas_call | solution.py:166
  189.4 55.8 %attention_backward.1 = (bf16[6,1024,128]{2,1,0:T(8,128)(2,1)}, bf16[256,1024]{1,0:T(8,128)(2,1)}, f32[32,1024]{1,0:T(8,128)}, f32[32,4096]{1,0:T(8,128)}, f32[8,128]{1,0:T(8,128)}) custom-call(f32[2,32]{1,0:T(2,128)} %table_ref.3, f32[1,2]{1,0:T(1,128)} %bitcast.38, s32[32,256]{1,0:T(8,128)} %reshape.66.seg_ref, bf16[2,1024,128]{2,1,0:T(8,128)(2,1)} %slice.22.q_ref, ...), custom_call_target="tpu_custom_call" | custom-call | tf_op jit(solution)/shard_map/attention_backward/pallas_call | solution.py:166
  245.2 43.4 %input_gradient.1 = (bf16[256,1024]{1,0:T(8,128)(2,1)}, f32[32,1024]{1,0:T(8,128)}, f32[32,1024]{1,0:T(8,128)}, f32[32,1024]{1,0:T(8,128)}, f32[8,1024]{1,0:T(8,128)}, /*index=5*/f32[8,128]{1,0:T(8,128)}) custom-call(bf16[6,1024,128]{2,1,0:T(8,128)(2,1)} %get-tuple-element.65.dqkv_ref, bf16[1024,1024]{1,0:T(8,128)(2,1)} %get-tuple-element.66.hall_ref, ...), custom_call_target="tpu_custom_call" | custom-call | tf_op jit(solution)/shard_map/input_gradient/pallas_call | solution.py:166
  288.7 0.8 constant_dynamic-slice_fusion
  290.0 1.3 slice_bitcast_fusion
  291.3 0.7 slice_reduce_fusion
  292.6 0.8 copy.44
  293.4 1.9 copy.45
  295.3 0.7 copy.46
  296.0 0.7 copy.47
  296.6 0.7 copy.48
  297.3 0.7 copy.49
  297.9 0.8 copy.50
  298.7 0.8 copy.51
  (22 shorter events, 1.5 us)
Async XLA Ops:
  245.2 47.4 %copy-start.2 = (bf16[256,1024]{1,0:T(8,128)(2,1)S(1)}, bf16[256,1024]{1,0:T(8,128)(2,1)}, u32[]{:S(2)}) copy-start(bf16[256,1024]{1,0:T(8,128)(2,1)} %get-tuple-element.98) | copy-start | bytes 1572868
  288.6 6.7 %copy-start.6 = (f32[32,1024]{1,0:T(8,128)S(1)}, f32[32,1024]{1,0:T(8,128)}, u32[]{:S(2)}) copy-start(f32[32,1024]{1,0:T(8,128)} %get-tuple-element.100) | copy-start | bytes 393220
  288.7 7.3 %copy-start.5 = (f32[32,1024]{1,0:T(8,128)S(1)}, f32[32,1024]{1,0:T(8,128)}, u32[]{:S(2)}) copy-start(f32[32,1024]{1,0:T(8,128)} %get-tuple-element.101) | copy-start | bytes 393220
  288.7 8.0 %copy-start.4 = (f32[32,1024]{1,0:T(8,128)S(1)}, f32[32,1024]{1,0:T(8,128)}, u32[]{:S(2)}) copy-start(f32[32,1024]{1,0:T(8,128)} %get-tuple-element.102) | copy-start | bytes 393220
  288.7 8.6 %copy-start.3 = (f32[32,1024]{1,0:T(8,128)S(1)}, f32[32,1024]{1,0:T(8,128)}, u32[]{:S(2)}) copy-start(f32[32,1024]{1,0:T(8,128)} %get-tuple-element.103) | copy-start | bytes 393220
  288.7 9.3 %copy-start.1 = (f32[32,4096]{1,0:T(8,128)S(1)}, f32[32,4096]{1,0:T(8,128)}, u32[]{:S(2)}) copy-start(f32[32,4096]{1,0:T(8,128)} %get-tuple-element.104) | copy-start | bytes 1572868
  292.6 6.1 %copy-start = (f32[128,1024]{1,0:T(8,128)S(1)}, f32[128,1024]{1,0:T(8,128)}, u32[]{:S(2)}) copy-start(f32[128,1024]{1,0:T(8,128)} %get-tuple-element.105) | copy-start | bytes 1572868

commit v2 on v0

--- a/solution.py
+++ b/solution.py
@@ -1,19 +1,884 @@
+import functools
 import math
 
 import jax
 import jax.numpy as jnp
 import numpy as np
 from jax import lax
+from jax.experimental import pallas as pl
+from jax.experimental.pallas import tpu as pltpu
 from jax.sharding import PartitionSpec as P
 
 HD = 128
 BUCKETS = 32
 WIN = 512
-
+TILE = 256
 
 epsilon = 1e-06
 negative = -1e30
 state_scale = 1.0 / 1024.0
+MESH = pl.DeviceIdType.MESH
+f32 = jnp.float32
+bf16 = jnp.bfloat16
+
+
+def dot(a, b):
+    return jnp.dot(a, b, preferred_element_type=f32)
+
+
+def dot_t(a, b):
+    return lax.dot_general(a, b, (((1,), (1,)), ((), ())), preferred_element_type=f32)
+
+
+def t_dot(a, b):
+    return lax.dot_general(a, b, (((0,), (0,)), ((), ())), preferred_element_type=f32)
+
+
+class Place:
+    def __init__(self):
+        self.h = lax.axis_index("head")
+        self.s = lax.axis_index("seq")
+        self.n = lax.axis_size("seq")
+        self.nz = self.n // 2
+        self.z = self.s // 2
+        self.core = self.s % 2
+        x, y = self.h % 2, self.h // 2
+        self.heads = [2 * y + 1 - x, 2 * (1 - y) + x, 2 * (1 - y) + 1 - x]
+
+    def head_dev(self, k):
+        return (self.heads[k], self.s)
+
+    def z_to(self, k):
+        return ((self.z + k) % self.nz) * 2 + self.core
+
+    def z_from(self, k):
+        return ((self.z + self.nz - k) % self.nz) * 2 + self.core
+
+    def z_dev(self, k):
+        return (self.h, self.z_to(k))
+
+    def other(self):
+        return self.z * 2 + 1 - self.core
+
+    def core_dev(self):
+        return (self.h, self.other())
+
+    def seq_dev(self, by):
+        return (self.h, (self.s + self.n + by) % self.n)
+
+
+def greet(devices):
+    barrier = pltpu.get_barrier_semaphore()
+    for device in devices:
+        pl.semaphore_signal(barrier, inc=1, device_id=device, device_id_type=MESH)
+    pl.semaphore_wait(barrier, len(devices))
+
+
+class Sends:
+    def __init__(self, send_sems, recv_sems):
+        self.send_sems, self.recv_sems = send_sems, recv_sems
+        self.at, self.all = 0, []
+
+    def put(self, src, dst, device, start=True):
+        copy = pltpu.make_async_remote_copy(
+            src_ref=src,
+            dst_ref=dst,
+            send_sem=self.send_sems.at[self.at],
+            recv_sem=self.recv_sems.at[self.at],
+            device_id=device,
+            device_id_type=MESH,
+        )
+        self.at += 1
+        self.all.append(copy)
+        if start:
+            copy.start()
+        return copy
+
+    def sent(self, copy):
+        copy.wait_send()
+        self.all = [c for c in self.all if c is not copy]
+
+    def finish(self):
+        for copy in self.all:
+            copy.wait_send()
+
+
+def rms(x):
+    return lax.rsqrt(jnp.mean(x * x, axis=-1, keepdims=True) + epsilon)
+
+
+LOG2E = math.log2(math.e)
+KEY_SCALE = LOG2E / math.sqrt(HD)
+
+
+def bucket_starts():
+    distance = np.arange(WIN)
+    scaled = np.floor(np.log(np.maximum(distance, 1) / 16.0) / np.log(8.0) * 16.0)
+    larger = np.minimum(16 + np.maximum(scaled, 0), BUCKETS - 1)
+    bucket = np.where(distance < 16, distance, larger).astype(np.int32)
+    return [int(np.argmax(bucket == b)) for b in range(BUCKETS)]
+
+
+STARTS = bucket_starts()
+
+
+def grid_of(axis, shape=(TILE, TILE)):
+    return lax.broadcasted_iota(jnp.int32, shape, axis)
+
+
+def column(row):
+    eye = grid_of(0) == grid_of(1)
+    return jnp.sum(jnp.where(eye, row, 0.0), axis=1, keepdims=True)
+
+
+class Segs:
+    def __init__(self, me, seg_ref, rows, cols):
+        total = 4 * me.n
+        self.rows, self.cols = rows, cols
+
+        def row_at(offset):
+            at = 2 * ((4 * me.s + total + offset) % total)
+            pair = [seg_ref[pl.ds(at + i, 1)].astype(f32) for i in range(2)]
+            return jnp.concatenate(pair, axis=1)
+
+        for j in range(6):
+            row = row_at(j - 2)
+            rows[j] = row
+            if j >= 2:
+                cols[j - 2] = column(row)
+        last = lambda offset: row_at(offset)[:, TILE - 1 : TILE]
+        self.last = [last(j - 2) for j in range(6)]
+        same = lambda a, b: (a == b).astype(f32)
+        self.keep = [same(self.last[t + 2], self.last[t + 1]) for t in range(4)]
+        self.keep_before = same(last(-1), last(-5))
+        self.keep_after = same(last(7), last(3))
+
+    def live(self, t):
+        return (self.cols[t] == self.last[t + 1]).astype(f32)
+
+    def kept(self, t):
+        return (self.cols[t] == self.last[t + 2]).astype(f32)
+
+
+def fill_tables(table_ref, decay_ref, near, far, decay, enter, leave):
+    gap = grid_of(0) - grid_of(1)
+    place = grid_of(0, (TILE, 1)).astype(f32)
+    for head in range(2):
+        rate = decay_ref[0, head]
+        for out, shift in ((near, 0), (far, TILE)):
+            bias = jnp.full((TILE, TILE), table_ref[head, 0] * LOG2E, f32)
+            for b in range(1, BUCKETS):
+                bias = jnp.where(gap + shift >= STARTS[b], table_ref[head, b] * LOG2E, bias)
+            out[head] = jnp.where(gap + shift >= 0, bias, negative)
+        fall = jnp.exp(-rate * jnp.maximum(gap, 0).astype(f32)) * state_scale
+        decay[head] = jnp.where(gap >= 0, fall, 0.0)
+        enter[head] = jnp.exp(-rate * (place + 1.0)) * state_scale
+        leave[head] = jnp.exp(-rate * (TILE - 1.0 - place))
+
+
+def power(rate, steps):
+    return jnp.exp(jnp.full((1, HD), -rate * steps, f32))
+
+
+def tile_scores(raw, head, t, table_ref, near, far, segs):
+    col = segs.cols[t]
+    same = [col == segs.rows[t + j] for j in range(3)]
+    reach = grid_of(0) < grid_of(1)
+    rest = table_ref[head, BUCKETS - 1] * LOG2E
+    s0 = jnp.where(same[0] & reach, raw[:, :TILE] * KEY_SCALE + rest, negative)
+    s1 = jnp.where(same[1], raw[:, TILE : 2 * TILE] * KEY_SCALE + far[head], negative)
+    s2 = jnp.where(same[2], raw[:, 2 * TILE :] * KEY_SCALE + near[head], negative)
+    return s0, s1, s2, same[2]
+
+
+GELU_C = math.sqrt(2.0 / math.pi)
+GELU_A = 0.044715
+
+
+def part(i, size):
+    return pl.ds(pl.multiple_of(i * size, size), size)
+
+
+class Reduce:
+    def __init__(self, me, sends, own, given, core_in, z_in, keep):
+        self.me, self.sends = me, sends
+        self.own, self.given, self.core_in, self.z_in, self.keep = own, given, core_in, z_in, keep
+        self.width = keep.shape[-1]
+
+    def start(self):
+        self.core = self.sends.put(self.given, self.core_in, self.me.core_dev())
+
+    def along(self):
+        me, lanes = self.me, pl.ds(0, self.width)
+        self.core.wait_recv()
+        self.sends.sent(self.core)
+        self.copies = []
+        for k in range(1, me.nz):
+            to = (me.z + k) % me.nz
+
+            def both(i, at):
+                both = self.own[to, at, lanes] + self.core_in[to, at].astype(f32)
+                self.given[to, at] = both.astype(bf16)
+
+            each(128, 32, both)
+            self.copies.append(
+                self.sends.put(self.given.at[to], self.z_in.at[k - 1], me.z_dev(k))
+            )
+
+        def mine(i, at):
+            self.keep[at] = self.own[me.z, at, lanes] + self.core_in[me.z, at].astype(f32)
+
+        each(128, 32, mine)
+
+    def total(self):
+        for copy in self.copies:
+            copy.wait_recv()
+
+        def more(i, at):
+            self.keep[at] += sum(self.z_in[k, at].astype(f32) for k in range(self.me.nz - 1))
+
+        each(128, 32, more)
+
+
+def each(count, step, body):
+    def one(i, _):
+        body(i, part(i, step))
+        return 0
+
+    lax.fori_loop(0, count // step, one, 0)
+
+
+def whole_kernel(ins, outs, b, send_sems, recv_sems):
+    me = Place()
+    nz, n = me.nz, me.n
+    rows, tok = ins.w_out.shape[0], ins.tokens.shape[0]
+    peers = [me.head_dev(k) for k in range(3)]
+    greet(
+        peers
+        + [me.z_dev(k) for k in range(1, nz)]
+        + [me.core_dev()]
+        + [me.seq_dev(k) for k in (1, 2, -1, -2)]
+    )
+    sends = Sends(send_sems, recv_sems)
+    core_dev = me.core_dev()
+    half = pl.ds(me.core * nz, nz)
+    wide = 6 * HD
+
+    lane = lax.broadcasted_iota(jnp.int32, (rows, 128), 1)
+    line = lax.broadcasted_iota(jnp.int32, (rows, 128), 0)
+    group = 128 // rows
+    gains = jnp.zeros((rows, 128), f32)
+    for j, gain in enumerate((ins.norm_one, ins.norm_two)):
+        row = jnp.concatenate([gain[...].astype(f32)] * group, axis=1)
+        gains = jnp.where((lane // rows == me.s % group) & (line == j), row, gains)
+    b.gains[...] = gains.astype(bf16)
+    first, first_up, toks = [], [], []
+    parts = (ins.w_query, ins.w_key, ins.w_value)
+    for k in range(3):
+        for j, w in enumerate(parts):
+            src = w.at[:, part(me.heads[k], 256)]
+            first.append(sends.put(src, b.a1.at[me.h, :, j * 256 : j * 256 + 256], peers[k]))
+        first.append(sends.put(b.gains, b.a1.at[me.h, :, wide:], peers[k]))
+    for k in range(3):
+        own = b.x.at[part(me.h, tok)]
+        toks.append(sends.put(ins.tokens, own, peers[k]))
+    for k in range(3):
+        src = ins.w_up.at[:, part(me.heads[k], 1024)]
+        first_up.append(sends.put(src, b.u1.at[me.h], peers[k]))
+    for j, w in enumerate(parts):
+        b.a1[me.h, :, j * 256 : j * 256 + 256] = w[:, part(me.h, 256)]
+    b.a1[me.h, :, wide:] = b.gains[...]
+    b.x[part(me.h, tok)] = ins.tokens[...]
+    b.u1[me.h] = ins.w_up[:, part(me.h, 1024)]
+    b.wo[me.h, me.s] = ins.w_out[...]
+    b.dn[me.s] = ins.w_down[...]
+    b.cots[part(me.h, tok)] = ins.cotangent[...]
+    for copy in first:
+        copy.wait_recv()
+    w_z = [sends.put(b.a1, b.wb.at[:, me.s], me.z_dev(k)) for k in range(1, nz)]
+    w_c = [sends.put(b.a1, b.wb.at[:, me.s], core_dev)]
+    b.wb[:, me.s] = b.a1[...]
+    own = b.wo.at[me.h, me.s]
+    wo_z = [sends.put(ins.w_out, own, me.z_dev(k)) for k in range(1, nz)]
+    wo_c = [sends.put(ins.w_out, own, core_dev)]
+    segs = Segs(me, ins.segments, b.rows, b.cols)
+    fill_tables(ins.table, ins.decay, b.near, b.far, b.decay, b.enter, b.leave)
+    for k in range(1, nz):
+        w_z[k - 1].wait_recv()
+        piece = b.wb.at[:, me.z_from(k)]
+        w_c.append(sends.put(piece, piece, core_dev))
+    for copy in first_up:
+        copy.wait_recv()
+    up_z = [sends.put(b.u1, b.up.at[:, me.s], me.z_dev(k)) for k in range(1, nz)]
+    up_c = [sends.put(b.u1, b.up.at[:, me.s], core_dev)]
+    b.up[:, me.s] = b.u1[...]
+    dn_z = [sends.put(ins.w_down, b.dn.at[me.s], me.z_dev(k)) for k in range(1, nz)]
+    dn_c = [sends.put(ins.w_down, b.dn.at[me.s], core_dev)]
+    for copy in w_c:
+        copy.wait_recv()
+    lanes = []
+    for h in range(4):
+        for s in range(0, n, group):
+            lanes.append(sum(b.wb[h, s + i, :, wide:].astype(f32) for i in range(group)))
+    gains = jnp.concatenate(lanes, axis=1)
+    gain_one, gain_two = gains[0:1], gains[1:2]
+    for copy in toks:
+        copy.wait_recv()
+
+    def norm_one(i, at):
+        x = b.x[at].astype(f32)
+        b.hall[at] = (x * rms(x) * gain_one).astype(bf16)
+
+    each(4 * tok, 32, norm_one)
+
+    def project(t, _):
+        at = part(t, tok)
+        for j in range(3):
+            w = b.wb[:, :, :, j * 256 : j * 256 + 256].reshape(1024, 256)
+            out = dot(b.hall[at], w).astype(bf16)
+            for head in range(2):
+                mine = out[:, head * HD : head * HD + HD]
+                if j == 0:
+                    b.q[head, at] = mine
+                else:
+                    b.kvx[2 * (j - 1) + head, part(t + 2, tok)] = mine
+        return 0
+
+    lax.fori_loop(0, 4, project, 0)
+    halo = sends.put(b.kvx.at[:, 4 * TILE :], b.kvx.at[:, : 2 * TILE], me.seq_dev(1))
+
+    falls = [power(ins.decay[0, head], float(TILE)) for head in range(2)]
+    for head in range(2):
+        state = jnp.zeros((HD, HD), f32)
+        for t in range(4):
+            at = pl.ds((t + 2) * TILE, TILE)
+            key = (b.kvx[head, at].astype(f32) * (b.leave[head] * segs.kept(t))).astype(bf16)
+            add = t_dot(key, b.kvx[2 + head, at])
+            b.local[4 * head + t] = add
+            state = falls[head] * segs.keep[t] * state + add
+        b.sent[head] = state.astype(bf16)
+    carry = [sends.put(b.sent, b.got.at[k - 1], me.seq_dev(k)) for k in (1, 2)]
+    for k in range(1, nz):
+        wo_z[k - 1].wait_recv()
+        piece = b.wo.at[me.h, me.z_from(k)]
+        wo_c.append(sends.put(piece, piece, core_dev))
+    for copy in wo_c:
+        copy.wait_recv()
+    own = b.wo.at[me.h, half]
+    wo_h = [sends.put(own, own, peers[k]) for k in range(3)]
+    own = b.cots.at[part(me.h, tok)]
+    cots = [sends.put(ins.cotangent, own, peers[k]) for k in range(3)]
+
+    def forward(index, base):
+        head, t = index // 2, base + index % 2
+        at, own = part(t, TILE), part(t + 2, TILE)
+        wide = pl.ds(pl.multiple_of(t * TILE, TILE), 3 * TILE)
+        raw = dot_t(b.q[head, at], b.kvx[head, wide])
+        s0, s1, s2, same = tile_scores(raw, head, t, ins.table, b.near, b.far, segs)
+        top = jnp.maximum(jnp.maximum(s0, s1), s2).max(axis=1, keepdims=True)
+        e0, e1, e2 = jnp.exp2(s0 - top), jnp.exp2(s1 - top), jnp.exp2(s2 - top)
+        mass = (e0 + e1 + e2).sum(axis=1, keepdims=True)
+        b.lse[4 * head + t] = top + jnp.log2(mass)
+        mix = jnp.concatenate([e0.astype(bf16), e1.astype(bf16), e2.astype(bf16)], axis=1)
+        att = dot(mix, b.kvx[2 + head, wide]) / mass
+        weight = jnp.where(same, raw[:, 2 * TILE :] * b.decay[head], 0.0).astype(bf16)
+        b.acc[head, at] = att + dot(weight, b.kvx[2 + head, own])
+        return base
+
+    lax.fori_loop(0, 4, forward, 2)
+    halo.wait_recv()
+    lax.fori_loop(0, 4, forward, 0)
+    for copy in wo_h:
+        copy.wait_recv()
+    for k in range(3):
+        piece = b.wo.at[me.heads[k], half]
+        wo_c.append(sends.put(piece, piece, core_dev))
+    for copy in carry:
+        copy.wait_recv()
+    for head in range(2):
+        past = power(ins.decay[0, head], 4.0 * TILE) * segs.keep_before
+        state = b.got[0, head].astype(f32) + past * b.got[1, head].astype(f32)
+        for t in range(4):
+            at = pl.ds(t * TILE, TILE)
+            b.state[4 * head + t] = state
+            reach = b.enter[head] * segs.live(t)
+            y = b.acc[head, at] + dot(b.q[head, at], state.astype(bf16)) * reach
+            b.dyt[2 * t + head] = y.astype(bf16)
+            state = falls[head] * segs.keep[t] * state + b.local[4 * head + t]
+    ys = []
+    for k in range(3):
+        for head in range(2):
+            src = b.dyt.at[2 * me.heads[k] + head]
+            ys.append(sends.put(src, b.ymix.at[:, part(2 * me.h + head, HD)], peers[k]))
+    for head in range(2):
+        b.ymix[:, part(2 * me.h + head, HD)] = b.dyt[2 * me.h + head]
+    for k in range(1, nz):
+        up_z[k - 1].wait_recv()
+        piece = b.up.at[:, me.z_from(k)]
+        up_c.append(sends.put(piece, piece, core_dev))
+    for copy in ys + wo_c[-3:]:
+        copy.wait_recv()
+
+    def out_tile(j, _):
+        cols = part(j, 256)
+        w = b.wo[:, :, :, cols].reshape(1024, 256)
+        b.x1[:, cols] = ins.tokens[:, cols].astype(f32) + dot(b.ymix[...], w)
+        return 0
+
+    lax.fori_loop(0, 4, out_tile, 0)
+    def norm_two(i, at):
+        x = b.x1[at]
+        b.h2all[pl.ds(pl.multiple_of(me.h * tok + i * 32, 32), 32)] = (x * rms(x) * gain_two).astype(bf16)
+        b.base[at] = x
+
+    each(tok, 32, norm_two)
+    own = b.h2all.at[part(me.h, tok)]
+    h2s = [sends.put(own, own, peers[k]) for k in range(3)]
+    for k in range(1, nz):
+        dn_z[k - 1].wait_recv()
+        piece = b.dn.at[me.z_from(k)]
+        dn_c.append(sends.put(piece, piece, core_dev))
+    for copy in up_c + dn_c + cots:
+        copy.wait_recv()
+    dn2_copies = []
+    for k in range(-1, 3):
+        at = part(me.h if k < 0 else me.heads[k], tok)
+        if k >= 0:
+            h2s[k].wait_recv()
+
+        def hidden(j, _):
+            cols = part(j, 256)
+            u = dot(b.h2all[at], b.up[:, :, :, cols].reshape(1024, 256))
+            dg = dot_t(b.cots[at], b.dn[pl.ds(2 * j, 2)].reshape(256, 1024))
+            uu = u * u
+            t = jnp.tanh(GELU_C * u * (1.0 + GELU_A * uu))
+            b.x[at, cols] = (0.5 * u * (1.0 + t)).astype(bf16)
+            slope = 0.5 * (1.0 + t) + (0.5 * GELU_C) * u * (1.0 - t * t) * (1.0 + 3.0 * GELU_A * uu)
+            b.du[at, cols] = (slope * dg).astype(bf16)
+            return 0
+
+        lax.fori_loop(0, 4, hidden, 0)
+
+        def back(j, _):
+            w = b.up[j].reshape(256, 1024)
+            b.dn2s[k + 1, :, part(j, 256)] = dot_t(b.du[at], w).astype(bf16)
+            return 0
+
+        lax.fori_loop(0, 4, back, 0)
+        if k >= 0:
+            dn2_copies.append(sends.put(b.dn2s.at[k + 1], b.dnin.at[k], peers[k]))
+
+        def ahead(j, _):
+            cols = part(j, 256)
+            out = dot(b.x[at], b.dn[:, :, cols].reshape(1024, 256))
+            if k < 0:
+                b.base[:, cols] = b.base[:, cols] + out
+            else:
+                b.outp[k, :, cols] = out.astype(bf16)
+            return 0
+
+        lax.fori_loop(0, 4, ahead, 0)
+
+    def down_tile(j, _):
+        b.tile[...] = t_dot(b.x[:, part(j, 256)], b.cots[...])
+        b.own[j] = b.tile[part(me.core, 128)]
+        b.given_a[j] = b.tile[part(1 - me.core, 128)].astype(bf16)
+        return 0
+
+    lax.fori_loop(0, 4, down_tile, 0)
+    down = Reduce(me, sends, b.own, b.given_a, b.core_a, b.z_a, outs.grad_down)
+    down.start()
+
+    for copy in dn2_copies:
+        copy.wait_recv()
+    b.norms[...] = jnp.zeros_like(b.norms)
+
+    def second_norm_back(i, at):
+        dn2 = b.dn2s[0, at].astype(f32) + sum(b.dnin[k, at].astype(f32) for k in range(3))
+        x = b.x1[at]
+        scale = rms(x)
+        n2 = x * scale
+        b.norms[1:2] += jnp.sum(dn2 * n2, axis=0, keepdims=True)
+        spread = dn2 * gain_two
+        dx1 = ins.cotangent[at].astype(f32) + scale * (
+            spread - n2 * jnp.mean(spread * n2, axis=-1, keepdims=True)
+        )
+        b.x1[at] = dx1
+        b.da[at] = dx1.astype(bf16)
+
+    each(tok, 32, second_norm_back)
+    for copy in ys + dn2_copies + dn_c[1:]:
+        sends.sent(copy)
+
+    def back_tile(j, _):
+        out = dot_t(b.da[...], b.wo[j].reshape(256, 1024)).astype(bf16)
+        b.dyt[2 * j] = out[:, :HD]
+        b.dyt[2 * j + 1] = out[:, HD:]
+        return 0
+
+    lax.fori_loop(0, 4, back_tile, 0)
+    dys = []
+    for k in range(3):
+        src = b.dyt.at[pl.ds(2 * me.heads[k], 2)]
+        dys.append(sends.put(src, b.dyh.at[:, part(me.h, tok)], peers[k]))
+    b.dyh[:, part(me.h, tok)] = b.dyt[pl.ds(2 * me.h, 2)]
+    down.along()
+
+    def up_tile(j, _):
+        b.tile[...] = t_dot(b.h2all[:, part(j, 256)], b.du[...])
+        for z in range(nz):
+            b.own[z, part(j, 32)] = b.tile[part(2 * z + me.core, 32)]
+            b.given_b[z, part(j, 32)] = b.tile[part(2 * z + 1 - me.core, 32)].astype(bf16)
+        return 0
+
+    lax.fori_loop(0, 4, up_tile, 0)
+    up = Reduce(me, sends, b.own, b.given_b, b.core_b, b.z_b, b.up_sum)
+    up.start()
+    for copy in dys:
+        copy.wait_recv()
+    for zero in (b.sums, b.dks, b.dvs, b.diag, b.below, b.rest):
+        zero[...] = jnp.zeros_like(zero)
+    for head in range(2):
+        grad = jnp.zeros((HD, HD), f32)
+        for t in range(3, -1, -1):
+            at = pl.ds(t * TILE, TILE)
+            query = (b.q[head, at].astype(f32) * (b.enter[head] * segs.live(t))).astype(bf16)
+            add = t_dot(query, b.dyh[head, at])
+            b.local[4 * head + t] = add
+            grad = falls[head] * segs.keep[t] * grad + add
+        b.sent_back[head] = grad.astype(bf16)
+    carry = [sends.put(b.sent_back, b.got_back.at[k - 1], me.seq_dev(-k)) for k in (1, 2)]
+    up.along()
+
+    def grad_out_tile(j, _):
+        b.tile[...] = t_dot(b.ymix[:, part(j, 256)], b.da[...])
+        for z in range(nz):
+            b.own[j, part(z, 32)] = b.tile[part(2 * z + me.core, 32)]
+            b.dn[j, part(z, 32)] = b.tile[part(2 * z + 1 - me.core, 32)].astype(bf16)
+        return 0
+
+    lax.fori_loop(0, 4, grad_out_tile, 0)
+    o_core = sends.put(b.dn.at[0:4], b.core_o, core_dev)
+    outp = [sends.put(b.outp.at[k], b.dnin.at[k], peers[k]) for k in range(3)]
+
+    gap = (grid_of(0) - grid_of(1)).astype(f32)
+
+    def backward(index, base):
+        head, t = index // 2, base + index % 2
+        at, wide = part(t, TILE), pl.ds(pl.multiple_of(t * TILE, TILE), 3 * TILE)
+        query, dy = b.q[head, at], b.dyh[head, at]
+        keys, values = b.kvx[head, wide], b.kvx[2 + head, wide]
+        raw = dot_t(query, keys)
+        s0, s1, s2, same = tile_scores(raw, head, t, ins.table, b.near, b.far, segs)
+        lse = b.lse[4 * head + t]
+        p0, p1, p2 = jnp.exp2(s0 - lse), jnp.exp2(s1 - lse), jnp.exp2(s2 - lse)
+        dp = dot_t(dy, values)
+        dp0, dp1, dp2 = dp[:, :TILE], dp[:, TILE : 2 * TILE], dp[:, 2 * TILE :]
+        mean = (p0 * dp0 + p1 * dp1 + p2 * dp2).sum(axis=1, keepdims=True)
+        d0, d1, d2 = p0 * (dp0 - mean), p1 * (dp1 - mean), p2 * (dp2 - mean)
+        b.diag[head] += d2[:HD, :HD] + d2[HD:, HD:]
+        b.below[head] += d2[HD:, :HD] + d1[:HD, HD:]
+        b.rest[head] += (
+            (d0[:, :HD] + d0[:, HD:]).sum(axis=0, keepdims=True)
+            + d1[:, :HD].sum(axis=0, keepdims=True)
+            + d1[HD:, HD:].sum(axis=0, keepdims=True)
+        )
+        weight = jnp.where(same, b.decay[head], 0.0)
+        mixed = weight * raw[:, 2 * TILE :]
+        turn = weight * dp2
+        slope = mixed * dp2 * gap
+        b.sums[head] -= (slope[:, :HD] + slope[:, HD:]).sum(axis=0, keepdims=True)
+        scale = 1.0 / math.sqrt(HD)
+        x = jnp.concatenate(
+            [(d0 * scale).astype(bf16), (d1 * scale).astype(bf16), (d2 * scale + turn).astype(bf16)],
+            axis=1,
+        )
+        p = jnp.concatenate([p0.astype(bf16), p1.astype(bf16), (p2 + mixed).astype(bf16)], axis=1)
+        b.acc[head, at] = dot(x, keys)
+        b.dks[head, wide] += t_dot(x, query)
+        b.dvs[head, wide] += t_dot(p, dy)
+        return base
+
+    lax.fori_loop(0, 4, backward, 0)
+    for copy in dys:
+        sends.sent(copy)
+    for head in range(2):
+        for i in range(2):
+            at = pl.ds(i * TILE, TILE)
+            b.dyt[2 * head + i] = b.dks[head, at].astype(bf16)
+            b.dyt[4 + 2 * head + i] = b.dvs[head, at].astype(bf16)
+    halo = sends.put(b.dyt, b.halo_in, me.seq_dev(-1))
+    o_core.wait_recv()
+    for copy in down.copies:
+        sends.sent(copy)
+    o_head = []
+    for k in range(3):
+        to = me.heads[k]
+
+        def chip_sum(i, at):
+            both = b.own[to, at] + b.core_o[to, at].astype(f32)
+            b.given_a[k, at] = both.astype(bf16)
+
+        each(128, 32, chip_sum)
+        o_head.append(sends.put(b.given_a.at[k], b.o_in.at[k], peers[k]))
+
+    def keep(i, at):
+        b.o_keep[at] = b.own[me.h, at] + b.core_o[me.h, at].astype(f32)
+
+    each(128, 32, keep)
+    lax.fori_loop(0, 4, backward, 2)
+    for copy in carry:
+        copy.wait_recv()
+    place = grid_of(0, (TILE, 1)).astype(f32)
+    halo.wait_recv()
+    for head in range(2):
+        past = power(ins.decay[0, head], 4.0 * TILE) * segs.keep_after
+        grad = b.got_back[0, head].astype(f32) + past * b.got_back[1, head].astype(f32)
+        fall = falls[head]
+        total = jnp.zeros((1, HD), f32)
+        for t in range(3, -1, -1):
+            at = pl.ds(t * TILE, TILE)
+            ext = pl.ds((t + 2) * TILE, TILE)
+            low = grad.astype(bf16)
+            state = b.state[4 * head + t]
+            give = b.leave[head] * segs.kept(t)
+            take = b.enter[head] * segs.live(t)
+            query, key, value = b.q[head, at], b.kvx[head, ext], b.kvx[2 + head, ext]
+            dq = dot_t(b.dyh[head, at], state.astype(bf16)) * take
+            dv = dot(key, low) * give
+            dk = dot_t(value, low) * give + b.dks[head, ext]
+            slope = dq * query.astype(f32) * (place + 1.0)
+            slope = slope + dv * value.astype(f32) * (TILE - 1.0 - place)
+            crossing = fall * segs.keep[t]
+            total = total - slope.sum(axis=0, keepdims=True)
+            total = total - TILE * crossing * (grad * state).sum(axis=0, keepdims=True)
+            dv = dv + b.dvs[head, ext]
+            if t >= 2:
+                dk = dk + b.halo_in[2 * head + t - 2].astype(f32)
+                dv = dv + b.halo_in[4 + 2 * head + t - 2].astype(f32)
+            for j, grads in enumerate((b.acc[head, at] + dq, dk, dv)):
+                col = (2 * j + head) * HD
+                b.x[at, col : col + HD] = grads.astype(bf16)
+            grad = b.local[4 * head + t] + crossing * grad
+        b.sums[head] += total
+
+    backs = []
+    for k in range(3):
+        at, to = part(me.heads[k], tok), pl.ds(k * tok, tok)
+
+        def spread_back(j, _):
+            w = b.wb[j, :, :, 0:wide].reshape(256, wide)
+            b.du[to, part(j, 256)] = dot_t(b.x[at, 0:wide], w).astype(bf16)
+            return 0
+
+        lax.fori_loop(0, 4, spread_back, 0)
+        backs.append(sends.put(b.du.at[to], b.dn2s.at[k + 1], peers[k]))
+
+    def grad_tile(j, _):
+        tile = pl.ds(0, wide)
+        b.tile[:, tile] = t_dot(b.hall[:, part(j, 256)], b.x[:, 0:wide])
+        for z in range(nz):
+            b.own[z, part(j, 32), tile] = b.tile[part(2 * z + me.core, 32), tile]
+            b.dn[4 + z, part(j, 32), tile] = b.tile[part(2 * z + 1 - me.core, 32), tile].astype(bf16)
+        return 0
+
+    lax.fori_loop(0, 4, grad_tile, 0)
+    grads = Reduce(me, sends, b.own, b.dn.at[4:8, :, 0:wide], b.core_q, b.z_q, b.q_sum)
+    grads.start()
+    for copy in outp:
+        copy.wait_recv()
+
+    def output(i, at):
+        total = b.base[at] + sum(b.dnin[k, at].astype(f32) for k in range(3))
+        outs.output[at] = total.astype(bf16)
+
+    each(tok, 32, output)
+
+    def own_back(j, _):
+        w = b.wb[j, :, :, 0:wide].reshape(256, wide)
+        b.base[:, part(j, 256)] = dot_t(b.x[part(me.h, tok), 0:wide], w)
+        return 0
+
+    lax.fori_loop(0, 4, own_back, 0)
+    grads.along()
+    for copy in o_head:
+        copy.wait_recv()
+
+    def grad_out_sum(i, at):
+        total = b.o_keep[at] + sum(b.o_in[k, at].astype(f32) for k in range(3))
+        b.o_keep[at] = total
+        b.o_low[at] = total.astype(bf16)
+
+    each(128, 32, grad_out_sum)
+    o_z = []
+    for k in range(1, nz):
+        src = b.o_low.at[part((me.z + k) % nz, 32)]
+        o_z.append(sends.put(src, b.o_z.at[k - 1], me.z_dev(k)))
+    down.total()
+    up.total()
+    ups = []
+    for k in range(3):
+        src = b.up_sum.at[part(me.heads[k], 32)]
+        ups.append(sends.put(src, outs.grad_up.at[:, part(me.h, 1024)], peers[k]))
+    outs.grad_up[:, part(me.h, 1024)] = b.up_sum[part(me.h, 32)]
+    gap_near = grid_of(0, (HD, HD)) - grid_of(1, (HD, HD))
+    gap_far = gap_near + HD
+    table = []
+    for head in range(2):
+        last = b.rest[head]
+        for i in range(BUCKETS):
+            up_to = STARTS[i + 1] if i + 1 < BUCKETS else 2 * WIN
+            inside = lambda g: (g >= STARTS[i]) & (g < up_to)
+            total = jnp.where(inside(gap_near), b.diag[head], 0.0)
+            total = total + jnp.where(inside(gap_far), b.below[head], 0.0)
+            total = total.sum(axis=0, keepdims=True)
+            table.append(total + last if i == BUCKETS - 1 else total)
+    table += [b.sums[0], b.sums[1], jnp.zeros((HD - 2 * BUCKETS - 2, HD), f32)]
+    small = lax.dot_general(
+        jnp.ones((8, HD), f32), jnp.concatenate(table, axis=0), (((1,), (1,)), ((), ())),
+        precision=lax.Precision.HIGHEST, preferred_element_type=f32,
+    )
+    b.norms[2:3, 0:HD] = small[0:1]
+    for copy in backs:
+        copy.wait_recv()
+
+    def first_norm_back(i, at):
+        dn1 = b.base[at] + sum(b.dn2s[k + 1, at].astype(f32) for k in range(3))
+        x = ins.tokens[at].astype(f32)
+        scale = rms(x)
+        n1 = x * scale
+        b.norms[0:1] += jnp.sum(dn1 * n1, axis=0, keepdims=True)
+        spread = dn1 * gain_one
+        dx = b.x1[at] + scale * (spread - n1 * jnp.mean(spread * n1, axis=-1, keepdims=True))
+        outs.input_grad[at] = dx.astype(bf16)
+
+    each(tok, 32, first_norm_back)
+    n_core = sends.put(b.norms, b.n_core, core_dev)
+    n_core.wait_recv()
+    b.n_chip[...] = b.norms[...] + b.n_core[...]
+    n_z = [sends.put(b.n_chip, b.n_z.at[k - 1], me.z_dev(k)) for k in range(1, nz)]
+    grads.total()
+    g_head = []
+    for k in range(3):
+        src = b.q_sum.at[part(me.heads[k], 32)]
+        g_head.append(sends.put(src, b.q_in.at[me.h], peers[k]))
+    b.q_in[me.h] = b.q_sum[part(me.h, 32)]
+    total = b.n_chip[...]
+    for k in range(nz - 1):
+        n_z[k].wait_recv()
+        total = total + b.n_z[k]
+    b.n_line[...] = total
+    n_head = [sends.put(b.n_line, b.n_head.at[k], peers[k]) for k in range(3)]
+    outs.sums[...] = total[:, 0:HD]
+    total = b.o_keep[part(me.z, 32)]
+    for k in range(nz - 1):
+        o_z[k].wait_recv()
+        total = total + b.o_z[k].astype(f32)
+    outs.grad_out[...] = total
+    for copy in g_head:
+        copy.wait_recv()
+    for h in range(4):
+        for j, out in enumerate((outs.grad_query, outs.grad_key, outs.grad_value)):
+            out[:, h * 256 : h * 256 + 256] = b.q_in[h, :, j * 256 : j * 256 + 256]
+    for copy in n_head + ups:
+        copy.wait_recv()
+    outs.norms[...] = b.n_line[...] + sum(b.n_head[k] for k in range(3))
+    sends.finish()
+
+
+class Names:
+    def __init__(self, names, values):
+        self.__dict__.update(zip(names, values))
+
+
+def shards(
+    tokens, cotangent, segments, w_query, w_key, w_value, w_out, w_up, w_down,
+    norm_one, norm_two, rel_table, decay_rate,
+):
+    n = lax.axis_size("seq")
+    nz = n // 2
+    tok, rows = tokens.shape[0], w_query.shape[0]
+    block = 4 * tok
+    wide = 6 * HD
+    ins = dict(
+        table=rel_table, decay=decay_rate.reshape(1, 2), segments=segments.reshape(-1, 128),
+        tokens=tokens, cotangent=cotangent, w_query=w_query, w_key=w_key, w_value=w_value,
+        w_out=w_out, w_up=w_up, w_down=w_down,
+        norm_one=norm_one.reshape(1, rows), norm_two=norm_two.reshape(1, rows),
+    )
+    outs = dict(
+        output=((tok, 1024), bf16), input_grad=((tok, 1024), bf16),
+        grad_query=((rows, 1024), f32), grad_key=((rows, 1024), f32),
+        grad_value=((rows, 1024), f32), grad_out=((rows, 1024), f32),
+        grad_up=((rows, 4096), f32), grad_down=((128, 1024), f32),
+        norms=((8, 1024), f32), sums=((8, HD), f32),
+    )
+    pieces = (4, n, rows, 1024)
+    square = ((block, 1024), bf16)
+    three = ((3, tok, 1024), bf16)
+    tables = ((2, TILE, TILE), f32)
+    column = ((2, TILE, 1), f32)
+    heads = ((2, HD, HD), f32)
+    four = ((nz, 128, 1024), bf16)
+    room = dict(
+        gains=((rows, 128), bf16), a1=((4, rows, wide + 128), bf16), u1=((4, rows, 1024), bf16),
+        x=square, hall=square, wb=((4, n, rows, wide + 128), bf16), up=(pieces, bf16),
+        dn=((n, 128, 1024), bf16), wo=(pieces, bf16), cots=square,
+        q=((2, block, HD), bf16), kvx=((4, 6 * TILE, HD), bf16),
+        near=tables, far=tables, decay=tables, enter=column, leave=column,
+        rows=((6, 1, TILE), f32), cols=((4, TILE, 1), f32),
+        acc=((2, block, HD), f32), local=((8, HD, HD), f32), state=((8, HD, HD), f32),
+        lse=((8, TILE, 1), f32),
+        sent=((2, HD, HD), bf16), got=((2, 2, HD, HD), bf16),
+        sent_back=((2, HD, HD), bf16), got_back=((2, 2, HD, HD), bf16),
+        ymix=((tok, 1024), bf16),
+        x1=((tok, 1024), f32), base=((tok, 1024), f32), h2all=square, du=square,
+        dn2s=((4, tok, 1024), bf16), dnin=three, outp=three,
+        da=((tok, 1024), bf16), dyt=((8, tok, HD), bf16), dyh=((2, block, HD), bf16),
+        tile=((256, 1024), f32), own=((nz, 128, 1024), f32), o_keep=((128, 1024), f32),
+        given_a=four, core_a=four, z_a=((nz - 1, 128, 1024), bf16),
+        given_b=four, core_b=four, z_b=((nz - 1, 128, 1024), bf16), up_sum=((128, 1024), f32),
+        core_o=four, o_in=((3, 128, 1024), bf16), o_low=((128, 1024), bf16),
+        o_z=((nz - 1, 32, 1024), bf16),
+        core_q=((nz, 128, wide), bf16),
+        z_q=((nz - 1, 128, wide), bf16), q_sum=((128, wide), f32), q_in=((4, 32, wide), f32),
+        diag=heads, below=heads, rest=((2, 1, HD), f32), sums=((2, 1, HD), f32),
+        dks=((2, 6 * TILE, HD), f32), dvs=((2, 6 * TILE, HD), f32),
+        halo_in=((8, TILE, HD), bf16),
+        norms=((8, 1024), f32), n_core=((8, 1024), f32), n_chip=((8, 1024), f32),
+        n_z=((nz - 1, 8, 1024), f32), n_line=((8, 1024), f32), n_head=((3, 8, 1024), f32),
+    )
+    copies = 150
+
+    def kernel(*refs):
+        i, o = len(ins), len(ins) + len(outs)
+        r = o + len(room)
+        whole_kernel(Names(ins, refs[:i]), Names(outs, refs[i:o]), Names(room, refs[o:r]), *refs[r:])
+
+    results = pl.pallas_call(
+        kernel,
+        out_shape=[jax.ShapeDtypeStruct(shape, kind) for shape, kind in outs.values()],
+        in_specs=[pl.BlockSpec(memory_space=pltpu.SMEM)] * 2
+        + [pl.BlockSpec(memory_space=pltpu.VMEM)] * (len(ins) - 2),
+        out_specs=[pl.BlockSpec(memory_space=pltpu.VMEM)] * len(outs),
+        scratch_shapes=[pltpu.VMEM(shape, kind) for shape, kind in room.values()]
+        + [pltpu.SemaphoreType.DMA((copies,)), pltpu.SemaphoreType.DMA((copies,))],
+        compiler_params=pltpu.CompilerParams(
+            collective_id=0, has_side_effects=True, vmem_limit_bytes=63 << 20
+        ),
+        name="block_layer",
+    )(*ins.values())
+    r = Names(outs, results)
+    at = lax.axis_index("head") * 256 + lax.axis_index("seq") * rows
+    mine = lax.dynamic_slice(r.norms, (0, at), (2, rows))
+    sums = r.sums[2]
+    return (
+        r.output, r.input_grad, r.grad_query, r.grad_key, r.grad_value, r.grad_out, r.grad_up,
+        r.grad_down, mine[0], mine[1],
+        sums[: 2 * BUCKETS].reshape(2, BUCKETS), sums[2 * BUCKETS : 2 * BUCKETS + 2],
+    )
+
+
 highest = lax.Precision.HIGHEST
 
 
@@ -138,7 +1003,7 @@
     return (readouts.reshape(block_len, head_count, head_width), final_state)
 
 
-def shards(
+def general_shards(
     tokens,
     cotangent,
     segments,
@@ -403,8 +1268,10 @@
 
 
 def solution(mesh):
+    devices = mesh.shape["head"] * mesh.shape["seq"]
+    tiled = mesh.shape["head"] == 4 and 1024 // devices == 32
     return jax.shard_map(
-        shards,
+        shards if tiled else general_shards,
         mesh=mesh,
         in_specs=(
             P(("seq", "head"), None),

time: 1560 us -> 248 us (0.16)
  waiting for transfers between devices: 847 us -> 0 us
  Pallas kernels: 0 us -> 235 us
  local copies, waits for them, and re-layouts: 227 us -> 11.7 us
  matrix products: 183 us -> 0 us
  blocking collectives: 172 us -> 0 us
  other arithmetic: 73.9 us -> 0 us
  between operations: 17.6 us -> 0.68 us
  starting transfers between devices: 16.7 us -> 0 us
    reduce_scatter x6 -> x0, waiting for transfers between devices: 697 us -> none  [the longest x1 187 us: shards(): lax.psum_scatter(grad_down_w, ('head', 'seq'), scatter_dimension=0, tiled...]
    pallas_call x0 -> x1, Pallas kernels: none -> 235 us  [shards(): pl.pallas_call(kernel, out_shape=[jax.ShapeDtypeStruct(shape, kind) for s...]
    dot_general x61 -> x0, matrix products: 183 us -> none  [the longest x6 33.1 us: transposed_times(): lax.dot_general(left, right, (((0,), (0,)), ((), ())), preferred_element_...]
    all_gather x6 -> x0, waiting for transfers between devices: 133 us -> none  [the longest x1 56 us: shards(): lax.all_gather(w_query, ('head', 'seq'), axis=0, tiled=True)]
    unnamed x3 -> x0, blocking collectives: 95.1 us -> none
    dynamic_update_slice x18 -> x0, local copies, waits for them, and re-layouts: 38.3 us -> none  [the longest x12 36.3 us: shards(): attended_blocks, log_mass = lax.map(forward_block, numbers)]
    all_gather x2 -> x0, blocking collectives: 32.9 us -> none  [prefix(): lax.all_gather(a.astype(kind), axis)]
    reshape x10 -> x1, local copies, waits for them, and re-layouts: 30.4 us -> 0.64 us  [shards(): sums[:2 * BUCKETS].reshape(2, BUCKETS)]
  transfers between devices with their start and end apart: 17 -> 0, of which waited for: 11 -> 0; matrix products, arithmetic and copies ran while one was open for 29% -> 0% of each run, Pallas kernels for 0% -> 0%
where the time goes in v2:
time: 248 us
  Pallas kernels  235 us (95%)
  local copies, waits for them, and re-layouts  11.7 us (5%)
    pallas_call x1, Pallas kernels, shards(): pl.pallas_call(kernel, out_shape=[jax.ShapeDtypeStruct(shape, kind) for s...  235 us
    unnamed x22, local copies, waits for them, and re-layouts  7.87 us

profile of v2, /device:TPU:0, one launch (start us, length us, event | category | flops | bytes accessed | tf_op | source)
XLA Modules:
  0.0 247.8 jit_solution(9433463382887421138)
XLA Ops:
  0.7 235.4 %block_layer.1 = (bf16[256,1024]{1,0:T(8,128)(2,1)}, bf16[256,1024]{1,0:T(8,128)(2,1)}, f32[32,1024]{1,0:T(8,128)}, f32[32,1024]{1,0:T(8,128)}, f32[32,1024]{1,0...) custom-call(f32[2,32]{1,0:T(2,128)} %refs_0_.1, ...), custom_call_target="tpu_custom_call" | custom-call | tf_op jit(solution)/shard_map/block_layer/pallas_call | solution.py:858
  236.0 0.8 constant_dynamic-slice_fusion
  236.8 0.5 slice_bitcast_fusion.1
  237.3 0.7 slice_reduce_fusion
  238.0 0.6 reshape.46
  238.6 1.3 slice_bitcast_fusion
  239.9 0.0 copy-start.2
  239.9 1.9 copy.33
  241.8 0.0 copy-done.2
  241.8 0.0 copy-start.6
  241.8 0.0 copy-start.5
  241.8 0.8 copy.34
  242.6 0.2 copy-done.6
  242.8 0.7 copy.35
  243.5 0.0 copy-done.5
  243.5 0.7 copy.36
  244.1 0.0 copy-done.4
  244.1 0.7 copy.37
  244.8 0.3 copy-done.3
  245.1 0.7 copy.38
  245.8 0.0 copy-done.1
  245.8 0.8 copy.39
  246.5 0.4 copy-done
  247.0 0.8 copy.40
  (4 shorter events, 0.0 us)
Async XLA Ops:
  239.9 1.9 copy-start.2
  241.8 1.0 copy-start.6
  241.8 1.7 copy-start.5
  241.8 2.3 copy-start.4
  242.8 2.9 %copy-start.1 = (f32[32,4096]{1,0:T(8,128)S(1)}, f32[32,4096]{1,0:T(8,128)}, u32[]{:S(2)}) copy-start(f32[32,4096]{1,0:T(8,128)} %get-tuple-element.52) | copy-start | bytes 1572868
  244.1 1.0 copy-start.3
  245.8 1.2 copy-start

commit v3 on v2

--- a/solution.py
+++ b/solution.py
@@ -77,30 +77,129 @@
 class Sends:
     def __init__(self, send_sems, recv_sems):
         self.send_sems, self.recv_sems = send_sems, recv_sems
-        self.at, self.all = 0, []
-
-    def put(self, src, dst, device, start=True):
-        copy = pltpu.make_async_remote_copy(
+        self.sent_at, self.recv_at, self.all = 0, 0, []
+
+    def claim(self, count):
+        self.recv_at += count
+        return self.recv_at - count
+
+    def copy(self, src, dst, device, send, recv):
+        return pltpu.make_async_remote_copy(
             src_ref=src,
             dst_ref=dst,
-            send_sem=self.send_sems.at[self.at],
-            recv_sem=self.recv_sems.at[self.at],
+            send_sem=self.send_sems.at[send],
+            recv_sem=self.recv_sems.at[recv],
             device_id=device,
             device_id_type=MESH,
         )
-        self.at += 1
+
+    def put(self, src, dst, device, recv=None):
+        recv = self.claim(1) if recv is None else recv
+        copy = self.copy(src, dst, device, self.sent_at, recv)
+        self.sent_at += 1
         self.all.append(copy)
-        if start:
-            copy.start()
+        copy.start()
         return copy
 
-    def sent(self, copy):
-        copy.wait_send()
-        self.all = [c for c in self.all if c is not copy]
+    def sent(self, copies):
+        for copy in copies:
+            copy.wait_send()
+        self.all = [c for c in self.all if not any(c is d for d in copies)]
 
     def finish(self):
         for copy in self.all:
             copy.wait_send()
+
+
+class Line:
+    def __init__(self, me, sends, place):
+        self.me, self.sends, self.place = me, sends, place
+        z = me.z
+        inner = (z * (3 - z)) // 2
+        self.near, self.next = 1 + z % 2, 2 * (1 - z % 2) + z // 2
+        self.order = [self.near, self.next, 6 - z - self.near - self.next]
+        self.piece, self.end = z + inner * (3 - 2 * z), 3 * (1 - z % 2)
+        self.base = sends.claim(4)
+        self.copies = []
+
+    def put(self, src, chip, to):
+        me = self.me
+        device = (me.h, 2 * to + me.core)
+        self.copies.append(self.sends.put(src, self.place(chip), device, self.base + chip))
+
+    def start(self, own):
+        for to in (self.near, self.next):
+            self.put(own, self.me.z, to)
+
+    def wait(self, i):
+        chip = self.order[i]
+        ref = self.place(chip)
+        device = (self.me.h, 2 * chip + self.me.core)
+        self.sends.copy(ref, ref, device, 0, self.base + chip).wait_recv()
+        return ref
+
+    def relay(self):
+        ref = self.wait(0)
+        self.put(self.place(self.piece), self.piece, self.end)
+        return ref
+
+
+class Square:
+    def __init__(self, me, sends, block):
+        self.me, self.sends, self.block = me, sends, block
+
+    def start(self, own):
+        me = self.me
+        self.got = [
+            self.sends.put(own, self.block(me.h, None), me.head_dev(k)) for k in range(2)
+        ]
+        self.halves = []
+
+    def relay(self):
+        me = self.me
+        for k in range(2):
+            self.got[k].wait_recv()
+            ref = self.block(me.heads[k], k)
+            self.halves.append(self.sends.put(ref, ref, me.head_dev(1 - k)))
+
+    def last(self):
+        for copy in self.halves:
+            copy.wait_recv()
+
+
+class SquareSum:
+    def __init__(self, me, sends, give, land):
+        self.me, self.sends, self.give, self.land = me, sends, give, land
+        half = give(2).shape[0] // 2
+        self.parts = [pl.ds(0, half), pl.ds(half, half)]
+        self.half = half
+
+    def first(self):
+        me, give, land = self.me, self.give(2), self.land(2)
+        self.halves = [
+            self.sends.put(give.at[self.parts[k]], land.at[self.parts[k]], me.head_dev(k))
+            for k in range(2)
+        ]
+
+    def second(self):
+        me, land = self.me, self.land(2)
+        self.copies = []
+        for k in range(2):
+            self.halves[k].wait_recv()
+            give = self.give(1 - k)
+
+            def add(i, _):
+                at = pl.ds(pl.multiple_of(k * self.half + i * 32, 32), 32)
+                give[at] = (give[at].astype(f32) + land[at].astype(f32)).astype(bf16)
+                return 0
+
+            lax.fori_loop(0, self.half // 32, add, 0)
+        for k in range(2):
+            self.copies.append(self.sends.put(self.give(k), self.land(k), me.head_dev(k)))
+
+    def last(self):
+        for copy in self.copies:
+            copy.wait_recv()
 
 
 def rms(x):
@@ -208,36 +307,72 @@
     def start(self):
         self.core = self.sends.put(self.given, self.core_in, self.me.core_dev())
 
+    def put(self, chunk, to, slot):
+        me = self.me
+        device = (me.h, 2 * to + me.core)
+        src, dst = self.given.at[chunk], self.z_in.at[slot]
+        self.copies.append(self.sends.put(src, dst, device, self.base + slot))
+
+    def wait(self, slot):
+        ref = self.z_in.at[slot]
+        self.sends.copy(ref, ref, self.me.core_dev(), 0, self.base + slot).wait_recv()
+
+    def join(self):
+        me, lanes = self.me, pl.ds(0, self.width)
+        z = me.z
+        self.core.wait_recv()
+        self.sends.sent([self.core])
+        self.inner = (z * (3 - z)) // 2
+        self.beside, self.across, self.far = z + 1 - 2 * (z % 2), (z + 2) % 4, 3 - z
+        for chunk in (self.beside, self.across, self.far):
+
+            def both(i, at):
+                total = self.own[chunk, at, lanes] + self.core_in[chunk, at].astype(f32)
+                self.given[chunk, at] = total.astype(bf16)
+
+            each(128, 32, both)
+
+        def mine(i, at):
+            self.keep[at] = self.own[z, at, lanes] + self.core_in[z, at].astype(f32)
+
+        each(128, 32, mine)
+
     def along(self):
-        me, lanes = self.me, pl.ds(0, self.width)
-        self.core.wait_recv()
-        self.sends.sent(self.core)
-        self.copies = []
-        for k in range(1, me.nz):
-            to = (me.z + k) % me.nz
-
-            def both(i, at):
-                both = self.own[to, at, lanes] + self.core_in[to, at].astype(f32)
-                self.given[to, at] = both.astype(bf16)
-
-            each(128, 32, both)
-            self.copies.append(
-                self.sends.put(self.given.at[to], self.z_in.at[k - 1], me.z_dev(k))
-            )
-
-        def mine(i, at):
-            self.keep[at] = self.own[me.z, at, lanes] + self.core_in[me.z, at].astype(f32)
-
-        each(128, 32, mine)
+        self.base, self.copies = self.sends.claim(3), []
+        self.put(self.beside, self.beside, 0)
+        to = self.inner * self.across + (1 - self.inner) * self.beside
+        self.put(self.across, to, 2 - self.inner)
+
+    def late(self):
+        @pl.when(self.inner == 1)
+        def _():
+            self.wait(2)
+
+            def add(i, at):
+                total = self.given[self.far, at].astype(f32) + self.z_in[2, at].astype(f32)
+                self.given[self.far, at] = total.astype(bf16)
+
+            each(128, 32, add)
+
+        self.put(self.far, self.far, 2 - self.inner)
 
     def total(self):
-        for copy in self.copies:
-            copy.wait_recv()
+        for slot in range(2):
+            self.wait(slot)
 
         def more(i, at):
-            self.keep[at] += sum(self.z_in[k, at].astype(f32) for k in range(self.me.nz - 1))
+            self.keep[at] += self.z_in[0, at].astype(f32) + self.z_in[1, at].astype(f32)
 
         each(128, 32, more)
+
+        @pl.when(self.inner == 0)
+        def _():
+            self.wait(2)
+
+            def add(i, at):
+                self.keep[at] += self.z_in[2, at].astype(f32)
+
+            each(128, 32, add)
 
 
 def each(count, step, body):
@@ -255,9 +390,7 @@
     peers = [me.head_dev(k) for k in range(3)]
     greet(
         peers
-        + [me.z_dev(k) for k in range(1, nz)]
-        + [me.core_dev()]
-        + [me.seq_dev(k) for k in (1, 2, -1, -2)]
+        + [me.seq_dev(k) for k in range(1, n)]
     )
     sends = Sends(send_sems, recv_sems)
     core_dev = me.core_dev()
@@ -272,48 +405,63 @@
         row = jnp.concatenate([gain[...].astype(f32)] * group, axis=1)
         gains = jnp.where((lane // rows == me.s % group) & (line == j), row, gains)
     b.gains[...] = gains.astype(bf16)
-    first, first_up, toks = [], [], []
+    first = []
     parts = (ins.w_query, ins.w_key, ins.w_value)
     for k in range(3):
         for j, w in enumerate(parts):
             src = w.at[:, part(me.heads[k], 256)]
             first.append(sends.put(src, b.a1.at[me.h, :, j * 256 : j * 256 + 256], peers[k]))
         first.append(sends.put(b.gains, b.a1.at[me.h, :, wide:], peers[k]))
-    for k in range(3):
-        own = b.x.at[part(me.h, tok)]
-        toks.append(sends.put(ins.tokens, own, peers[k]))
+
+    def token_block(ref):
+        def block(i, piece):
+            if piece is None:
+                return ref.at[part(i, tok)]
+            return ref.at[part(2 * i + piece, tok // 2)]
+
+        return block
+
+    toks = Square(me, sends, token_block(b.x))
+    toks.start(ins.tokens)
+    first_up = []
     for k in range(3):
         src = ins.w_up.at[:, part(me.heads[k], 1024)]
         first_up.append(sends.put(src, b.u1.at[me.h], peers[k]))
+    w_line = Line(me, sends, lambda z: b.wb.at[:, 2 * z + me.core])
+    wo_line = Line(me, sends, lambda z: b.wo.at[me.h, 2 * z + me.core])
+    up_line = Line(me, sends, lambda z: b.up.at[:, 2 * z + me.core])
+    dn_line = Line(me, sends, lambda z: b.dn.at[2 * z + me.core])
     for j, w in enumerate(parts):
         b.a1[me.h, :, j * 256 : j * 256 + 256] = w[:, part(me.h, 256)]
     b.a1[me.h, :, wide:] = b.gains[...]
+    for copy in first:
+        copy.wait_recv()
+    w_line.start(b.a1)
+    w_c = [sends.put(b.a1, b.wb.at[:, me.s], core_dev)]
+    b.wb[:, me.s] = b.a1[...]
     b.x[part(me.h, tok)] = ins.tokens[...]
     b.u1[me.h] = ins.w_up[:, part(me.h, 1024)]
     b.wo[me.h, me.s] = ins.w_out[...]
     b.dn[me.s] = ins.w_down[...]
     b.cots[part(me.h, tok)] = ins.cotangent[...]
-    for copy in first:
-        copy.wait_recv()
-    w_z = [sends.put(b.a1, b.wb.at[:, me.s], me.z_dev(k)) for k in range(1, nz)]
-    w_c = [sends.put(b.a1, b.wb.at[:, me.s], core_dev)]
-    b.wb[:, me.s] = b.a1[...]
     own = b.wo.at[me.h, me.s]
-    wo_z = [sends.put(ins.w_out, own, me.z_dev(k)) for k in range(1, nz)]
+    w_c.append(sends.put((ref := w_line.relay()), ref, core_dev))
+    wo_line.start(ins.w_out)
     wo_c = [sends.put(ins.w_out, own, core_dev)]
+    toks.relay()
+    cots = Square(me, sends, token_block(b.cots))
+    cots.start(ins.cotangent)
     segs = Segs(me, ins.segments, b.rows, b.cols)
     fill_tables(ins.table, ins.decay, b.near, b.far, b.decay, b.enter, b.leave)
-    for k in range(1, nz):
-        w_z[k - 1].wait_recv()
-        piece = b.wb.at[:, me.z_from(k)]
-        w_c.append(sends.put(piece, piece, core_dev))
+    for i in (1, 2):
+        ref = w_line.wait(i)
+        w_c.append(sends.put(ref, ref, core_dev))
     for copy in first_up:
         copy.wait_recv()
-    up_z = [sends.put(b.u1, b.up.at[:, me.s], me.z_dev(k)) for k in range(1, nz)]
+    up_line.start(b.u1)
     up_c = [sends.put(b.u1, b.up.at[:, me.s], core_dev)]
     b.up[:, me.s] = b.u1[...]
-    dn_z = [sends.put(ins.w_down, b.dn.at[me.s], me.z_dev(k)) for k in range(1, nz)]
-    dn_c = [sends.put(ins.w_down, b.dn.at[me.s], core_dev)]
+    wo_c.append(sends.put((ref := wo_line.relay()), ref, core_dev))
     for copy in w_c:
         copy.wait_recv()
     lanes = []
@@ -322,8 +470,7 @@
             lanes.append(sum(b.wb[h, s + i, :, wide:].astype(f32) for i in range(group)))
     gains = jnp.concatenate(lanes, axis=1)
     gain_one, gain_two = gains[0:1], gains[1:2]
-    for copy in toks:
-        copy.wait_recv()
+    toks.last()
 
     def norm_one(i, at):
         x = b.x[at].astype(f32)
@@ -345,6 +492,7 @@
         return 0
 
     lax.fori_loop(0, 4, project, 0)
+    sends.sent(toks.halves)
     halo = sends.put(b.kvx.at[:, 4 * TILE :], b.kvx.at[:, : 2 * TILE], me.seq_dev(1))
 
     falls = [power(ins.decay[0, head], float(TILE)) for head in range(2)]
@@ -358,16 +506,23 @@
             state = falls[head] * segs.keep[t] * state + add
         b.sent[head] = state.astype(bf16)
     carry = [sends.put(b.sent, b.got.at[k - 1], me.seq_dev(k)) for k in (1, 2)]
-    for k in range(1, nz):
-        wo_z[k - 1].wait_recv()
-        piece = b.wo.at[me.h, me.z_from(k)]
-        wo_c.append(sends.put(piece, piece, core_dev))
+    up_c.append(sends.put((ref := up_line.relay()), ref, core_dev))
+    for i in (1, 2):
+        ref = wo_line.wait(i)
+        wo_c.append(sends.put(ref, ref, core_dev))
+    dn_line.start(ins.w_down)
+    dn_c = [sends.put(ins.w_down, b.dn.at[me.s], core_dev)]
+    cots.relay()
     for copy in wo_c:
         copy.wait_recv()
-    own = b.wo.at[me.h, half]
-    wo_h = [sends.put(own, own, peers[k]) for k in range(3)]
-    own = b.cots.at[part(me.h, tok)]
-    cots = [sends.put(ins.cotangent, own, peers[k]) for k in range(3)]
+
+    def wo_block(i, piece):
+        if piece is None:
+            return b.wo.at[i, half]
+        return b.wo.at[i, pl.ds(me.core * nz + piece * (nz // 2), nz // 2)]
+
+    wo_square = Square(me, sends, wo_block)
+    wo_square.start(b.wo.at[me.h, half])
 
     def forward(index, base):
         head, t = index // 2, base + index % 2
@@ -388,8 +543,9 @@
     lax.fori_loop(0, 4, forward, 2)
     halo.wait_recv()
     lax.fori_loop(0, 4, forward, 0)
-    for copy in wo_h:
-        copy.wait_recv()
+    wo_square.relay()
+    dn_c.append(sends.put((ref := dn_line.relay()), ref, core_dev))
+    wo_square.last()
     for k in range(3):
         piece = b.wo.at[me.heads[k], half]
         wo_c.append(sends.put(piece, piece, core_dev))
@@ -412,10 +568,9 @@
             ys.append(sends.put(src, b.ymix.at[:, part(2 * me.h + head, HD)], peers[k]))
     for head in range(2):
         b.ymix[:, part(2 * me.h + head, HD)] = b.dyt[2 * me.h + head]
-    for k in range(1, nz):
-        up_z[k - 1].wait_recv()
-        piece = b.up.at[:, me.z_from(k)]
-        up_c.append(sends.put(piece, piece, core_dev))
+    for i in (1, 2):
+        ref = up_line.wait(i)
+        up_c.append(sends.put(ref, ref, core_dev))
     for copy in ys + wo_c[-3:]:
         copy.wait_recv()
 
@@ -433,18 +588,21 @@
 
     each(tok, 32, norm_two)
     own = b.h2all.at[part(me.h, tok)]
-    h2s = [sends.put(own, own, peers[k]) for k in range(3)]
-    for k in range(1, nz):
-        dn_z[k - 1].wait_recv()
-        piece = b.dn.at[me.z_from(k)]
-        dn_c.append(sends.put(piece, piece, core_dev))
-    for copy in up_c + dn_c + cots:
+    h2s = Square(me, sends, token_block(b.h2all))
+    h2s.start(own)
+    for i in (1, 2):
+        ref = dn_line.wait(i)
+        dn_c.append(sends.put(ref, ref, core_dev))
+    cots.last()
+    for copy in up_c + dn_c:
         copy.wait_recv()
     dn2_copies = []
     for k in range(-1, 3):
         at = part(me.h if k < 0 else me.heads[k], tok)
-        if k >= 0:
-            h2s[k].wait_recv()
+        if k == 0:
+            h2s.relay()
+        elif k == 2:
+            h2s.last()
 
         def hidden(j, _):
             cols = part(j, 256)
@@ -507,8 +665,7 @@
         b.da[at] = dx1.astype(bf16)
 
     each(tok, 32, second_norm_back)
-    for copy in ys + dn2_copies + dn_c[1:]:
-        sends.sent(copy)
+    sends.sent(ys + dn2_copies + dn_c[1:] + dn_line.copies)
 
     def back_tile(j, _):
         out = dot_t(b.da[...], b.wo[j].reshape(256, 1024)).astype(bf16)
@@ -522,6 +679,7 @@
         src = b.dyt.at[pl.ds(2 * me.heads[k], 2)]
         dys.append(sends.put(src, b.dyh.at[:, part(me.h, tok)], peers[k]))
     b.dyh[:, part(me.h, tok)] = b.dyt[pl.ds(2 * me.h, 2)]
+    down.join()
     down.along()
 
     def up_tile(j, _):
@@ -534,8 +692,11 @@
     lax.fori_loop(0, 4, up_tile, 0)
     up = Reduce(me, sends, b.own, b.given_b, b.core_b, b.z_b, b.up_sum)
     up.start()
+    down.late()
     for copy in dys:
         copy.wait_recv()
+    outp = SquareSum(me, sends, lambda k: b.outp.at[k], lambda k: b.dnin.at[k])
+    outp.first()
     for zero in (b.sums, b.dks, b.dvs, b.diag, b.below, b.rest):
         zero[...] = jnp.zeros_like(zero)
     for head in range(2):
@@ -548,7 +709,7 @@
             grad = falls[head] * segs.keep[t] * grad + add
         b.sent_back[head] = grad.astype(bf16)
     carry = [sends.put(b.sent_back, b.got_back.at[k - 1], me.seq_dev(-k)) for k in (1, 2)]
-    up.along()
+    up.join()
 
     def grad_out_tile(j, _):
         b.tile[...] = t_dot(b.ymix[:, part(j, 256)], b.da[...])
@@ -559,7 +720,7 @@
 
     lax.fori_loop(0, 4, grad_out_tile, 0)
     o_core = sends.put(b.dn.at[0:4], b.core_o, core_dev)
-    outp = [sends.put(b.outp.at[k], b.dnin.at[k], peers[k]) for k in range(3)]
+    outp.second()
 
     gap = (grid_of(0) - grid_of(1)).astype(f32)
 
@@ -600,18 +761,16 @@
         return base
 
     lax.fori_loop(0, 4, backward, 0)
-    for copy in dys:
-        sends.sent(copy)
+    sends.sent(dys)
     for head in range(2):
         for i in range(2):
             at = pl.ds(i * TILE, TILE)
             b.dyt[2 * head + i] = b.dks[head, at].astype(bf16)
             b.dyt[4 + 2 * head + i] = b.dvs[head, at].astype(bf16)
     halo = sends.put(b.dyt, b.halo_in, me.seq_dev(-1))
+    up.along()
     o_core.wait_recv()
-    for copy in down.copies:
-        sends.sent(copy)
-    o_head = []
+    sends.sent(down.copies)
     for k in range(3):
         to = me.heads[k]
 
@@ -620,13 +779,16 @@
             b.given_a[k, at] = both.astype(bf16)
 
         each(128, 32, chip_sum)
-        o_head.append(sends.put(b.given_a.at[k], b.o_in.at[k], peers[k]))
+    o_square = SquareSum(me, sends, lambda k: b.given_a.at[k], lambda k: b.o_in.at[k])
+    o_square.first()
 
     def keep(i, at):
         b.o_keep[at] = b.own[me.h, at] + b.core_o[me.h, at].astype(f32)
 
     each(128, 32, keep)
     lax.fori_loop(0, 4, backward, 2)
+    o_square.second()
+    up.late()
     for copy in carry:
         copy.wait_recv()
     place = grid_of(0, (TILE, 1)).astype(f32)
@@ -662,8 +824,10 @@
             grad = b.local[4 * head + t] + crossing * grad
         b.sums[head] += total
 
-    backs = []
-    for k in range(3):
+    backs = SquareSum(
+        me, sends, lambda k: b.du.at[pl.ds(k * tok, tok)], lambda k: b.dn2s.at[k + 1]
+    )
+    for k in (2, 0, 1):
         at, to = part(me.heads[k], tok), pl.ds(k * tok, tok)
 
         def spread_back(j, _):
@@ -672,7 +836,8 @@
             return 0
 
         lax.fori_loop(0, 4, spread_back, 0)
-        backs.append(sends.put(b.du.at[to], b.dn2s.at[k + 1], peers[k]))
+        if k == 2:
+            backs.first()
 
     def grad_tile(j, _):
         tile = pl.ds(0, wide)
@@ -685,11 +850,11 @@
     lax.fori_loop(0, 4, grad_tile, 0)
     grads = Reduce(me, sends, b.own, b.dn.at[4:8, :, 0:wide], b.core_q, b.z_q, b.q_sum)
     grads.start()
-    for copy in outp:
-        copy.wait_recv()
+    backs.second()
+    outp.last()
 
     def output(i, at):
-        total = b.base[at] + sum(b.dnin[k, at].astype(f32) for k in range(3))
+        total = b.base[at] + sum(b.dnin[k, at].astype(f32) for k in range(2))
         outs.output[at] = total.astype(bf16)
 
     each(tok, 32, output)
@@ -700,12 +865,12 @@
         return 0
 
     lax.fori_loop(0, 4, own_back, 0)
+    grads.join()
     grads.along()
-    for copy in o_head:
-        copy.wait_recv()
+    o_square.last()
 
     def grad_out_sum(i, at):
-        total = b.o_keep[at] + sum(b.o_in[k, at].astype(f32) for k in range(3))
+        total = b.o_keep[at] + sum(b.o_in[k, at].astype(f32) for k in range(2))
         b.o_keep[at] = total
         b.o_low[at] = total.astype(bf16)
 
@@ -738,12 +903,11 @@
         jnp.ones((8, HD), f32), jnp.concatenate(table, axis=0), (((1,), (1,)), ((), ())),
         precision=lax.Precision.HIGHEST, preferred_element_type=f32,
     )
-    b.norms[2:3, 0:HD] = small[0:1]
-    for copy in backs:
-        copy.wait_recv()
+    grads.late()
+    backs.last()
 
     def first_norm_back(i, at):
-        dn1 = b.base[at] + sum(b.dn2s[k + 1, at].astype(f32) for k in range(3))
+        dn1 = b.base[at] + sum(b.dn2s[k + 1, at].astype(f32) for k in range(2))
         x = ins.tokens[at].astype(f32)
         scale = rms(x)
         n1 = x * scale
@@ -753,23 +917,23 @@
         outs.input_grad[at] = dx.astype(bf16)
 
     each(tok, 32, first_norm_back)
-    n_core = sends.put(b.norms, b.n_core, core_dev)
-    n_core.wait_recv()
-    b.n_chip[...] = b.norms[...] + b.n_core[...]
-    n_z = [sends.put(b.n_chip, b.n_z.at[k - 1], me.z_dev(k)) for k in range(1, nz)]
+    lines = [b.norms[j : j + 1, i * HD : i * HD + HD] for j in range(2) for i in range(8)]
+    b.small[...] = jnp.concatenate(lines + [small], axis=0)
+    n_seq = [sends.put(b.small, b.n_seq.at[k - 1], me.seq_dev(k)) for k in range(1, n)]
     grads.total()
     g_head = []
     for k in range(3):
         src = b.q_sum.at[part(me.heads[k], 32)]
         g_head.append(sends.put(src, b.q_in.at[me.h], peers[k]))
     b.q_in[me.h] = b.q_sum[part(me.h, 32)]
-    total = b.n_chip[...]
-    for k in range(nz - 1):
-        n_z[k].wait_recv()
-        total = total + b.n_z[k]
+    total = b.small[...]
+    for k in range(n - 1):
+        n_seq[k].wait_recv()
+        total = total + b.n_seq[k]
     b.n_line[...] = total
     n_head = [sends.put(b.n_line, b.n_head.at[k], peers[k]) for k in range(3)]
-    outs.sums[...] = total[:, 0:HD]
+    outs.table[...] = jnp.concatenate([total[16:17, i * BUCKETS : (i + 1) * BUCKETS] for i in range(2)], axis=0)
+    outs.rate[...] = total[16:17, 2 * BUCKETS : 2 * BUCKETS + 2]
     total = b.o_keep[part(me.z, 32)]
     for k in range(nz - 1):
         o_z[k].wait_recv()
@@ -782,8 +946,37 @@
             out[:, h * 256 : h * 256 + 256] = b.q_in[h, :, j * 256 : j * 256 + 256]
     for copy in n_head + ups:
         copy.wait_recv()
-    outs.norms[...] = b.n_line[...] + sum(b.n_head[k] for k in range(3))
+    total = b.n_line[...] + sum(b.n_head[k] for k in range(3))
+    b.norms[0:8, 0:HD], b.norms[0:8, HD : 2 * HD] = total[0:8], total[8:16]
+    mine = b.norms[pl.ds(2 * me.h + me.s // group, 1), 0 : 2 * HD]
+    for j, out in enumerate((outs.norm_one, outs.norm_two)):
+        row = jnp.zeros((1, rows), f32)
+        for i in range(group):
+            cut = mine[:, j * HD + i * rows : j * HD + (i + 1) * rows]
+            row = jnp.where(me.s % group == i, cut, row)
+        out[...] = row
     sends.finish()
+
+
+def placed(arrays):
+    def kernel(*refs):
+        count = len(refs) // 2
+        copies = [
+            pltpu.make_async_copy(refs[i], refs[count + i], refs[-1].at[i]) for i in range(count)
+        ]
+        for copy in copies:
+            copy.start()
+        for copy in copies:
+            copy.wait()
+
+    return pl.pallas_call(
+        kernel,
+        out_shape=[jax.ShapeDtypeStruct(a.shape, a.dtype) for a in arrays],
+        in_specs=[pl.BlockSpec(memory_space=pltpu.VMEM)] * len(arrays),
+        out_specs=[pl.BlockSpec(memory_space=pl.ANY)] * len(arrays),
+        scratch_shapes=[pltpu.SemaphoreType.DMA((len(arrays),))],
+        name="results",
+    )(*arrays)
 
 
 class Names:
@@ -811,7 +1004,8 @@
         grad_query=((rows, 1024), f32), grad_key=((rows, 1024), f32),
         grad_value=((rows, 1024), f32), grad_out=((rows, 1024), f32),
         grad_up=((rows, 4096), f32), grad_down=((128, 1024), f32),
-        norms=((8, 1024), f32), sums=((8, HD), f32),
+        norm_one=((1, rows), f32), norm_two=((1, rows), f32),
+        table=((2, BUCKETS), f32), rate=((1, 2), f32),
     )
     pieces = (4, n, rows, 1024)
     square = ((block, 1024), bf16)
@@ -836,7 +1030,7 @@
         dn2s=((4, tok, 1024), bf16), dnin=three, outp=three,
         da=((tok, 1024), bf16), dyt=((8, tok, HD), bf16), dyh=((2, block, HD), bf16),
         tile=((256, 1024), f32), own=((nz, 128, 1024), f32), o_keep=((128, 1024), f32),
-        given_a=four, core_a=four, z_a=((nz - 1, 128, 1024), bf16),
+        given_a=four, core_a=four, z_a=((3, 128, 1024), bf16),
         given_b=four, core_b=four, z_b=((nz - 1, 128, 1024), bf16), up_sum=((128, 1024), f32),
         core_o=four, o_in=((3, 128, 1024), bf16), o_low=((128, 1024), bf16),
         o_z=((nz - 1, 32, 1024), bf16),
@@ -845,8 +1039,8 @@
         diag=heads, below=heads, rest=((2, 1, HD), f32), sums=((2, 1, HD), f32),
         dks=((2, 6 * TILE, HD), f32), dvs=((2, 6 * TILE, HD), f32),
         halo_in=((8, TILE, HD), bf16),
-        norms=((8, 1024), f32), n_core=((8, 1024), f32), n_chip=((8, 1024), f32),
-        n_z=((nz - 1, 8, 1024), f32), n_line=((8, 1024), f32), n_head=((3, 8, 1024), f32),
+        norms=((8, 1024), f32), small=((24, HD), f32), n_seq=((n - 1, 24, HD), f32),
+        n_line=((24, HD), f32), n_head=((3, 24, HD), f32),
     )
     copies = 150
 
@@ -868,15 +1062,9 @@
         ),
         name="block_layer",
     )(*ins.values())
-    r = Names(outs, results)
-    at = lax.axis_index("head") * 256 + lax.axis_index("seq") * rows
-    mine = lax.dynamic_slice(r.norms, (0, at), (2, rows))
-    sums = r.sums[2]
-    return (
-        r.output, r.input_grad, r.grad_query, r.grad_key, r.grad_value, r.grad_out, r.grad_up,
-        r.grad_down, mine[0], mine[1],
-        sums[: 2 * BUCKETS].reshape(2, BUCKETS), sums[2 * BUCKETS : 2 * BUCKETS + 2],
-    )
+    results = placed(results)
+    *large, norm_one, norm_two, table, rate = results
+    return (*large, norm_one.reshape(rows), norm_two.reshape(rows), table, rate.reshape(2))
 
 
 highest = lax.Precision.HIGHEST

time: 248 us -> 209 us (0.84)
  Pallas kernels: 235 us -> 206 us
  local copies, waits for them, and re-layouts: 11.7 us -> 0 us
    pallas_call x1, Pallas kernels: 235 us -> 203 us  [shards(): pl.pallas_call(kernel, out_shape=[jax.ShapeDtypeStruct(shape, kind) for s...]
    unnamed x22 -> x0, local copies, waits for them, and re-layouts: 7.87 us -> none
    pallas_call x0 -> x1, Pallas kernels: none -> 3.3 us  [placed(): pl.pallas_call(kernel, out_shape=[jax.ShapeDtypeStruct(a.shape, a.dtype)...]
where the time goes in v3:
time: 209 us; the launch traced here: 207 us
  Pallas kernels  206 us (99%)
    pallas_call x1, Pallas kernels, shards(): pl.pallas_call(kernel, out_shape=[jax.ShapeDtypeStruct(shape, kind) for s...  203 us

profile of v3, /device:TPU:0, one launch (start us, length us, event | category | flops | bytes accessed | tf_op | source)
XLA Modules:
  0.0 207.0 jit_solution(8318237134109840279)
XLA Ops:
  0.6 202.9 %block_layer.1 = (bf16[256,1024]{1,0:T(8,128)(2,1)}, bf16[256,1024]{1,0:T(8,128)(2,1)}, f32[32,1024]{1,0:T(8,128)}, f32[32,1024]{1,0:T(8,128)}, f32[32,1024]{1,0...) custom-call(f32[2,32]{1,0:T(2,128)} %refs_0_.1, ...), custom_call_target="tpu_custom_call" | custom-call | tf_op jit(solution)/shard_map/block_layer/pallas_call | solution.py:1052
  203.6 3.3 %results.1 = (bf16[256,1024]{1,0:T(8,128)(2,1)}, bf16[256,1024]{1,0:T(8,128)(2,1)}, f32[32,1024]{1,0:T(8,128)}, f32[32,1024]{1,0:T(8,128)}, f32[32,1024]{1,0:T(8...) custom-call(bf16[256,1024]{1,0:T(8,128)(2,1)} %get-tuple-element.36., ...), custom_call_target="tpu_custom_call" | custom-call | tf_op jit(solution)/shard_map/results/pallas_call | solution.py:972

commit v4 on v3

--- a/solution.py
+++ b/solution.py
@@ -170,20 +170,25 @@
 class SquareSum:
     def __init__(self, me, sends, give, land):
         self.me, self.sends, self.give, self.land = me, sends, give, land
-        half = give(2).shape[0] // 2
-        self.parts = [pl.ds(0, half), pl.ds(half, half)]
-        self.half = half
+        self.half = give(2).shape[0] // 2
+        self.parts = [pl.ds(0, self.half), pl.ds(self.half, self.half)]
+        self.copies = []
+
+    def put(self, block, piece, to):
+        at = self.parts[piece]
+        device = self.me.head_dev(to)
+        copy = self.sends.put(self.give(block).at[at], self.land(block).at[at], device)
+        self.copies.append(copy)
+        return copy
 
     def first(self):
-        me, give, land = self.me, self.give(2), self.land(2)
-        self.halves = [
-            self.sends.put(give.at[self.parts[k]], land.at[self.parts[k]], me.head_dev(k))
-            for k in range(2)
-        ]
+        self.halves = [self.put(2, k, k) for k in range(2)]
+
+    def early(self, k):
+        self.put(k, k, k)
 
     def second(self):
-        me, land = self.me, self.land(2)
-        self.copies = []
+        land = self.land(2)
         for k in range(2):
             self.halves[k].wait_recv()
             give = self.give(1 - k)
@@ -193,13 +198,14 @@
                 give[at] = (give[at].astype(f32) + land[at].astype(f32)).astype(bf16)
                 return 0
 
-            lax.fori_loop(0, self.half // 32, add, 0)
+            lax.fori_loop(0, self.half // 32, add, 0, unroll=True)
         for k in range(2):
-            self.copies.append(self.sends.put(self.give(k), self.land(k), me.head_dev(k)))
+            self.put(k, 1 - k, k)
 
     def last(self):
         for copy in self.copies:
-            copy.wait_recv()
+            if not any(copy is half for half in self.halves):
+                copy.wait_recv()
 
 
 def rms(x):
@@ -340,6 +346,8 @@
     def along(self):
         self.base, self.copies = self.sends.claim(3), []
         self.put(self.beside, self.beside, 0)
+
+    def on(self):
         to = self.inner * self.across + (1 - self.inner) * self.beside
         self.put(self.across, to, 2 - self.inner)
 
@@ -375,12 +383,12 @@
             each(128, 32, add)
 
 
-def each(count, step, body):
+def each(count, step, body, unroll=4):
     def one(i, _):
         body(i, part(i, step))
         return 0
 
-    lax.fori_loop(0, count // step, one, 0)
+    lax.fori_loop(0, count // step, one, 0, unroll=unroll)
 
 
 def whole_kernel(ins, outs, b, send_sems, recv_sems):
@@ -397,21 +405,12 @@
     half = pl.ds(me.core * nz, nz)
     wide = 6 * HD
 
-    lane = lax.broadcasted_iota(jnp.int32, (rows, 128), 1)
-    line = lax.broadcasted_iota(jnp.int32, (rows, 128), 0)
-    group = 128 // rows
-    gains = jnp.zeros((rows, 128), f32)
-    for j, gain in enumerate((ins.norm_one, ins.norm_two)):
-        row = jnp.concatenate([gain[...].astype(f32)] * group, axis=1)
-        gains = jnp.where((lane // rows == me.s % group) & (line == j), row, gains)
-    b.gains[...] = gains.astype(bf16)
     first = []
     parts = (ins.w_query, ins.w_key, ins.w_value)
     for k in range(3):
         for j, w in enumerate(parts):
             src = w.at[:, part(me.heads[k], 256)]
             first.append(sends.put(src, b.a1.at[me.h, :, j * 256 : j * 256 + 256], peers[k]))
-        first.append(sends.put(b.gains, b.a1.at[me.h, :, wide:], peers[k]))
 
     def token_block(ref):
         def block(i, piece):
@@ -433,7 +432,16 @@
     dn_line = Line(me, sends, lambda z: b.dn.at[2 * z + me.core])
     for j, w in enumerate(parts):
         b.a1[me.h, :, j * 256 : j * 256 + 256] = w[:, part(me.h, 256)]
-    b.a1[me.h, :, wide:] = b.gains[...]
+    lane = lax.broadcasted_iota(jnp.int32, (8, 128), 1)
+    line = lax.broadcasted_iota(jnp.int32, (8, 128), 0)
+    group = 128 // rows
+    gains = jnp.zeros((8, 128), f32)
+    for j, gain in enumerate((ins.norm_one, ins.norm_two)):
+        row = jnp.concatenate([gain[...].astype(f32)] * group, axis=1)
+        gains = jnp.where((lane // rows == me.s % group) & (line == j), row, gains)
+    b.gains[me.h] = gains
+    own = b.gains.at[me.h]
+    first_gains = [sends.put(own, own, peers[k]) for k in range(3)]
     for copy in first:
         copy.wait_recv()
     w_line.start(b.a1)
@@ -444,8 +452,14 @@
     b.wo[me.h, me.s] = ins.w_out[...]
     b.dn[me.s] = ins.w_down[...]
     b.cots[part(me.h, tok)] = ins.cotangent[...]
+    w_c.append(sends.put((ref := w_line.relay()), ref, core_dev))
+    for copy in first_gains:
+        copy.wait_recv()
+    b.all_gains[me.s] = b.gains[...]
+    all_gains = []
+    for k in range(1, n):
+        all_gains.append(sends.put(b.gains, b.all_gains.at[me.s], me.seq_dev(k)))
     own = b.wo.at[me.h, me.s]
-    w_c.append(sends.put((ref := w_line.relay()), ref, core_dev))
     wo_line.start(ins.w_out)
     wo_c = [sends.put(ins.w_out, own, core_dev)]
     toks.relay()
@@ -464,36 +478,38 @@
     wo_c.append(sends.put((ref := wo_line.relay()), ref, core_dev))
     for copy in w_c:
         copy.wait_recv()
+    for copy in all_gains:
+        copy.wait_recv()
     lanes = []
     for h in range(4):
         for s in range(0, n, group):
-            lanes.append(sum(b.wb[h, s + i, :, wide:].astype(f32) for i in range(group)))
+            lanes.append(sum(b.all_gains[s + i, h] for i in range(group)))
     gains = jnp.concatenate(lanes, axis=1)
     gain_one, gain_two = gains[0:1], gains[1:2]
     toks.last()
-
-    def norm_one(i, at):
-        x = b.x[at].astype(f32)
-        b.hall[at] = (x * rms(x) * gain_one).astype(bf16)
-
-    each(4 * tok, 32, norm_one)
-
-    def project(t, _):
-        at = part(t, tok)
-        for j in range(3):
-            w = b.wb[:, :, :, j * 256 : j * 256 + 256].reshape(1024, 256)
-            out = dot(b.hall[at], w).astype(bf16)
-            for head in range(2):
-                mine = out[:, head * HD : head * HD + HD]
-                if j == 0:
-                    b.q[head, at] = mine
-                else:
-                    b.kvx[2 * (j - 1) + head, part(t + 2, tok)] = mine
-        return 0
-
-    lax.fori_loop(0, 4, project, 0)
+    for pair in (2, 0):
+
+        def norm_one(i, _):
+            at = pl.ds(pair * tok + i * 32, 32)
+            x = b.x[at].astype(f32)
+            b.hall[at] = (x * rms(x) * gain_one).astype(bf16)
+
+        each(2 * tok, 32, norm_one)
+
+        for t in (pair, pair + 1):
+            at = pl.ds(t * tok, tok)
+            for j in range(3):
+                w = b.wb[:, :, :, j * 256 : j * 256 + 256].reshape(1024, 256)
+                out = dot(b.hall[at], w).astype(bf16)
+                for head in range(2):
+                    mine = out[:, head * HD : head * HD + HD]
+                    if j == 0:
+                        b.q[head, at] = mine
+                    else:
+                        b.kvx[2 * (j - 1) + head, pl.ds((t + 2) * tok, tok)] = mine
+        if pair == 2:
+            halo = sends.put(b.kvx.at[:, 4 * TILE :], b.kvx.at[:, : 2 * TILE], me.seq_dev(1))
     sends.sent(toks.halves)
-    halo = sends.put(b.kvx.at[:, 4 * TILE :], b.kvx.at[:, : 2 * TILE], me.seq_dev(1))
 
     falls = [power(ins.decay[0, head], float(TILE)) for head in range(2)]
     for head in range(2):
@@ -506,12 +522,9 @@
             state = falls[head] * segs.keep[t] * state + add
         b.sent[head] = state.astype(bf16)
     carry = [sends.put(b.sent, b.got.at[k - 1], me.seq_dev(k)) for k in (1, 2)]
-    up_c.append(sends.put((ref := up_line.relay()), ref, core_dev))
     for i in (1, 2):
         ref = wo_line.wait(i)
         wo_c.append(sends.put(ref, ref, core_dev))
-    dn_line.start(ins.w_down)
-    dn_c = [sends.put(ins.w_down, b.dn.at[me.s], core_dev)]
     cots.relay()
     for copy in wo_c:
         copy.wait_recv()
@@ -540,11 +553,13 @@
         b.acc[head, at] = att + dot(weight, b.kvx[2 + head, own])
         return base
 
-    lax.fori_loop(0, 4, forward, 2)
+    lax.fori_loop(0, 4, forward, 2, unroll=2)
     halo.wait_recv()
-    lax.fori_loop(0, 4, forward, 0)
+    up_c.append(sends.put((ref := up_line.relay()), ref, core_dev))
+    dn_line.start(ins.w_down)
+    dn_c = [sends.put(ins.w_down, b.dn.at[me.s], core_dev)]
     wo_square.relay()
-    dn_c.append(sends.put((ref := dn_line.relay()), ref, core_dev))
+    lax.fori_loop(0, 4, forward, 0, unroll=2)
     wo_square.last()
     for k in range(3):
         piece = b.wo.at[me.heads[k], half]
@@ -568,9 +583,6 @@
             ys.append(sends.put(src, b.ymix.at[:, part(2 * me.h + head, HD)], peers[k]))
     for head in range(2):
         b.ymix[:, part(2 * me.h + head, HD)] = b.dyt[2 * me.h + head]
-    for i in (1, 2):
-        ref = up_line.wait(i)
-        up_c.append(sends.put(ref, ref, core_dev))
     for copy in ys + wo_c[-3:]:
         copy.wait_recv()
 
@@ -580,7 +592,7 @@
         b.x1[:, cols] = ins.tokens[:, cols].astype(f32) + dot(b.ymix[...], w)
         return 0
 
-    lax.fori_loop(0, 4, out_tile, 0)
+    lax.fori_loop(0, 4, out_tile, 0, unroll=4)
     def norm_two(i, at):
         x = b.x1[at]
         b.h2all[pl.ds(pl.multiple_of(me.h * tok + i * 32, 32), 32)] = (x * rms(x) * gain_two).astype(bf16)
@@ -590,14 +602,18 @@
     own = b.h2all.at[part(me.h, tok)]
     h2s = Square(me, sends, token_block(b.h2all))
     h2s.start(own)
+    dn_c.append(sends.put((ref := dn_line.relay()), ref, core_dev))
+    for i in (1, 2):
+        ref = up_line.wait(i)
+        up_c.append(sends.put(ref, ref, core_dev))
     for i in (1, 2):
         ref = dn_line.wait(i)
         dn_c.append(sends.put(ref, ref, core_dev))
     cots.last()
     for copy in up_c + dn_c:
         copy.wait_recv()
-    dn2_copies = []
-    for k in range(-1, 3):
+    dn2s = SquareSum(me, sends, lambda k: b.dn2s.at[k + 1], lambda k: b.dnin.at[k])
+    for k in (0, 1, 2, -1):
         at = part(me.h if k < 0 else me.heads[k], tok)
         if k == 0:
             h2s.relay()
@@ -615,16 +631,18 @@
             b.du[at, cols] = (slope * dg).astype(bf16)
             return 0
 
-        lax.fori_loop(0, 4, hidden, 0)
+        lax.fori_loop(0, 4, hidden, 0, unroll=4)
 
         def back(j, _):
             w = b.up[j].reshape(256, 1024)
             b.dn2s[k + 1, :, part(j, 256)] = dot_t(b.du[at], w).astype(bf16)
             return 0
 
-        lax.fori_loop(0, 4, back, 0)
-        if k >= 0:
-            dn2_copies.append(sends.put(b.dn2s.at[k + 1], b.dnin.at[k], peers[k]))
+        lax.fori_loop(0, 4, back, 0, unroll=4)
+        if k == 2:
+            dn2s.first()
+        elif k >= 0:
+            dn2s.early(k)
 
         def ahead(j, _):
             cols = part(j, 256)
@@ -635,7 +653,7 @@
                 b.outp[k, :, cols] = out.astype(bf16)
             return 0
 
-        lax.fori_loop(0, 4, ahead, 0)
+        lax.fori_loop(0, 4, ahead, 0, unroll=4)
 
     def down_tile(j, _):
         b.tile[...] = t_dot(b.x[:, part(j, 256)], b.cots[...])
@@ -643,16 +661,29 @@
         b.given_a[j] = b.tile[part(1 - me.core, 128)].astype(bf16)
         return 0
 
-    lax.fori_loop(0, 4, down_tile, 0)
+    lax.fori_loop(0, 4, down_tile, 0, unroll=2)
     down = Reduce(me, sends, b.own, b.given_a, b.core_a, b.z_a, outs.grad_down)
     down.start()
-
-    for copy in dn2_copies:
-        copy.wait_recv()
+    dn2s.second()
+    down.join()
+    down.along()
+    down.on()
+
+    def up_tile(j, _):
+        b.tile[...] = t_dot(b.h2all[:, part(j, 256)], b.du[...])
+        for z in range(nz):
+            b.own[z, part(j, 32)] = b.tile[part(2 * z + me.core, 32)]
+            b.given_b[z, part(j, 32)] = b.tile[part(2 * z + 1 - me.core, 32)].astype(bf16)
+        return 0
+
+    lax.fori_loop(0, 4, up_tile, 0, unroll=2)
+    up = Reduce(me, sends, b.own, b.given_b, b.core_b, b.z_b, b.up_sum)
+    up.start()
+    dn2s.last()
     b.norms[...] = jnp.zeros_like(b.norms)
 
     def second_norm_back(i, at):
-        dn2 = b.dn2s[0, at].astype(f32) + sum(b.dnin[k, at].astype(f32) for k in range(3))
+        dn2 = b.dn2s[0, at].astype(f32) + sum(b.dnin[k, at].astype(f32) for k in range(2))
         x = b.x1[at]
         scale = rms(x)
         n2 = x * scale
@@ -665,7 +696,7 @@
         b.da[at] = dx1.astype(bf16)
 
     each(tok, 32, second_norm_back)
-    sends.sent(ys + dn2_copies + dn_c[1:] + dn_line.copies)
+    sends.sent(ys + dn2s.copies + dn_c[1:] + dn_line.copies)
 
     def back_tile(j, _):
         out = dot_t(b.da[...], b.wo[j].reshape(256, 1024)).astype(bf16)
@@ -673,30 +704,19 @@
         b.dyt[2 * j + 1] = out[:, HD:]
         return 0
 
-    lax.fori_loop(0, 4, back_tile, 0)
+    lax.fori_loop(0, 4, back_tile, 0, unroll=4)
     dys = []
     for k in range(3):
         src = b.dyt.at[pl.ds(2 * me.heads[k], 2)]
         dys.append(sends.put(src, b.dyh.at[:, part(me.h, tok)], peers[k]))
     b.dyh[:, part(me.h, tok)] = b.dyt[pl.ds(2 * me.h, 2)]
-    down.join()
-    down.along()
-
-    def up_tile(j, _):
-        b.tile[...] = t_dot(b.h2all[:, part(j, 256)], b.du[...])
-        for z in range(nz):
-            b.own[z, part(j, 32)] = b.tile[part(2 * z + me.core, 32)]
-            b.given_b[z, part(j, 32)] = b.tile[part(2 * z + 1 - me.core, 32)].astype(bf16)
-        return 0
-
-    lax.fori_loop(0, 4, up_tile, 0)
-    up = Reduce(me, sends, b.own, b.given_b, b.core_b, b.z_b, b.up_sum)
-    up.start()
     down.late()
     for copy in dys:
         copy.wait_recv()
     outp = SquareSum(me, sends, lambda k: b.outp.at[k], lambda k: b.dnin.at[k])
     outp.first()
+    outp.early(0)
+    outp.early(1)
     for zero in (b.sums, b.dks, b.dvs, b.diag, b.below, b.rest):
         zero[...] = jnp.zeros_like(zero)
     for head in range(2):
@@ -710,6 +730,7 @@
         b.sent_back[head] = grad.astype(bf16)
     carry = [sends.put(b.sent_back, b.got_back.at[k - 1], me.seq_dev(-k)) for k in (1, 2)]
     up.join()
+    up.along()
 
     def grad_out_tile(j, _):
         b.tile[...] = t_dot(b.ymix[:, part(j, 256)], b.da[...])
@@ -718,9 +739,8 @@
             b.dn[j, part(z, 32)] = b.tile[part(2 * z + 1 - me.core, 32)].astype(bf16)
         return 0
 
-    lax.fori_loop(0, 4, grad_out_tile, 0)
+    lax.fori_loop(0, 4, grad_out_tile, 0, unroll=2)
     o_core = sends.put(b.dn.at[0:4], b.core_o, core_dev)
-    outp.second()
 
     gap = (grid_of(0) - grid_of(1)).astype(f32)
 
@@ -760,7 +780,8 @@
         b.dvs[head, wide] += t_dot(p, dy)
         return base
 
-    lax.fori_loop(0, 4, backward, 0)
+    lax.fori_loop(0, 4, backward, 0, unroll=2)
+    outp.second()
     sends.sent(dys)
     for head in range(2):
         for i in range(2):
@@ -768,7 +789,7 @@
             b.dyt[2 * head + i] = b.dks[head, at].astype(bf16)
             b.dyt[4 + 2 * head + i] = b.dvs[head, at].astype(bf16)
     halo = sends.put(b.dyt, b.halo_in, me.seq_dev(-1))
-    up.along()
+    up.on()
     o_core.wait_recv()
     sends.sent(down.copies)
     for k in range(3):
@@ -781,18 +802,19 @@
         each(128, 32, chip_sum)
     o_square = SquareSum(me, sends, lambda k: b.given_a.at[k], lambda k: b.o_in.at[k])
     o_square.first()
+    o_square.early(0)
+    o_square.early(1)
 
     def keep(i, at):
         b.o_keep[at] = b.own[me.h, at] + b.core_o[me.h, at].astype(f32)
 
     each(128, 32, keep)
-    lax.fori_loop(0, 4, backward, 2)
+    lax.fori_loop(0, 4, backward, 2, unroll=2)
     o_square.second()
     up.late()
     for copy in carry:
         copy.wait_recv()
     place = grid_of(0, (TILE, 1)).astype(f32)
-    halo.wait_recv()
     for head in range(2):
         past = power(ins.decay[0, head], 4.0 * TILE) * segs.keep_after
         grad = b.got_back[0, head].astype(f32) + past * b.got_back[1, head].astype(f32)
@@ -815,29 +837,21 @@
             total = total - slope.sum(axis=0, keepdims=True)
             total = total - TILE * crossing * (grad * state).sum(axis=0, keepdims=True)
             dv = dv + b.dvs[head, ext]
+            b.x[at, head * HD : head * HD + HD] = (b.acc[head, at] + dq).astype(bf16)
             if t >= 2:
-                dk = dk + b.halo_in[2 * head + t - 2].astype(f32)
-                dv = dv + b.halo_in[4 + 2 * head + t - 2].astype(f32)
-            for j, grads in enumerate((b.acc[head, at] + dq, dk, dv)):
-                col = (2 * j + head) * HD
-                b.x[at, col : col + HD] = grads.astype(bf16)
+                b.dks[head, ext], b.dvs[head, ext] = dk, dv
+            else:
+                for j, grad_tile in ((2, dk), (4, dv)):
+                    b.x[at, (j + head) * HD : (j + head + 1) * HD] = grad_tile.astype(bf16)
             grad = b.local[4 * head + t] + crossing * grad
         b.sums[head] += total
-
-    backs = SquareSum(
-        me, sends, lambda k: b.du.at[pl.ds(k * tok, tok)], lambda k: b.dn2s.at[k + 1]
-    )
-    for k in (2, 0, 1):
-        at, to = part(me.heads[k], tok), pl.ds(k * tok, tok)
-
-        def spread_back(j, _):
-            w = b.wb[j, :, :, 0:wide].reshape(256, wide)
-            b.du[to, part(j, 256)] = dot_t(b.x[at, 0:wide], w).astype(bf16)
-            return 0
-
-        lax.fori_loop(0, 4, spread_back, 0)
-        if k == 2:
-            backs.first()
+    halo.wait_recv()
+    for head in range(2):
+        for t in (2, 3):
+            at, ext = pl.ds(t * TILE, TILE), pl.ds((t + 2) * TILE, TILE)
+            for j, ref in ((2, b.dks), (4, b.dvs)):
+                total = ref[head, ext] + b.halo_in[2 * j - 4 + 2 * head + t - 2].astype(f32)
+                b.x[at, (j + head) * HD : (j + head + 1) * HD] = total.astype(bf16)
 
     def grad_tile(j, _):
         tile = pl.ds(0, wide)
@@ -847,10 +861,26 @@
             b.dn[4 + z, part(j, 32), tile] = b.tile[part(2 * z + 1 - me.core, 32), tile].astype(bf16)
         return 0
 
-    lax.fori_loop(0, 4, grad_tile, 0)
+    lax.fori_loop(0, 4, grad_tile, 0, unroll=2)
     grads = Reduce(me, sends, b.own, b.dn.at[4:8, :, 0:wide], b.core_q, b.z_q, b.q_sum)
     grads.start()
-    backs.second()
+    backs = SquareSum(
+        me, sends, lambda k: b.du.at[pl.ds(k * tok, tok)], lambda k: b.dn2s.at[k + 1]
+    )
+    for k in (2, 0, 1):
+        at, to = part(me.heads[k], tok), pl.ds(k * tok, tok)
+
+        def spread_back(j, _):
+            w = b.wb[j, :, :, 0:wide].reshape(256, wide)
+            b.du[to, part(j, 256)] = dot_t(b.x[at, 0:wide], w).astype(bf16)
+            return 0
+
+        lax.fori_loop(0, 4, spread_back, 0, unroll=4)
+        if k == 2:
+            backs.first()
+        else:
+            backs.early(k)
+
     outp.last()
 
     def output(i, at):
@@ -864,9 +894,11 @@
         b.base[:, part(j, 256)] = dot_t(b.x[part(me.h, tok), 0:wide], w)
         return 0
 
-    lax.fori_loop(0, 4, own_back, 0)
+    lax.fori_loop(0, 4, own_back, 0, unroll=4)
+
     grads.join()
     grads.along()
+    grads.on()
     o_square.last()
 
     def grad_out_sum(i, at):
@@ -881,10 +913,11 @@
         o_z.append(sends.put(src, b.o_z.at[k - 1], me.z_dev(k)))
     down.total()
     up.total()
+    b.up_low[...] = b.up_sum[...].astype(bf16)
     ups = []
     for k in range(3):
-        src = b.up_sum.at[part(me.heads[k], 32)]
-        ups.append(sends.put(src, outs.grad_up.at[:, part(me.h, 1024)], peers[k]))
+        src = b.up_low.at[part(me.heads[k], 32)]
+        ups.append(sends.put(src, b.up_in.at[k], peers[k]))
     outs.grad_up[:, part(me.h, 1024)] = b.up_sum[part(me.h, 32)]
     gap_near = grid_of(0, (HD, HD)) - grid_of(1, (HD, HD))
     gap_far = gap_near + HD
@@ -903,6 +936,7 @@
         jnp.ones((8, HD), f32), jnp.concatenate(table, axis=0), (((1,), (1,)), ((), ())),
         precision=lax.Precision.HIGHEST, preferred_element_type=f32,
     )
+    backs.second()
     grads.late()
     backs.last()
 
@@ -921,11 +955,11 @@
     b.small[...] = jnp.concatenate(lines + [small], axis=0)
     n_seq = [sends.put(b.small, b.n_seq.at[k - 1], me.seq_dev(k)) for k in range(1, n)]
     grads.total()
+    b.q_low[...] = b.q_sum[...].astype(bf16)
     g_head = []
     for k in range(3):
-        src = b.q_sum.at[part(me.heads[k], 32)]
-        g_head.append(sends.put(src, b.q_in.at[me.h], peers[k]))
-    b.q_in[me.h] = b.q_sum[part(me.h, 32)]
+        src = b.q_low.at[part(me.heads[k], 32)]
+        g_head.append(sends.put(src, b.q_in.at[k], peers[k]))
     total = b.small[...]
     for k in range(n - 1):
         n_seq[k].wait_recv()
@@ -941,11 +975,16 @@
     outs.grad_out[...] = total
     for copy in g_head:
         copy.wait_recv()
-    for h in range(4):
-        for j, out in enumerate((outs.grad_query, outs.grad_key, outs.grad_value)):
-            out[:, h * 256 : h * 256 + 256] = b.q_in[h, :, j * 256 : j * 256 + 256]
+    weights = (outs.grad_query, outs.grad_key, outs.grad_value)
+    for j, out in enumerate(weights):
+        cols = pl.ds(j * 256, 256)
+        out[:, part(me.h, 256)] = b.q_sum[part(me.h, 32), cols]
+        for k in range(3):
+            out[:, part(me.heads[k], 256)] = b.q_in[k, :, cols].astype(f32)
     for copy in n_head + ups:
         copy.wait_recv()
+    for k in range(3):
+        outs.grad_up[:, part(me.heads[k], 1024)] = b.up_in[k].astype(f32)
     total = b.n_line[...] + sum(b.n_head[k] for k in range(3))
     b.norms[0:8, 0:HD], b.norms[0:8, HD : 2 * HD] = total[0:8], total[8:16]
     mine = b.norms[pl.ds(2 * me.h + me.s // group, 1), 0 : 2 * HD]
@@ -1015,8 +1054,8 @@
     heads = ((2, HD, HD), f32)
     four = ((nz, 128, 1024), bf16)
     room = dict(
-        gains=((rows, 128), bf16), a1=((4, rows, wide + 128), bf16), u1=((4, rows, 1024), bf16),
-        x=square, hall=square, wb=((4, n, rows, wide + 128), bf16), up=(pieces, bf16),
+        gains=((4, 8, 128), f32), all_gains=((n, 4, 8, 128), f32), a1=((4, rows, wide), bf16), u1=((4, rows, 1024), bf16),
+        x=square, hall=square, wb=((4, n, rows, wide), bf16), up=(pieces, bf16),
         dn=((n, 128, 1024), bf16), wo=(pieces, bf16), cots=square,
         q=((2, block, HD), bf16), kvx=((4, 6 * TILE, HD), bf16),
         near=tables, far=tables, decay=tables, enter=column, leave=column,
@@ -1035,7 +1074,8 @@
         core_o=four, o_in=((3, 128, 1024), bf16), o_low=((128, 1024), bf16),
         o_z=((nz - 1, 32, 1024), bf16),
         core_q=((nz, 128, wide), bf16),
-        z_q=((nz - 1, 128, wide), bf16), q_sum=((128, wide), f32), q_in=((4, 32, wide), f32),
+        z_q=((nz - 1, 128, wide), bf16), q_sum=((128, wide), f32), q_in=((3, 32, wide), bf16), q_low=((128, wide), bf16),
+        up_low=((128, 1024), bf16), up_in=((3, 32, 1024), bf16),
         diag=heads, below=heads, rest=((2, 1, HD), f32), sums=((2, 1, HD), f32),
         dks=((2, 6 * TILE, HD), f32), dvs=((2, 6 * TILE, HD), f32),
         halo_in=((8, TILE, HD), bf16),

time: 209 us -> 186 us (0.89)
  Pallas kernels: 206 us -> 184 us
    pallas_call x1, Pallas kernels: 203 us -> 181 us  [shards(): pl.pallas_call(kernel, out_shape=[jax.ShapeDtypeStruct(shape, kind) for s...]
where the time goes in v4:
time: 186 us; the launch traced here: 185 us
  Pallas kernels  184 us (99%)
    pallas_call x1, Pallas kernels, shards(): pl.pallas_call(kernel, out_shape=[jax.ShapeDtypeStruct(shape, kind) for s...  181 us

profile of v4, /device:TPU:0, one launch (start us, length us, event | category | flops | bytes accessed | tf_op | source)
XLA Modules:
  0.0 185.3 jit_solution(6540644999093122498)
XLA Ops:
  0.6 181.2 %block_layer.1 = (bf16[256,1024]{1,0:T(8,128)(2,1)}, bf16[256,1024]{1,0:T(8,128)(2,1)}, f32[32,1024]{1,0:T(8,128)}, f32[32,1024]{1,0:T(8,128)}, f32[32,1024]{1,0...) custom-call(f32[2,32]{1,0:T(2,128)} %refs_0_.1, ...), custom_call_target="tpu_custom_call" | custom-call | tf_op jit(solution)/shard_map/block_layer/pallas_call | solution.py:1092
  181.8 3.3 %results.1 = (bf16[256,1024]{1,0:T(8,128)(2,1)}, bf16[256,1024]{1,0:T(8,128)(2,1)}, f32[32,1024]{1,0:T(8,128)}, f32[32,1024]{1,0:T(8,128)}, f32[32,1024]{1,0:T(8...) custom-call(bf16[256,1024]{1,0:T(8,128)(2,1)} %get-tuple-element.36., ...), custom_call_target="tpu_custom_call" | custom-call | tf_op jit(solution)/shard_map/results/pallas_call | solution.py:1011

commit v5 on v4

--- a/solution.py
+++ b/solution.py
@@ -402,7 +402,6 @@
     )
     sends = Sends(send_sems, recv_sems)
     core_dev = me.core_dev()
-    half = pl.ds(me.core * nz, nz)
     wide = 6 * HD
 
     first = []
@@ -412,6 +411,9 @@
             src = w.at[:, part(me.heads[k], 256)]
             first.append(sends.put(src, b.a1.at[me.h, :, j * 256 : j * 256 + 256], peers[k]))
 
+    own = b.wo.at[me.h, me.z, me.core]
+    wo_z = [sends.put(ins.w_out, own, me.z_dev(k)) for k in range(1, nz)]
+
     def token_block(ref):
         def block(i, piece):
             if piece is None:
@@ -426,10 +428,7 @@
     for k in range(3):
         src = ins.w_up.at[:, part(me.heads[k], 1024)]
         first_up.append(sends.put(src, b.u1.at[me.h], peers[k]))
-    w_line = Line(me, sends, lambda z: b.wb.at[:, 2 * z + me.core])
-    wo_line = Line(me, sends, lambda z: b.wo.at[me.h, 2 * z + me.core])
     up_line = Line(me, sends, lambda z: b.up.at[:, 2 * z + me.core])
-    dn_line = Line(me, sends, lambda z: b.dn.at[2 * z + me.core])
     for j, w in enumerate(parts):
         b.a1[me.h, :, j * 256 : j * 256 + 256] = w[:, part(me.h, 256)]
     lane = lax.broadcasted_iota(jnp.int32, (8, 128), 1)
@@ -444,38 +443,44 @@
     first_gains = [sends.put(own, own, peers[k]) for k in range(3)]
     for copy in first:
         copy.wait_recv()
-    w_line.start(b.a1)
+    w_z = [sends.put(b.a1, b.wb.at[:, me.s], me.z_dev(k)) for k in range(1, nz)]
     w_c = [sends.put(b.a1, b.wb.at[:, me.s], core_dev)]
     b.wb[:, me.s] = b.a1[...]
     b.x[part(me.h, tok)] = ins.tokens[...]
     b.u1[me.h] = ins.w_up[:, part(me.h, 1024)]
-    b.wo[me.h, me.s] = ins.w_out[...]
+    b.wo[me.h, me.z, me.core] = ins.w_out[...]
     b.dn[me.s] = ins.w_down[...]
     b.cots[part(me.h, tok)] = ins.cotangent[...]
-    w_c.append(sends.put((ref := w_line.relay()), ref, core_dev))
     for copy in first_gains:
         copy.wait_recv()
     b.all_gains[me.s] = b.gains[...]
     all_gains = []
     for k in range(1, n):
         all_gains.append(sends.put(b.gains, b.all_gains.at[me.s], me.seq_dev(k)))
-    own = b.wo.at[me.h, me.s]
-    wo_line.start(ins.w_out)
-    wo_c = [sends.put(ins.w_out, own, core_dev)]
     toks.relay()
+    for copy in wo_z:
+        copy.wait_recv()
+
+    def wo_block(i, piece):
+        at = pl.ds(0, nz) if piece is None else pl.ds(piece * (nz // 2), nz // 2)
+        return b.wo.at[i, at, me.core]
+
+    wo_square = Square(me, sends, wo_block)
+    wo_square.start(wo_block(me.h, None))
     cots = Square(me, sends, token_block(b.cots))
     cots.start(ins.cotangent)
     segs = Segs(me, ins.segments, b.rows, b.cols)
     fill_tables(ins.table, ins.decay, b.near, b.far, b.decay, b.enter, b.leave)
-    for i in (1, 2):
-        ref = w_line.wait(i)
+    for k in range(1, nz):
+        w_z[k - 1].wait_recv()
+        ref = b.wb.at[:, me.z_from(k)]
         w_c.append(sends.put(ref, ref, core_dev))
-    for copy in first_up:
-        copy.wait_recv()
-    up_line.start(b.u1)
+        if k == nz - 2:
+            for copy in first_up:
+                copy.wait_recv()
+            up_line.start(b.u1)
     up_c = [sends.put(b.u1, b.up.at[:, me.s], core_dev)]
     b.up[:, me.s] = b.u1[...]
-    wo_c.append(sends.put((ref := wo_line.relay()), ref, core_dev))
     for copy in w_c:
         copy.wait_recv()
     for copy in all_gains:
@@ -522,20 +527,9 @@
             state = falls[head] * segs.keep[t] * state + add
         b.sent[head] = state.astype(bf16)
     carry = [sends.put(b.sent, b.got.at[k - 1], me.seq_dev(k)) for k in (1, 2)]
-    for i in (1, 2):
-        ref = wo_line.wait(i)
-        wo_c.append(sends.put(ref, ref, core_dev))
+    wo_square.relay()
     cots.relay()
-    for copy in wo_c:
-        copy.wait_recv()
-
-    def wo_block(i, piece):
-        if piece is None:
-            return b.wo.at[i, half]
-        return b.wo.at[i, pl.ds(me.core * nz + piece * (nz // 2), nz // 2)]
-
-    wo_square = Square(me, sends, wo_block)
-    wo_square.start(b.wo.at[me.h, half])
+    up_c.append(sends.put((ref := up_line.relay()), ref, core_dev))
 
     def forward(index, base):
         head, t = index // 2, base + index % 2
@@ -550,20 +544,12 @@
         mix = jnp.concatenate([e0.astype(bf16), e1.astype(bf16), e2.astype(bf16)], axis=1)
         att = dot(mix, b.kvx[2 + head, wide]) / mass
         weight = jnp.where(same, raw[:, 2 * TILE :] * b.decay[head], 0.0).astype(bf16)
-        b.acc[head, at] = att + dot(weight, b.kvx[2 + head, own])
+        b.acc[head, at] += att + dot(weight, b.kvx[2 + head, own])
         return base
 
+    for head in range(2):
+        b.acc[head, 2 * TILE :] = jnp.zeros((2 * TILE, HD), f32)
     lax.fori_loop(0, 4, forward, 2, unroll=2)
-    halo.wait_recv()
-    up_c.append(sends.put((ref := up_line.relay()), ref, core_dev))
-    dn_line.start(ins.w_down)
-    dn_c = [sends.put(ins.w_down, b.dn.at[me.s], core_dev)]
-    wo_square.relay()
-    lax.fori_loop(0, 4, forward, 0, unroll=2)
-    wo_square.last()
-    for k in range(3):
-        piece = b.wo.at[me.heads[k], half]
-        wo_c.append(sends.put(piece, piece, core_dev))
     for copy in carry:
         copy.wait_recv()
     for head in range(2):
@@ -573,9 +559,20 @@
             at = pl.ds(t * TILE, TILE)
             b.state[4 * head + t] = state
             reach = b.enter[head] * segs.live(t)
-            y = b.acc[head, at] + dot(b.q[head, at], state.astype(bf16)) * reach
-            b.dyt[2 * t + head] = y.astype(bf16)
+            y = dot(b.q[head, at], state.astype(bf16)) * reach
+            b.acc[head, at] = b.acc[head, at] + y if t >= 2 else y
             state = falls[head] * segs.keep[t] * state + b.local[4 * head + t]
+    halo.wait_recv()
+    own = b.dn.at[me.s]
+    dn_z = [sends.put(ins.w_down, own, me.z_dev(k)) for k in range(1, nz)]
+    dn_c = [sends.put(ins.w_down, own, core_dev)]
+    wo_square.last()
+    own = b.wo.at[:, :, me.core]
+    wo_c = [sends.put(own, own, core_dev)]
+    lax.fori_loop(0, 4, forward, 0, unroll=2)
+    for t in range(4):
+        for head in range(2):
+            b.dyt[2 * t + head] = b.acc[head, pl.ds(t * TILE, TILE)].astype(bf16)
     ys = []
     for k in range(3):
         for head in range(2):
@@ -583,12 +580,12 @@
             ys.append(sends.put(src, b.ymix.at[:, part(2 * me.h + head, HD)], peers[k]))
     for head in range(2):
         b.ymix[:, part(2 * me.h + head, HD)] = b.dyt[2 * me.h + head]
-    for copy in ys + wo_c[-3:]:
+    for copy in ys + wo_c:
         copy.wait_recv()
 
     def out_tile(j, _):
         cols = part(j, 256)
-        w = b.wo[:, :, :, cols].reshape(1024, 256)
+        w = b.wo[:, :, :, :, cols].reshape(1024, 256)
         b.x1[:, cols] = ins.tokens[:, cols].astype(f32) + dot(b.ymix[...], w)
         return 0
 
@@ -602,12 +599,12 @@
     own = b.h2all.at[part(me.h, tok)]
     h2s = Square(me, sends, token_block(b.h2all))
     h2s.start(own)
-    dn_c.append(sends.put((ref := dn_line.relay()), ref, core_dev))
     for i in (1, 2):
         ref = up_line.wait(i)
         up_c.append(sends.put(ref, ref, core_dev))
-    for i in (1, 2):
-        ref = dn_line.wait(i)
+    for k in range(1, nz):
+        dn_z[k - 1].wait_recv()
+        ref = b.dn.at[me.z_from(k)]
         dn_c.append(sends.put(ref, ref, core_dev))
     cots.last()
     for copy in up_c + dn_c:
@@ -696,7 +693,7 @@
         b.da[at] = dx1.astype(bf16)
 
     each(tok, 32, second_norm_back)
-    sends.sent(ys + dn2s.copies + dn_c[1:] + dn_line.copies)
+    sends.sent(ys + dn2s.copies + dn_c[1:])
 
     def back_tile(j, _):
         out = dot_t(b.da[...], b.wo[j].reshape(256, 1024)).astype(bf16)
@@ -899,26 +896,6 @@
     grads.join()
     grads.along()
     grads.on()
-    o_square.last()
-
-    def grad_out_sum(i, at):
-        total = b.o_keep[at] + sum(b.o_in[k, at].astype(f32) for k in range(2))
-        b.o_keep[at] = total
-        b.o_low[at] = total.astype(bf16)
-
-    each(128, 32, grad_out_sum)
-    o_z = []
-    for k in range(1, nz):
-        src = b.o_low.at[part((me.z + k) % nz, 32)]
-        o_z.append(sends.put(src, b.o_z.at[k - 1], me.z_dev(k)))
-    down.total()
-    up.total()
-    b.up_low[...] = b.up_sum[...].astype(bf16)
-    ups = []
-    for k in range(3):
-        src = b.up_low.at[part(me.heads[k], 32)]
-        ups.append(sends.put(src, b.up_in.at[k], peers[k]))
-    outs.grad_up[:, part(me.h, 1024)] = b.up_sum[part(me.h, 32)]
     gap_near = grid_of(0, (HD, HD)) - grid_of(1, (HD, HD))
     gap_far = gap_near + HD
     table = []
@@ -937,6 +914,18 @@
         precision=lax.Precision.HIGHEST, preferred_element_type=f32,
     )
     backs.second()
+    o_square.last()
+
+    def grad_out_sum(i, at):
+        total = b.o_keep[at] + sum(b.o_in[k, at].astype(f32) for k in range(2))
+        b.o_keep[at] = total
+        b.o_low[at] = total.astype(bf16)
+
+    each(128, 32, grad_out_sum)
+    o_z = []
+    for k in range(1, nz):
+        src = b.o_low.at[part((me.z + k) % nz, 32)]
+        o_z.append(sends.put(src, b.o_z.at[k - 1], me.z_dev(k)))
     grads.late()
     backs.last()
 
@@ -954,6 +943,13 @@
     lines = [b.norms[j : j + 1, i * HD : i * HD + HD] for j in range(2) for i in range(8)]
     b.small[...] = jnp.concatenate(lines + [small], axis=0)
     n_seq = [sends.put(b.small, b.n_seq.at[k - 1], me.seq_dev(k)) for k in range(1, n)]
+    up.total()
+    b.up_low[...] = b.up_sum[...].astype(bf16)
+    ups = []
+    for k in range(3):
+        src = b.up_low.at[part(me.heads[k], 32)]
+        ups.append(sends.put(src, b.up_in.at[k], peers[k]))
+    outs.grad_up[:, part(me.h, 1024)] = b.up_sum[part(me.h, 32)]
     grads.total()
     b.q_low[...] = b.q_sum[...].astype(bf16)
     g_head = []
@@ -973,6 +969,7 @@
         o_z[k].wait_recv()
         total = total + b.o_z[k].astype(f32)
     outs.grad_out[...] = total
+    down.total()
     for copy in g_head:
         copy.wait_recv()
     weights = (outs.grad_query, outs.grad_key, outs.grad_value)
@@ -1056,7 +1053,7 @@
     room = dict(
         gains=((4, 8, 128), f32), all_gains=((n, 4, 8, 128), f32), a1=((4, rows, wide), bf16), u1=((4, rows, 1024), bf16),
         x=square, hall=square, wb=((4, n, rows, wide), bf16), up=(pieces, bf16),
-        dn=((n, 128, 1024), bf16), wo=(pieces, bf16), cots=square,
+        dn=((n, 128, 1024), bf16), wo=((4, nz, 2, rows, 1024), bf16), cots=square,
         q=((2, block, HD), bf16), kvx=((4, 6 * TILE, HD), bf16),
         near=tables, far=tables, decay=tables, enter=column, leave=column,
         rows=((6, 1, TILE), f32), cols=((4, TILE, 1), f32),

time: 186 us -> 185 us (level)
  no operation moved by 1% of the time
where the time goes in v5:
time: 185 us
  Pallas kernels  184 us (99%)
    pallas_call x1, Pallas kernels, shards(): pl.pallas_call(kernel, out_shape=[jax.ShapeDtypeStruct(shape, kind) for s...  181 us

profile of v5, /device:TPU:0, one launch (start us, length us, event | category | flops | bytes accessed | tf_op | source)
XLA Modules:
  0.0 184.8 jit_solution(11659959885893780263)
XLA Ops:
  0.6 180.6 %block_layer.1 = (bf16[256,1024]{1,0:T(8,128)(2,1)}, bf16[256,1024]{1,0:T(8,128)(2,1)}, f32[32,1024]{1,0:T(8,128)}, f32[32,1024]{1,0:T(8,128)}, f32[32,1024]{1,0...) custom-call(f32[2,32]{1,0:T(2,128)} %refs_0_.1, ...), custom_call_target="tpu_custom_call" | custom-call | tf_op jit(solution)/shard_map/block_layer/pallas_call | solution.py:1089
  181.3 3.3 %results.1 = (bf16[256,1024]{1,0:T(8,128)(2,1)}, bf16[256,1024]{1,0:T(8,128)(2,1)}, f32[32,1024]{1,0:T(8,128)}, f32[32,1024]{1,0:T(8,128)}, f32[32,1024]{1,0:T(8...) custom-call(bf16[256,1024]{1,0:T(8,128)(2,1)} %get-tuple-element.36., ...), custom_call_target="tpu_custom_call" | custom-call | tf_op jit(solution)/shard_map/results/pallas_call | solution.py:1008
